TPU v7x, 128 devices: a whole 4x4x4 slice. The times are simulated.
128 devices in a mesh: src: 8 (over z, core), tgt: 16 (over y, x).
Axes of the slice: x: 4, y: 4, z: 4, core: 2. Of those that a mesh axis runs over, the one named last changes fastest.
Arguments:
- src_points: bfloat16 [16384, 512], P(('src', 'tgt')), may hold values from -1 to 1
- tgt_points: bfloat16 [32768, 512], P(('tgt', 'src')), may hold values from -0.5 to 0.5
- tgt_start: float32 [32768], P('tgt'), may hold values from -2 to 10
Outputs:
- src_potential: float32 [16384], P('src')
- tgt_potential: float32 [32768], P('tgt')
All inputs are finite; a program needn't handle non-finite values.
Results may differ from a plain program's by a relative error of at most 0.0003.
Values may be sent and summed in bfloat16 or wider, within the bound.
No kernel may reach another device: no remote copies, remote signals or barrier semaphores. Data moves between devices by JAX's collectives and lax.ppermute only.
A program may use at most 64 MiB of HBM per device.

v0:
```python
import jax
import jax.numpy as jnp
from jax import lax
from jax.sharding import PartitionSpec as P

ITERS = 2


EPSILON = 0.05


def norms(points):
    wide = points.astype(jnp.float32)
    return jnp.sum(wide * wide, axis=1)


def row_update(tile, pot_g, count):
    score = (pot_g[None, :] - tile) / EPSILON
    peak = lax.pmax(jnp.max(score, axis=1), "tgt")
    total = lax.psum(jnp.sum(jnp.exp(score - peak[:, None]), axis=1), "tgt")
    return -EPSILON * (peak + jnp.log(total)) + EPSILON * jnp.log(jnp.float32(count))


def col_update(tile, pot_f, count):
    score = (pot_f[:, None] - tile) / EPSILON
    peak = lax.pmax(jnp.max(score, axis=0), "src")
    total = lax.psum(jnp.sum(jnp.exp(score - peak[None, :]), axis=0), "src")
    return -EPSILON * (peak + jnp.log(total)) + EPSILON * jnp.log(jnp.float32(count))


def local(src_points, tgt_points, tgt_start):
    sources = lax.all_gather(src_points, "tgt", axis=0, tiled=True)
    targets = lax.all_gather(tgt_points, "src", axis=0, tiled=True)
    src_sq = norms(sources)
    tgt_sq = norms(targets)
    total_src = sources.shape[0] * lax.axis_size("src")
    total_tgt = targets.shape[0] * lax.axis_size("tgt")

    def make_cost():
        inner = lax.dot_general(
            sources, targets, (((1,), (1,)), ((), ())), preferred_element_type=jnp.float32
        )
        return src_sq[:, None] + tgt_sq[None, :] - 2.0 * inner

    pot_g = tgt_start
    pot_f = jnp.zeros_like(src_sq)
    for step in range(ITERS):
        tile = make_cost()
        pot_f = row_update(tile, pot_g, total_tgt)
        tile = make_cost()
        pot_g = col_update(tile, pot_f, total_src)
    return (pot_f, pot_g)


def solution(mesh):
    return jax.shard_map(
        local,
        mesh=mesh,
        in_specs=(P(("src", "tgt"), None), P(("tgt", "src"), None), P("tgt")),
        out_specs=(P("src"), P("tgt")),
        check_vma=False,
    )
```

profile of v0, /device:TPU:1, one launch (start us, length us, event | category | flops | bytes accessed | tf_op | source)
XLA Modules:
  0.0 359.5 jit_solution(8973466041568834855)
XLA Ops:
  7.2 0.0 all-gather.5.cloned.1.call-start
  7.2 0.7 all-gather.5.cloned.1.call-update
  7.9 0.0 all-gather.3.cloned.1.call-start
  7.9 0.7 all-gather.3.cloned.1.call-update
  8.6 30.1 %all-gather.5.cloned.1.call-done = bf16[2048,512]{1,0:T(8,128)(2,1)} async-done(((bf16[256,512]{1,0:T(8,128)(2,1)}), bf16[2048,512]{1,0:T(8,128)(2,1)}) %all-gather.5.cloned.1.call-update) | async-done | bytes 2097168 | tf_op jit(solution)/shard_map/all_gather | solution.py:33
  38.8 2.1 multiply_reduce_fusion
  40.8 44.0 %all-gather.3.cloned.1.call-done = bf16[2048,512]{1,0:T(8,128)(2,1)} async-done(((bf16[128,512]{1,0:T(8,128)(2,1)}), bf16[2048,512]{1,0:T(8,128)(2,1)}) %all-gather.3.cloned.1.call-update) | async-done | bytes 2097168 | tf_op jit(solution)/shard_map/all_gather | solution.py:32
  84.8 2.1 multiply_reduce_fusion.1
  86.9 0.0 copy-start.1
  86.9 10.5 %fusion = (f32[2048]{0:T(1024)S(1)}, f32[2048,2048]{1,0:T(8,128)}) fusion(f32[2048]{0:T(1024)} %param.5, bf16[2048,512]{1,0:T(8,128)(2,1)} %all-gather.3.cloned.1.call-done, bf16[2048,512]{1,0:T(8,128)(2,1)} %all-gather.5.cloned.1.call-done, f32[2048]{0:T(1024)S(1)} %multiply_reduce_fusion, f32[2048]{0:T(1024)S(1)} %multiply_reduce_fusion.1), kind=kOutput, calls=%fused_computation.9 | convolution fusion | flops 4320131072 | bytes 21004288 | tf_op jit(solution)/shard_map/dot_general | solution.py:40
  97.4 31.4 %pmax.28 = f32[2048]{0:T(1024)S(1)} all-reduce(f32[2048]{0:T(1024)S(1)} %get-tuple-element.2), channel_id=1, replica_groups=mesh['src'=8,'tgt'=16] {'tgt'}, use_global_device_ids=true, to_apply=%region_3.0 | all-reduce | flops 2048 | bytes 16384 | tf_op jit(solution)/shard_map/pmax | solution.py:19
  128.8 0.0 copy-done.1
  128.8 7.9 %exponential_reduce_fusion.3 = f32[2048]{0:T(1024)S(1)} fusion(f32[2048,2048]{1,0:T(8,128)} %get-tuple-element.3, f32[2048]{0:T(1024)S(1)} %pmax.28, f32[2048]{0:T(1024)S(1)} %copy-done.1), kind=kLoop, calls=%fused_computation.6 | loop fusion | flops 16775168 | bytes 16801792 | tf_op jit(solution)/shard_map/reduce_sum | solution.py:20
  136.8 29.0 %psum.28 = f32[2048]{0:T(1024)S(1)} all-reduce(f32[2048]{0:T(1024)S(1)} %exponential_reduce_fusion.3), channel_id=1, replica_groups=mesh['src'=8,'tgt'=16] {'tgt'}, use_global_device_ids=true, to_apply=%region_5.0 | all-reduce | flops 2048 | bytes 16384 | tf_op jit(solution)/shard_map/psum | solution.py:20
  165.8 7.5 %fusion.1 = f32[2048]{0:T(1024)S(1)} fusion(f32[2048,2048]{1,0:T(8,128)} %get-tuple-element.3, f32[2048]{0:T(1024)S(1)} %multiply_add_fusion.3), kind=kLoop, calls=%fused_computation.10 | loop fusion | flops 12580864 | bytes 16793600 | tf_op jit(solution)/shard_map/reduce_max | solution.py:26
  173.3 27.8 %pmax.29 = f32[2048]{0:T(1024)S(1)} all-reduce(f32[2048]{0:T(1024)S(1)} %fusion.1), channel_id=1, replica_groups=mesh['src'=8,'tgt'=16] {'src'}, use_global_device_ids=true, to_apply=%region_7.0 | all-reduce | flops 2048 | bytes 16384 | tf_op jit(solution)/shard_map/pmax | solution.py:26
  201.1 8.0 %exponential_reduce_fusion.2 = f32[2048]{0:T(1024)S(1)} fusion(f32[2048,2048]{1,0:T(8,128)} %get-tuple-element.3, f32[2048]{0:T(1024)S(1)} %pmax.29, f32[2048]{0:T(1024)S(1)} %multiply_add_fusion.3), kind=kLoop, calls=%fused_computation.4 | loop fusion | flops 16775168 | bytes 16801792 | tf_op jit(solution)/shard_map/reduce_sum | solution.py:27
  209.1 12.6 %psum.29 = f32[2048]{0:T(1024)S(1)} all-reduce(f32[2048]{0:T(1024)S(1)} %exponential_reduce_fusion.2), channel_id=1, replica_groups=mesh['src'=8,'tgt'=16] {'src'}, use_global_device_ids=true, to_apply=%region_9.0 | all-reduce | flops 2048 | bytes 16384 | tf_op jit(solution)/shard_map/psum | solution.py:27
  221.6 7.5 %fusion.2 = f32[2048]{0:T(1024)S(1)} fusion(f32[2048,2048]{1,0:T(8,128)} %get-tuple-element.3, f32[2048]{0:T(1024)S(1)} %multiply_add_fusion.2), kind=kLoop, calls=%fused_computation.11 | loop fusion | flops 12580864 | bytes 16793600 | tf_op jit(solution)/shard_map/reduce_max | solution.py:19
  229.1 30.7 %pmax.30 = f32[2048]{0:T(1024)S(1)} all-reduce(f32[2048]{0:T(1024)S(1)} %fusion.2), channel_id=1, replica_groups=mesh['src'=8,'tgt'=16] {'tgt'}, use_global_device_ids=true, to_apply=%region_11.0 | all-reduce | flops 2048 | bytes 16384 | tf_op jit(solution)/shard_map/pmax | solution.py:19
  259.9 7.9 %exponential_reduce_fusion.1 = f32[2048]{0:T(1024)S(1)} fusion(f32[2048,2048]{1,0:T(8,128)} %get-tuple-element.3, f32[2048]{0:T(1024)S(1)} %pmax.30, f32[2048]{0:T(1024)S(1)} %multiply_add_fusion.2), kind=kLoop, calls=%fused_computation.2 | loop fusion | flops 16775168 | bytes 16801792 | tf_op jit(solution)/shard_map/reduce_sum | solution.py:20
  267.8 29.2 %psum.30 = f32[2048]{0:T(1024)S(1)} all-reduce(f32[2048]{0:T(1024)S(1)} %exponential_reduce_fusion.1), channel_id=1, replica_groups=mesh['src'=8,'tgt'=16] {'tgt'}, use_global_device_ids=true, to_apply=%region_13.0 | all-reduce | flops 2048 | bytes 16384 | tf_op jit(solution)/shard_map/psum | solution.py:20
  297.0 0.0 copy-start
  297.0 7.5 %fusion.3 = f32[2048]{0:T(1024)S(1)} fusion(f32[2048,2048]{1,0:T(8,128)} %get-tuple-element.3, f32[2048]{0:T(1024)S(1)} %multiply_add_fusion.1), kind=kLoop, calls=%fused_computation.12 | loop fusion | flops 12580864 | bytes 16793600 | tf_op jit(solution)/shard_map/reduce_max | solution.py:26
  304.5 26.9 %pmax.31 = f32[2048]{0:T(1024)S(1)} all-reduce(f32[2048]{0:T(1024)S(1)} %fusion.3), channel_id=1, replica_groups=mesh['src'=8,'tgt'=16] {'src'}, use_global_device_ids=true, to_apply=%region_15.0 | all-reduce | flops 2048 | bytes 16384 | tf_op jit(solution)/shard_map/pmax | solution.py:26
  331.4 8.0 %exponential_reduce_fusion = f32[2048]{0:T(1024)S(1)} fusion(f32[2048,2048]{1,0:T(8,128)} %get-tuple-element.3, f32[2048]{0:T(1024)S(1)} %pmax.31, f32[2048]{0:T(1024)S(1)} %multiply_add_fusion.1), kind=kLoop, calls=%fused_computation | loop fusion | flops 16775168 | bytes 16801792 | tf_op jit(solution)/shard_map/reduce_sum | solution.py:27
  339.3 0.0 copy-done
  339.4 12.7 %psum.31 = f32[2048]{0:T(1024)S(1)} all-reduce(f32[2048]{0:T(1024)S(1)} %exponential_reduce_fusion), channel_id=1, replica_groups=mesh['src'=8,'tgt'=16] {'src'}, use_global_device_ids=true, to_apply=%region_17.0 | all-reduce | flops 2048 | bytes 16384 | tf_op jit(solution)/shard_map/psum | solution.py:27
  352.0 0.6 multiply_add_fusion
  (3 shorter events, 0.0 us)
Async XLA Ops:
  7.2 31.6 %all-gather.5.cloned.1.call-start = ((), (), s32[]{:S(2)}) async-start(), calls=%async_computation.1 | async-start | bytes 2359296 | tf_op jit(solution)/shard_map/all_gather | solution.py:33
  7.9 77.0 %all-gather.3.cloned.1.call-start = ((), (), s32[]{:S(2)}) async-start(), calls=%async_computation | async-start | bytes 2228224 | tf_op jit(solution)/shard_map/all_gather | solution.py:32
  86.9 41.9 %copy-start.1 = (f32[2048]{0:T(1024)S(1)}, f32[2048]{0:T(1024)}, u32[]{:S(2)}) copy-start(f32[2048]{0:T(1024)} %param.5) | copy-start | bytes 24580
  297.0 42.3 %copy-start = (f32[2048]{0:T(1024)}, f32[2048]{0:T(1024)S(1)}, u32[]{:S(2)}) copy-start(f32[2048]{0:T(1024)S(1)} %multiply_add_fusion.1) | copy-start | bytes 24580
Sparse Core Ops, SparseCore 0:
  9.7 28.9 all-gather.4
  40.9 43.9 all-gather.2
where the time goes:
time: 360 us; the launch traced here: 359 us
  blocking collectives  200 us (56%)
  waiting for transfers between devices  75.5 us (21%)
  other arithmetic  59 us (16%)
  between operations  14.2 us (4%)
  matrix products  10.5 us (3%)
    pmax x2, blocking collectives, row_update(): peak = lax.pmax(jnp.max(score, axis=1), 'tgt')  62.1 us
    psum x2, blocking collectives, row_update(): total = lax.psum(jnp.sum(jnp.exp(score - peak[:, None]), axis=1), 'tgt')  58.2 us
    pmax x2, blocking collectives, col_update(): peak = lax.pmax(jnp.max(score, axis=0), 'src')  54.6 us
    all_gather x1, waiting for transfers between devices, local(): sources = lax.all_gather(src_points, 'tgt', axis=0, tiled=True)  44 us
    all_gather x1, waiting for transfers between devices, local(): targets = lax.all_gather(tgt_points, 'src', axis=0, tiled=True)  30.1 us
    psum x2, blocking collectives, col_update(): total = lax.psum(jnp.sum(jnp.exp(score - peak[None, :]), axis=0), 'src')  25.2 us
    reduce_sum x2, other arithmetic, col_update(): total = lax.psum(jnp.sum(jnp.exp(score - peak[None, :]), axis=0), 'src')  15.9 us
    reduce_sum x2, other arithmetic, row_update(): total = lax.psum(jnp.sum(jnp.exp(score - peak[:, None]), axis=1), 'tgt')  15.9 us
  transfers between devices with their start and end apart: 2, of which 2 were waited for; matrix products, arithmetic and copies ran while one was open for 1% of the time, Pallas kernels for 0%

commit v1 on v0

v1 whole, which is shorter than its diff:
```python
import functools
import itertools
import math

import jax
import jax.numpy as jnp
from jax import lax
from jax.experimental import pallas as pl
from jax.experimental.pallas import tpu as pltpu
from jax.sharding import PartitionSpec as P

ITERS = 2


EPSILON = 0.05
UNIT = EPSILON

LANES = 128
SUB = 8
VMEM_LIMIT = 16 * 1024 * 1024


def tree(op, values):
    values = list(values)
    while len(values) > 1:
        values = [
            op(values[i], values[i + 1]) if i + 1 < len(values) else values[i]
            for i in range(0, len(values), 2)
        ]
    return values[0]


def merge(peaks, totals):
    peak = jnp.max(peaks, axis=0, keepdims=True)
    return peak + jnp.log(jnp.sum(totals * jnp.exp(peaks - peak), axis=0, keepdims=True))


def merge_parts(parts_ref, count, out_ref):
    parts = [parts_ref[i] for i in range(parts_ref.shape[0])]
    peak = tree(jnp.maximum, parts)
    total = tree(jnp.add, [jnp.exp(part - peak) for part in parts])
    out_ref[...] = math.log(count) - (peak + jnp.log(total))


def repeat(part_ref, part):
    for copy in range(part_ref.shape[0]):
        part_ref[copy] = part


def stacked(first, second):
    return jnp.concatenate([first, second], axis=0)


def power_sum(tiles, peak):
    both = [
        jnp.exp(stacked(tiles[i] - peak, tiles[i + 1] - peak).astype(jnp.bfloat16))
        for i in range(0, len(tiles), 2)
    ]
    total = tree(jnp.add, both).astype(jnp.float32)
    return total[:SUB] + total[SUB:]


def lane_tiles(rows):
    return [rows[:, k : k + LANES] for k in range(0, rows.shape[1], LANES)]


def row_part(load, pots):
    peaks, totals = [], []
    for first in range(0, LANES, SUB):
        tiles = [tile + pot for tile, pot in zip(lane_tiles(load(first)), pots)]
        peak = tree(jnp.maximum, tiles)
        peaks.append(peak)
        totals.append(power_sum(tiles, peak))
    return merge(jnp.concatenate(peaks, axis=0).T, jnp.concatenate(totals, axis=0).T)


def pot_rows(pot_ref):
    return [
        jnp.broadcast_to(pot_ref[k : k + 1, :], (SUB, LANES)) for k in range(pot_ref.shape[0])
    ]


def squares(points):
    wide = points.astype(jnp.float32)
    return jnp.sum(tree(jnp.add, lane_tiles(wide * wide)).T, axis=0, keepdims=True)


def place_kernel(
    own_ref, other_ref, side_ref, side_other_ref, far_ref, theirs_ref, theirs_far_ref, start_ref, targets, sq_ref, pot_ref
):
    own = lax.axis_index("src")
    core = own % 2
    size = own_ref.shape[0]
    chips = targets.shape[0] // (2 * size)

    def put(points, chip, core):
        index = (own // 2 + chip + chips) % chips * 2 + core
        targets[pl.ds(pl.multiple_of(index * size, size), size), :] = points
        per = size // LANES
        for sub in range(per):
            row = squares(points[sub * LANES : (sub + 1) * LANES])
            sq_ref[pl.ds(index * per + sub, 1), :] = row

    side = 2 * core - 1
    put(own_ref[...], 0, core)
    put(other_ref[...], 0, 1 - core)
    put(side_ref[...], side, core)
    put(side_other_ref[...], side, 1 - core)
    put(far_ref[...], 2, core)
    put(theirs_ref[:size, :], -side, 1 - core)
    put(theirs_ref[size:, :], -side, core)
    put(theirs_far_ref[...], 2, 1 - core)
    pot_ref[...] = (start_ref[...] - sq_ref[...]) * (1.0 / UNIT)


def bring_kernel(*refs):
    count = len(refs) // 3
    copies = [
        pltpu.make_async_copy(refs[i], refs[count + i], refs[2 * count + i]) for i in range(count)
    ]
    for copy in copies:
        copy.start()
    for copy in copies:
        copy.wait()


def block_pipeline(points_ref, index_of, tgt_ref, pot_ref, score_ref, rows_ref, sq_ref, even, odd):
    step = even.shape[0]
    per = step // LANES
    steps = points_ref.shape[0] // step

    def product(block, held):
        points = points_ref[pl.ds(pl.multiple_of(block * step, step), step), :]
        tile = lax.dot_general(
            points, tgt_ref[...], (((1,), (1,)), ((), ())), preferred_element_type=jnp.float32
        ) * (2.0 / UNIT)
        held[...] = tile
        for sub in range(per):
            part = slice(sub * LANES, (sub + 1) * LANES)
            index = index_of(block * per + sub)
            score_ref[pl.ds(pl.multiple_of(index * LANES, LANES), LANES), :] = tile[part]
            sq_ref[pl.ds(index, 1), :] = squares(points[part])

    def reduce(held):
        pots = pot_rows(pot_ref)

        def load(start):
            return lambda first: held[start + first : start + first + SUB, :]

        return [row_part(load(sub * LANES), pots) for sub in range(per)]

    def keep(block, rows):
        for sub, row in enumerate(rows):
            rows_ref[pl.ds(index_of(block * per + sub), 1), :] = row

    product(0, even)

    if steps > 2:

        @pl.loop(0, steps // 2 - 1)
        def _(pair):
            rows = reduce(even)
            product(2 * pair + 1, odd)
            keep(2 * pair, rows)
            rows = reduce(odd)
            product(2 * pair + 2, even)
            keep(2 * pair + 1, rows)

    rows = reduce(even)
    product(steps - 1, odd)
    keep(steps - 2, rows)
    keep(steps - 1, reduce(odd))


def row_index(lines):
    own, core = lax.axis_index("tgt"), lax.axis_index("src") % 2
    y, x = own // 4, own % 4
    line, place = y + core * (x - y), x + core * (y - x)

    def index_of(block):
        shift = lines[0] if len(lines) == 1 else lines[0] + block // 4 * (lines[1] - lines[0])
        to_line, to_place = (line + shift + 4) % 4, (place + block % 4 + 3) % 4
        return to_line * (4 - 3 * core) + to_place * (1 + 3 * core)

    return index_of


def own_kernel(points_ref, tgt_ref, pot_ref, score_ref, rows_ref, src_sq_ref, even, odd):
    block_pipeline(
        points_ref, row_index((0,)), tgt_ref, pot_ref, score_ref, rows_ref, src_sq_ref, even, odd
    )


def more_kernel(
    lines, score_in_ref, rows_in_ref, src_sq_in_ref, first_ref, second_ref, tgt_ref, pot_ref,
    score_ref, part_ref, src_sq_ref, rows_ref, points, even, odd,
):
    rows_ref[...] = rows_in_ref[...]
    src_sq_ref[...] = src_sq_in_ref[...]
    half = first_ref.shape[0]
    points[:half, :] = first_ref[...]
    points[half:, :] = second_ref[...]
    block_pipeline(
        points, row_index(lines), tgt_ref, pot_ref, score_ref, rows_ref, src_sq_ref, even, odd
    )
    repeat(part_ref, rows_ref[...])


def two_by_two(blocks, step):
    step(1, False)

    @pl.loop(1, blocks // 2)
    def _(pair):
        step(2 * pair, True)
        step(2 * pair + 1, False)


def row_kernel(count, score_ref, parts_ref, part_ref, pot_ref, rows_ref, *held):
    merge_parts(parts_ref, count, pot_ref)
    pots = pot_rows(pot_ref)
    blocks = score_ref.shape[0] // LANES
    even, odd = held[:2], held[2:]

    def reduce(block, into):
        peaks, totals = into
        start = pl.multiple_of(block * LANES, LANES)
        for first in range(0, LANES, SUB):
            loaded = score_ref[pl.ds(start + first, SUB), :]
            tiles = [tile + pot for tile, pot in zip(lane_tiles(loaded), pots)]
            peak = tree(jnp.maximum, tiles)
            peaks[first : first + SUB, :] = peak
            totals[first : first + SUB, :] = power_sum(tiles, peak)

    def finish(block, held):
        rows_ref[pl.ds(block, 1), :] = merge(held[0][...].T, held[1][...].T)

    def step(block, is_even):
        finish(block - 1, odd if is_even else even)
        reduce(block, even if is_even else odd)

    reduce(0, even)
    two_by_two(blocks, step)
    finish(blocks - 1, odd)
    repeat(part_ref, rows_ref[...])


def col_kernel(
    count, score_ref, parts_ref, sq_ref, pot_out_ref, part_ref, pot_ref, peaks, totals, even, odd
):
    merge_parts(parts_ref, count, pot_ref)
    pot_out_ref[...] = pot_ref[...] * UNIT + sq_ref[...]
    rows, cols = score_ref.shape
    blocks = rows // LANES

    def widen(block, into):
        into[...] = jnp.broadcast_to(pot_ref[pl.ds(block, 1), :], (LANES, LANES)).T

    def reduce(block, wide):
        here = pl.ds(pl.multiple_of(block * LANES, LANES), LANES)
        there = pl.ds(pl.multiple_of(block * SUB, SUB), SUB)
        pots = wide[...]
        for k in range(cols // LANES):
            lanes = slice(k * LANES, (k + 1) * LANES)
            tile = score_ref[here, lanes] + pots
            tiles = [tile[i : i + SUB] for i in range(0, LANES, SUB)]
            peak = tree(jnp.maximum, tiles)
            peaks[there, lanes] = peak
            totals[there, lanes] = power_sum(tiles, peak)

    def step(block, is_even):
        widen(block, even if is_even else odd)
        reduce(block - 1, odd if is_even else even)

    widen(0, even)
    two_by_two(blocks, step)
    reduce(blocks - 1, odd)
    for k in range(cols // LANES):
        lanes = slice(k * LANES, (k + 1) * LANES)
        pot_ref[k : k + 1, :] = merge(peaks[:, lanes], totals[:, lanes])
    repeat(part_ref, pot_ref[...])


def last_kernel(count, parts_ref, sq_ref, out_ref):
    merge_parts(parts_ref, count, out_ref)
    out_ref[...] = out_ref[...] * UNIT + sq_ref[...]


def params():
    return pltpu.CompilerParams(vmem_limit_bytes=VMEM_LIMIT)


def vec(size):
    return jax.ShapeDtypeStruct((size // LANES, LANES), jnp.float32)


def vecs(copies, size):
    return jax.ShapeDtypeStruct((copies, size // LANES, LANES), jnp.float32)


def scratch(*shape):
    return pltpu.VMEM(shape, jnp.float32)


ANYWHERE = pl.BlockSpec(memory_space=pl.ANY)
IN_VMEM = pl.BlockSpec(memory_space=pltpu.VMEM)


def place(own, other, side, side_other, far, theirs, theirs_far, start):
    rows, width = 8 * own.shape[0], own.shape[1]
    return pl.pallas_call(
        place_kernel,
        out_shape=(pltpu.VMEM((rows, width), own.dtype), vec(rows), vec(rows)),
        in_specs=[IN_VMEM] * 8,
        out_specs=(IN_VMEM,) * 3,
        cost_estimate=cost(rows, width, 1),
        compiler_params=params(),
        name="place",
    )(own, other, side, side_other, far, theirs, theirs_far, start)


def bring(*arrays):
    return pl.pallas_call(
        bring_kernel,
        out_shape=tuple(pltpu.VMEM(a.shape, a.dtype) for a in arrays),
        in_specs=[pl.BlockSpec(memory_space=pltpu.HBM)] * len(arrays),
        out_specs=(IN_VMEM,) * len(arrays),
        scratch_shapes=[pltpu.SemaphoreType.DMA] * len(arrays),
        compiler_params=params(),
        name="bring",
    )(*[pltpu.with_memory_space_constraint(a, pltpu.HBM) for a in arrays])


def cost(rows, cols, width):
    return pl.CostEstimate(
        flops=2 * rows * cols * width, bytes_accessed=8 * rows * cols, transcendentals=rows * cols
    )


def own_pass(points, targets, pot, rows):
    cols, width = targets.shape
    return pl.pallas_call(
        own_kernel,
        out_shape=(pltpu.VMEM((rows, cols), jnp.float32), vec(rows), vec(rows)),
        in_specs=[IN_VMEM] * 3,
        out_specs=(IN_VMEM,) * 3,
        scratch_shapes=[scratch(256, cols)] * 2,
        cost_estimate=cost(points.shape[0], cols, width),
        compiler_params=params(),
        name="own_pass",
    )(points, targets, pot)


def more_pass(state, first, second, lines, targets, pot, copies):
    score, row_parts, src_sq = state
    (rows, cols), width = score.shape, targets.shape[1]
    points = 2 * first.shape[0]
    score = pltpu.with_memory_space_constraint(score, pltpu.VMEM)
    return pl.pallas_call(
        functools.partial(more_kernel, lines),
        out_shape=(pltpu.VMEM((rows, cols), jnp.float32), vecs(copies, rows), vec(rows)),
        in_specs=[IN_VMEM] * 7,
        out_specs=(IN_VMEM,) * 3,
        scratch_shapes=[scratch(rows // LANES, LANES), pltpu.VMEM((points, width), first.dtype)]
        + [scratch(256, cols)] * 2,
        input_output_aliases={0: 0},
        cost_estimate=cost(points, cols, width),
        compiler_params=params(),
        name="more_pass",
    )(score, row_parts, src_sq, first, second, targets, pot)


def row_pass_call(score, parts, count, copies):
    rows, cols = score.shape
    return pl.pallas_call(
        functools.partial(row_kernel, count),
        out_shape=vecs(copies, rows),
        in_specs=[IN_VMEM] * 2,
        out_specs=IN_VMEM,
        scratch_shapes=[scratch(cols // LANES, LANES), scratch(rows // LANES, LANES)]
        + [scratch(LANES, LANES)] * 4,
        compiler_params=params(),
        name="row_pass",
    )(score, parts)


def col_pass_call(score, parts, sq, count, copies):
    rows, cols = score.shape
    return pl.pallas_call(
        functools.partial(col_kernel, count),
        out_shape=(vec(rows), vecs(copies, cols)),
        in_specs=[IN_VMEM] * 3,
        out_specs=(IN_VMEM, IN_VMEM),
        scratch_shapes=[scratch(max(rows, cols) // LANES, LANES)]
        + [scratch(rows // LANES * SUB, cols)] * 2
        + [scratch(LANES, LANES)] * 2,
        compiler_params=params(),
        name="col_pass",
    )(score, parts, sq)


def last_call(parts, sq, count):
    return pl.pallas_call(
        functools.partial(last_kernel, count),
        out_shape=jax.ShapeDtypeStruct(sq.shape, jnp.float32),
        in_specs=[IN_VMEM] * 2,
        out_specs=IN_VMEM,
        compiler_params=params(),
        name="last",
    )(parts, sq)


def exchange(part, axis):
    return lax.all_to_all(part, axis, 0, 0, tiled=True)


def move(block, to):
    pairs = []
    for z, core, y, x in itertools.product(range(4), range(2), range(4), range(4)):
        a, b, c, d = to(z, core, y, x)
        pairs.append((((z * 2 + core) * 4 + y) * 4 + x, ((a % 4 * 2 + b) * 4 + c % 4) * 4 + d % 4))
    return lax.ppermute(block, ("src", "tgt"), pairs)


def other_core(block):
    return move(block, lambda z, core, y, x: (z, 1 - core, y, x))


def round_z(block):
    return move(block, lambda z, core, y, x: (z + 1 - 2 * core, core, y, x))


def along_line(block, by):
    return move(block, lambda z, core, y, x: (z, core, y + core * by, x + (1 - core) * by))


def across_lines(block, by):
    return move(block, lambda z, core, y, x: (z, core, y + (1 - core) * by, x + core * by))


def after(value, earlier):
    def kernel(*refs):
        del refs

    return pl.pallas_call(
        kernel,
        out_shape=jax.ShapeDtypeStruct(value.shape, value.dtype),
        in_specs=[ANYWHERE] * 2,
        out_specs=ANYWHERE,
        input_output_aliases={0: 0},
        cost_estimate=pl.CostEstimate(flops=0, bytes_accessed=40_000_000, transcendentals=0),
        compiler_params=params(),
        name="after",
    )(value, earlier)


def gather_targets(own, earlier):
    side = round_z(own)
    other = other_core(own)
    far = round_z(after(side, earlier))
    side_other = round_z(other)
    theirs = other_core(jnp.concatenate([side, side_other]))
    return other, side, side_other, far, theirs, other_core(far)


def local(src_points, tgt_points, tgt_start):
    n_src, n_tgt = lax.axis_size("src"), lax.axis_size("tgt")
    own, size = src_points, src_points.shape[0]
    total_src = size * n_tgt * n_src
    total_tgt = tgt_points.shape[0] * n_src * n_tgt
    held, tgt_held, start = bring(own, tgt_points, tgt_start.reshape(-1, LANES))

    line = jnp.concatenate([along_line(own, 1), held, along_line(own, -1), along_line(own, 2)])
    before, behind = across_lines(line, 1), across_lines(line, -1)
    far_low, far_high = across_lines(before[: 2 * size], 1), across_lines(behind[2 * size :], -1)

    targets, tgt_sq, red_g = place(tgt_held, *gather_targets(tgt_points, line), start)
    targets = pltpu.with_memory_space_constraint(targets, pltpu.VMEM)
    state = own_pass(line, targets, red_g, size * n_tgt)
    score, part, src_sq = more_pass(state, before, behind, (-1, 1), targets, red_g, 1)
    state = score, part[0], src_sq
    score, part, src_sq = more_pass(state, far_low, far_high, (2,), targets, red_g, n_tgt)
    score = pltpu.with_memory_space_constraint(score, pltpu.VMEM)
    for step in range(ITERS):
        if step:
            part = row_pass_call(score, parts, total_src, n_tgt)
        parts = exchange(part, "tgt")
        pot_f, part = col_pass_call(score, parts, src_sq, total_tgt, n_src)
        parts = exchange(part, "src")
    pot_g = last_call(parts, tgt_sq, total_src)
    return (pot_f.reshape(-1), pot_g.reshape(-1))


def solution(mesh):
    return jax.shard_map(
        local,
        mesh=mesh,
        in_specs=(P(("src", "tgt"), None), P(("tgt", "src"), None), P("tgt")),
        out_specs=(P("src"), P("tgt")),
        check_vma=False,
    )
```

time: 360 us -> 93.1 us (0.26)
  blocking collectives: 200 us -> 43 us
  waiting for transfers between devices: 75.5 us -> 1.58 us
  other arithmetic: 59 us -> 0.03 us
  Pallas kernels: 0 us -> 24 us
  starting transfers between devices: 0.08 us -> 23.4 us
  between operations: 14.2 us -> 0.76 us
  matrix products: 10.5 us -> 0 us
    pmax x4 -> x0, blocking collectives: 117 us -> none  [the longest x2 62.1 us: row_update(): peak = lax.pmax(jnp.max(score, axis=1), 'tgt')]
    psum x4 -> x0, blocking collectives: 83.4 us -> none  [the longest x2 58.2 us: row_update(): total = lax.psum(jnp.sum(jnp.exp(score - peak[:, None]), axis=1), 'tgt')]
    all_gather x2 -> x0, waiting for transfers between devices: 74.1 us -> none  [the longest x1 44 us: local(): sources = lax.all_gather(src_points, 'tgt', axis=0, tiled=True)]
    all_to_all x0 -> x4, blocking collectives: none -> 43 us  [exchange(): return lax.all_to_all(part, axis, 0, 0, tiled=True)]
    reduce_sum x6 -> x0, other arithmetic: 36 us -> none  [the longest x2 15.9 us: col_update(): total = lax.psum(jnp.sum(jnp.exp(score - peak[None, :]), axis=0), 'src')]
    pallas_call x0 -> x10, Pallas kernels: none -> 24 us  [the longest x2 8.93 us: col_pass_call(): pl.pallas_call(functools.partial(col_kernel, count), out_shape=(vec(rows)...]
    ppermute x0 -> x13, starting transfers between devices: none -> 23.4 us  [move(): return lax.ppermute(block, ('src', 'tgt'), pairs)]
    reduce_max x3 -> x0, other arithmetic: 22.4 us -> none  [the longest x2 14.9 us: col_update(): peak = lax.pmax(jnp.max(score, axis=0), 'src')]
  transfers between devices with their start and end apart: 2 -> 13, of which waited for: 2 -> 1; matrix products, arithmetic and copies ran while one was open for 1% -> 0% of each run, Pallas kernels for 0% -> 8%
where the time goes in v1:
time: 93.1 us; the launch traced here: 92.9 us
  blocking collectives  43 us (46%)
  Pallas kernels  24 us (26%)
  starting transfers between devices  23.4 us (25%)
  waiting for transfers between devices  1.58 us (2%)
    all_to_all x4, blocking collectives, exchange(): return lax.all_to_all(part, axis, 0, 0, tiled=True)  43 us
    ppermute x13, starting transfers between devices, move(): return lax.ppermute(block, ('src', 'tgt'), pairs)  23.4 us
    pallas_call x2, Pallas kernels, col_pass_call(): pl.pallas_call(functools.partial(col_kernel, count), out_shape=(vec(rows)...  8.93 us
    pallas_call x2, Pallas kernels, more_pass(): pl.pallas_call(functools.partial(more_kernel, lines), out_shape=(pltpu.VM...  5.94 us
    pallas_call x1, Pallas kernels, row_pass_call(): pl.pallas_call(functools.partial(row_kernel, count), out_shape=vecs(copie...  4.89 us
    pallas_call x1, Pallas kernels, own_pass(): pl.pallas_call(own_kernel, out_shape=(pltpu.VMEM((rows, cols), jnp.float3...  2.03 us
  transfers between devices with their start and end apart: 13, of which 1 were waited for; matrix products, arithmetic and copies ran while one was open for 0% of the time, Pallas kernels for 8%

profile of v1, /device:TPU:1, one launch (start us, length us, event | category | flops | bytes accessed | tf_op | source)
XLA Modules:
  0.0 92.9 jit_solution(17430342696171684035)
XLA Ops:
  0.6 1.5 %collective-permute-start.3 = (bf16[256,512]{1,0:T(8,128)(2,1)}, bf16[256,512]{1,0:T(8,128)(2,1)S(1)}, u32[]{:S(2)}, u32[]{:S(2)}) collective-permute-start(bf16[256,512]{1,0:T(8,128)(2,1)} %refs_1_.1), channel_id=1, source_target_pairs={{0,16},{1,17},{2,18},{3,19},{4,20},{5,21},{6,22},{7,23},{8,24},{9,... | collective-permute-start | bytes 786440 | tf_op jit(solution)/shard_map/ppermute | solution.py:421
  2.1 1.4 %collective-permute-start = (bf16[128,512]{1,0:T(8,128)(2,1)}, bf16[128,512]{1,0:T(8,128)(2,1)S(1)}, u32[]{:S(2)}, u32[]{:S(2)}) collective-permute-start(bf16[128,512]{1,0:T(8,128)(2,1)} %refs_0_.1), channel_id=1, source_target_pairs={{0,1},{1,2},{2,3},{3,0},{4,5},{5,6},{6,7},{7,4},{8,9},{9,10},{10,1... | collective-permute-start | bytes 393224 | tf_op jit(solution)/shard_map/ppermute | solution.py:421
  3.5 1.4 %collective-permute-start.1 = (bf16[128,512]{1,0:T(8,128)(2,1)}, bf16[128,512]{1,0:T(8,128)(2,1)S(1)}, u32[]{:S(2)}, u32[]{:S(2)}) collective-permute-start(bf16[128,512]{1,0:T(8,128)(2,1)} %refs_0_.1), channel_id=1, source_target_pairs={{0,3},{1,0},{2,1},{3,2},{4,7},{5,4},{6,5},{7,6},{8,11},{9,8},{10,9... | collective-permute-start | bytes 393224 | tf_op jit(solution)/shard_map/ppermute | solution.py:421
  5.0 1.6 %collective-permute-start.2 = (bf16[128,512]{1,0:T(8,128)(2,1)}, bf16[128,512]{1,0:T(8,128)(2,1)S(1)}, u32[]{:S(2)}, u32[]{:S(2)}) collective-permute-start(bf16[128,512]{1,0:T(8,128)(2,1)} %refs_0_.1), channel_id=1, source_target_pairs={{0,2},{1,3},{2,0},{3,1},{4,6},{5,7},{6,4},{7,5},{8,10},{9,11},{10,... | collective-permute-start | bytes 393224 | tf_op jit(solution)/shard_map/ppermute | solution.py:421
  6.6 3.8 %collective-permute-start.4 = (bf16[256,512]{1,0:T(8,128)(2,1)}, bf16[256,512]{1,0:T(8,128)(2,1)S(1)}, u32[]{:S(2)}, u32[]{:S(2)}) collective-permute-start(bf16[256,512]{1,0:T(8,128)(2,1)} %refs_1_.1), channel_id=1, source_target_pairs={{0,32},{1,33},{2,34},{3,35},{4,36},{5,37},{6,38},{7,39},{8,40},{9,... | collective-permute-start | bytes 786440 | tf_op jit(solution)/shard_map/ppermute | solution.py:421
  10.4 1.1 %bring.1 = (bf16[128,512]{1,0:T(8,128)(2,1)S(1)}, bf16[256,512]{1,0:T(8,128)(2,1)S(1)}, f32[16,128]{1,0:T(8,128)S(1)}) custom-call(bf16[128,512]{1,0:T(8,128)(2,1)} %refs_0_.1, bf16[256,512]{1,0:T(8,128)(2,1)} %refs_1_.1, f32[16,128]{1,0:T(8,128)} %bitcast.5), custom_call_target="tpu_custom_call" | custom-call | tf_op jit(solution)/shard_map/bring/pallas_call | solution.py:322
  11.4 0.0 collective-permute-done
  11.5 0.2 collective-permute-start.5
  11.7 0.0 collective-permute-done.2
  11.7 2.5 %collective-permute-start.10 = (bf16[512,512]{1,0:T(8,128)(2,1)S(1)}, bf16[512,512]{1,0:T(8,128)(2,1)S(1)}, u32[]{:S(2)}, u32[]{:S(2)}) collective-permute-start(bf16[512,512]{1,0:T(8,128)(2,1)S(1)} %constant_dynamic-update-slice_fusion.refs_1_.points_ref), channel_id=1, source_target_pairs={{0,12},{1,13},{2,14},{3,15},{4,0},{5,1},{6,2},{7,3},{8,4},{9,5},{1... | collective-permute-start | bytes 1572872 | tf_op jit(solution)/shard_map/ppermute | solution.py:421
  14.3 2.8 %collective-permute-start.6 = (bf16[256,512]{1,0:T(8,128)(2,1)S(1)}, bf16[256,512]{1,0:T(8,128)(2,1)S(1)}, u32[]{:S(2)}, u32[]{:S(2)}) collective-permute-start(bf16[256,512]{1,0:T(8,128)(2,1)S(1)} %after.1), channel_id=1, source_target_pairs={{0,32},{1,33},{2,34},{3,35},{4,36},{5,37},{6,38},{7,39},{8,40},{9,... | collective-permute-start | bytes 786440 | tf_op jit(solution)/shard_map/ppermute | solution.py:421
  17.1 0.0 collective-permute-done.5.side_other_ref
  17.1 1.7 %collective-permute-start.7 = (bf16[512,512]{1,0:T(8,128)(2,1)S(1)}, bf16[512,512]{1,0:T(8,128)(2,1)S(1)}, u32[]{:S(2)}, u32[]{:S(2)}) collective-permute-start(bf16[512,512]{1,0:T(8,128)(2,1)S(1)} %pad_maximum_fusion), channel_id=1, source_target_pairs={{0,16},{1,17},{2,18},{3,19},{4,20},{5,21},{6,22},{7,23},{8,24},{9,... | collective-permute-start | bytes 1572872 | tf_op jit(solution)/shard_map/ppermute | solution.py:421
  18.9 1.5 %collective-permute-done.6.far_ref = bf16[256,512]{1,0:T(8,128)(2,1)S(1)} collective-permute-done((bf16[256,512]{1,0:T(8,128)(2,1)S(1)}, bf16[256,512]{1,0:T(8,128)(2,1)S(1)}, u32[]{:S(2)}, u32[]{:S(2)}) %collective-permute-start.6) | collective-permute-done | bytes 262176 | tf_op jit(solution)/shard_map/ppermute | solution.py:421
  20.4 3.4 %collective-permute-start.8 = (bf16[256,512]{1,0:T(8,128)(2,1)S(1)}, bf16[256,512]{1,0:T(8,128)(2,1)S(1)}, u32[]{:S(2)}, u32[]{:S(2)}) collective-permute-start(bf16[256,512]{1,0:T(8,128)(2,1)S(1)} %collective-permute-done.6.far_ref), channel_id=1, source_target_pairs={{0,16},{1,17},{2,18},{3,19},{4,20},{5,21},{6,22},{7,23},{8,24},{9,... | collective-permute-start | bytes 786440 | tf_op jit(solution)/shard_map/ppermute | solution.py:421
  23.8 0.0 collective-permute-done.9.first_ref
  23.8 0.2 collective-permute-start.11
  24.0 0.0 collective-permute-done.10.second_ref
  24.1 2.8 %collective-permute-start.12 = (bf16[256,512]{1,0:T(8,128)(2,1)S(1)}, bf16[256,512]{1,0:T(8,128)(2,1)S(1)}, u32[]{:S(2)}, u32[]{:S(2)}) collective-permute-start(bf16[256,512]{1,0:T(8,128)(2,1)S(1)} %slice.9), channel_id=1, source_target_pairs={{0,12},{1,13},{2,14},{3,15},{4,0},{5,1},{6,2},{7,3},{8,4},{9,5},{1... | collective-permute-start | bytes 786440 | tf_op jit(solution)/shard_map/ppermute | solution.py:421
  26.9 0.5 place.1
  27.4 2.0 %own_pass.1 = (f32[2048,2048]{1,0:T(8,128)S(1)}, f32[16,128]{1,0:T(8,128)S(1)}, f32[16,128]{1,0:T(8,128)S(1)}) custom-call(bf16[512,512]{1,0:T(8,128)(2,1)S(1)} %constant_dynamic-update-slice_fusion.refs_1_.points_ref, bf16[2048,512]{1,0:T(8,128)(2,1)S(1)} %get-tuple-element.23.tgt_ref, f32[16,128]{1,0:T(8,128)S(1)} %get-tuple-element.24.pot_ref), custom_call_target="tpu_custom_call" | custom-call | flops 1073741824 | bytes 8388608 | tf_op jit(solution)/shard_map/own_pass/pallas_call | solution.py:341
  29.4 3.8 %more_pass.2 = (f32[2048,2048]{1,0:T(8,128)S(1)}, f32[1,16,128]{2,1,0:T(8,128)S(1)}, f32[16,128]{1,0:T(8,128)S(1)}) custom-call(f32[2048,2048]{1,0:T(8,128)S(1)} %get-tuple-element.25.score_in_ref, f32[16,128]{1,0:T(8,128)S(1)} %get-tuple-element.26.rows_in_ref, f32[16,128]{1,0:T(8,128)S(1)} %get-tuple-element.27.src_sq_in_ref, ...), custom_call_target="tpu_custom_call", output_to_operand_aliasing={{0}: (0, {})} | custom-call | flops 2147483648 | bytes 16777216 | tf_op jit(solution)/shard_map/more_pass/pallas_call | solution.py:358
  33.3 0.0 collective-permute-done.12.second_ref
  33.3 2.1 %more_pass.3 = (f32[2048,2048]{1,0:T(8,128)S(1)}, f32[16,16,128]{2,1,0:T(8,128)S(1)}, f32[16,128]{1,0:T(8,128)S(1)}) custom-call(f32[2048,2048]{1,0:T(8,128)S(1)} %get-tuple-element.28.score_in_ref, f32[16,128]{1,0:T(8,128)S(1)} %bitcast.4, f32[16,128]{1,0:T(8,128)S(1)} %get-tuple-element.30.src_sq_in_ref, ...), custom_call_target="tpu_custom_call", output_to_operand_aliasing={{0}: (0, {})} | custom-call | flops 1073741824 | bytes 8388608 | tf_op jit(solution)/shard_map/more_pass/pallas_call | solution.py:358
  35.4 11.0 %all_to_all.20.parts_ref = f32[16,16,128]{2,1,0:T(8,128)S(1)} all-to-all(f32[16,16,128]{2,1,0:T(8,128)S(1)} %get-tuple-element.32), channel_id=1, replica_groups=mesh['src'=8,'tgt'=16] {'tgt'}, dimensions={0} | all-to-all | bytes 262144 | tf_op jit(solution)/shard_map/all_to_all | solution.py:413
  46.4 4.5 %col_pass.2 = (f32[16,128]{1,0:T(8,128)}, f32[8,16,128]{2,1,0:T(8,128)S(1)}) custom-call(f32[2048,2048]{1,0:T(8,128)S(1)} %get-tuple-element.31.score_ref, f32[16,16,128]{2,1,0:T(8,128)S(1)} %all_to_all.20.parts_ref, f32[16,128]{1,0:T(8,128)S(1)} %get-tuple-element.33.sq_ref), custom_call_target="tpu_custom_call" | custom-call | tf_op jit(solution)/shard_map/col_pass/pallas_call | solution.py:388
  50.9 12.9 %all_to_all.21.parts_ref = f32[8,16,128]{2,1,0:T(8,128)S(1)} all-to-all(f32[8,16,128]{2,1,0:T(8,128)S(1)} %get-tuple-element.34), channel_id=1, replica_groups=mesh['src'=8,'tgt'=16] {'src'}, dimensions={0} | all-to-all | bytes 131072 | tf_op jit(solution)/shard_map/all_to_all | solution.py:413
  63.8 4.9 %row_pass.1 = f32[16,16,128]{2,1,0:T(8,128)S(1)} custom-call(f32[2048,2048]{1,0:T(8,128)S(1)} %get-tuple-element.31.score_ref, f32[8,16,128]{2,1,0:T(8,128)S(1)} %all_to_all.21.parts_ref), custom_call_target="tpu_custom_call" | custom-call | tf_op jit(solution)/shard_map/row_pass/pallas_call | solution.py:374
  68.7 9.7 %all_to_all.22.parts_ref = f32[16,16,128]{2,1,0:T(8,128)S(1)} all-to-all(f32[16,16,128]{2,1,0:T(8,128)S(1)} %row_pass.1), channel_id=1, replica_groups=mesh['src'=8,'tgt'=16] {'tgt'}, dimensions={0} | all-to-all | bytes 262144 | tf_op jit(solution)/shard_map/all_to_all | solution.py:413
  78.4 4.5 %col_pass.3 = (f32[16,128]{1,0:T(8,128)}, f32[8,16,128]{2,1,0:T(8,128)S(1)}) custom-call(f32[2048,2048]{1,0:T(8,128)S(1)} %get-tuple-element.31.score_ref, f32[16,16,128]{2,1,0:T(8,128)S(1)} %all_to_all.22.parts_ref, f32[16,128]{1,0:T(8,128)S(1)} %get-tuple-element.33.sq_ref), custom_call_target="tpu_custom_call" | custom-call | tf_op jit(solution)/shard_map/col_pass/pallas_call | solution.py:388
  82.9 9.4 %all_to_all.23.parts_ref = f32[8,16,128]{2,1,0:T(8,128)S(1)} all-to-all(f32[8,16,128]{2,1,0:T(8,128)S(1)} %get-tuple-element.36), channel_id=1, replica_groups=mesh['src'=8,'tgt'=16] {'src'}, dimensions={0} | all-to-all | bytes 131072 | tf_op jit(solution)/shard_map/all_to_all | solution.py:413
  92.2 0.6 last.1
  (16 shorter events, 0.2 us)
Async XLA Ops:
  0.6 10.8 %collective-permute-start.3 = (bf16[256,512]{1,0:T(8,128)(2,1)}, bf16[256,512]{1,0:T(8,128)(2,1)S(1)}, u32[]{:S(2)}, u32[]{:S(2)}) collective-permute-start(bf16[256,512]{1,0:T(8,128)(2,1)} %refs_1_.1), channel_id=1, source_target_pairs={{0,16},{1,17},{2,18},{3,19},{4,20},{5,21},{6,22},{7,23},{8,24},{9,... | collective-permute-start | bytes 786440 | tf_op jit(solution)/shard_map/ppermute | solution.py:421
  2.1 9.3 %collective-permute-start = (bf16[128,512]{1,0:T(8,128)(2,1)}, bf16[128,512]{1,0:T(8,128)(2,1)S(1)}, u32[]{:S(2)}, u32[]{:S(2)}) collective-permute-start(bf16[128,512]{1,0:T(8,128)(2,1)} %refs_0_.1), channel_id=1, source_target_pairs={{0,1},{1,2},{2,3},{3,0},{4,5},{5,6},{6,7},{7,4},{8,9},{9,10},{10,1... | collective-permute-start | bytes 393224 | tf_op jit(solution)/shard_map/ppermute | solution.py:421
  3.5 8.2 %collective-permute-start.1 = (bf16[128,512]{1,0:T(8,128)(2,1)}, bf16[128,512]{1,0:T(8,128)(2,1)S(1)}, u32[]{:S(2)}, u32[]{:S(2)}) collective-permute-start(bf16[128,512]{1,0:T(8,128)(2,1)} %refs_0_.1), channel_id=1, source_target_pairs={{0,3},{1,0},{2,1},{3,2},{4,7},{5,4},{6,5},{7,6},{8,11},{9,8},{10,9... | collective-permute-start | bytes 393224 | tf_op jit(solution)/shard_map/ppermute | solution.py:421
  5.0 6.8 %collective-permute-start.2 = (bf16[128,512]{1,0:T(8,128)(2,1)}, bf16[128,512]{1,0:T(8,128)(2,1)S(1)}, u32[]{:S(2)}, u32[]{:S(2)}) collective-permute-start(bf16[128,512]{1,0:T(8,128)(2,1)} %refs_0_.1), channel_id=1, source_target_pairs={{0,2},{1,3},{2,0},{3,1},{4,6},{5,7},{6,4},{7,5},{8,10},{9,11},{10,... | collective-permute-start | bytes 393224 | tf_op jit(solution)/shard_map/ppermute | solution.py:421
  6.6 7.7 %collective-permute-start.4 = (bf16[256,512]{1,0:T(8,128)(2,1)}, bf16[256,512]{1,0:T(8,128)(2,1)S(1)}, u32[]{:S(2)}, u32[]{:S(2)}) collective-permute-start(bf16[256,512]{1,0:T(8,128)(2,1)} %refs_1_.1), channel_id=1, source_target_pairs={{0,32},{1,33},{2,34},{3,35},{4,36},{5,37},{6,38},{7,39},{8,40},{9,... | collective-permute-start | bytes 786440 | tf_op jit(solution)/shard_map/ppermute | solution.py:421
  11.5 5.6 %collective-permute-start.5 = (bf16[256,512]{1,0:T(8,128)(2,1)S(1)}, bf16[256,512]{1,0:T(8,128)(2,1)S(1)}, u32[]{:S(2)}, u32[]{:S(2)}) collective-permute-start(bf16[256,512]{1,0:T(8,128)(2,1)S(1)} %collective-permute-done.3.other_ref), channel_id=1, source_target_pairs={{0,32},{1,33},{2,34},{3,35},{4,36},{5,37},{6,38},{7,39},{8,40},{9,... | collective-permute-start | bytes 786440 | tf_op jit(solution)/shard_map/ppermute | solution.py:421
  11.7 12.3 %collective-permute-start.10 = (bf16[512,512]{1,0:T(8,128)(2,1)S(1)}, bf16[512,512]{1,0:T(8,128)(2,1)S(1)}, u32[]{:S(2)}, u32[]{:S(2)}) collective-permute-start(bf16[512,512]{1,0:T(8,128)(2,1)S(1)} %constant_dynamic-update-slice_fusion.refs_1_.points_ref), channel_id=1, source_target_pairs={{0,12},{1,13},{2,14},{3,15},{4,0},{5,1},{6,2},{7,3},{8,4},{9,5},{1... | collective-permute-start | bytes 1572872 | tf_op jit(solution)/shard_map/ppermute | solution.py:421
  14.3 9.5 %collective-permute-start.9 = (bf16[512,512]{1,0:T(8,128)(2,1)S(1)}, bf16[512,512]{1,0:T(8,128)(2,1)S(1)}, u32[]{:S(2)}, u32[]{:S(2)}) collective-permute-start(bf16[512,512]{1,0:T(8,128)(2,1)S(1)} %constant_dynamic-update-slice_fusion.refs_1_.points_ref), channel_id=1, source_target_pairs={{0,4},{1,5},{2,6},{3,7},{4,8},{5,9},{6,10},{7,11},{8,12},{9,13},{1... | collective-permute-start | bytes 1572872 | tf_op jit(solution)/shard_map/ppermute | solution.py:421
  14.3 6.1 %collective-permute-start.6 = (bf16[256,512]{1,0:T(8,128)(2,1)S(1)}, bf16[256,512]{1,0:T(8,128)(2,1)S(1)}, u32[]{:S(2)}, u32[]{:S(2)}) collective-permute-start(bf16[256,512]{1,0:T(8,128)(2,1)S(1)} %after.1), channel_id=1, source_target_pairs={{0,32},{1,33},{2,34},{3,35},{4,36},{5,37},{6,38},{7,39},{8,40},{9,... | collective-permute-start | bytes 786440 | tf_op jit(solution)/shard_map/ppermute | solution.py:421
  17.1 9.7 %collective-permute-start.7 = (bf16[512,512]{1,0:T(8,128)(2,1)S(1)}, bf16[512,512]{1,0:T(8,128)(2,1)S(1)}, u32[]{:S(2)}, u32[]{:S(2)}) collective-permute-start(bf16[512,512]{1,0:T(8,128)(2,1)S(1)} %pad_maximum_fusion), channel_id=1, source_target_pairs={{0,16},{1,17},{2,18},{3,19},{4,20},{5,21},{6,22},{7,23},{8,24},{9,... | collective-permute-start | bytes 1572872 | tf_op jit(solution)/shard_map/ppermute | solution.py:421
  20.4 6.4 %collective-permute-start.8 = (bf16[256,512]{1,0:T(8,128)(2,1)S(1)}, bf16[256,512]{1,0:T(8,128)(2,1)S(1)}, u32[]{:S(2)}, u32[]{:S(2)}) collective-permute-start(bf16[256,512]{1,0:T(8,128)(2,1)S(1)} %collective-permute-done.6.far_ref), channel_id=1, source_target_pairs={{0,16},{1,17},{2,18},{3,19},{4,20},{5,21},{6,22},{7,23},{8,24},{9,... | collective-permute-start | bytes 786440 | tf_op jit(solution)/shard_map/ppermute | solution.py:421
  23.8 9.4 %collective-permute-start.11 = (bf16[256,512]{1,0:T(8,128)(2,1)S(1)}, bf16[256,512]{1,0:T(8,128)(2,1)S(1)}, u32[]{:S(2)}, u32[]{:S(2)}) collective-permute-start(bf16[256,512]{1,0:T(8,128)(2,1)S(1)} %slice.8), channel_id=1, source_target_pairs={{0,4},{1,5},{2,6},{3,7},{4,8},{5,9},{6,10},{7,11},{8,12},{9,13},{1... | collective-permute-start | bytes 786440 | tf_op jit(solution)/shard_map/ppermute | solution.py:421
  24.1 9.2 %collective-permute-start.12 = (bf16[256,512]{1,0:T(8,128)(2,1)S(1)}, bf16[256,512]{1,0:T(8,128)(2,1)S(1)}, u32[]{:S(2)}, u32[]{:S(2)}) collective-permute-start(bf16[256,512]{1,0:T(8,128)(2,1)S(1)} %slice.9), channel_id=1, source_target_pairs={{0,12},{1,13},{2,14},{3,15},{4,0},{5,1},{6,2},{7,3},{8,4},{9,5},{1... | collective-permute-start | bytes 786440 | tf_op jit(solution)/shard_map/ppermute | solution.py:421

commit v2 on v1

--- a/solution.py
+++ b/solution.py
@@ -124,52 +124,55 @@
         copy.wait()
 
 
-def block_pipeline(points_ref, index_of, tgt_ref, pot_ref, score_ref, rows_ref, sq_ref, even, odd):
-    step = even.shape[0]
+CHUNK = 256
+
+
+def block_pipeline(points_ref, index_of, tgt_ref, pot_ref, score_ref, rows_ref, sq_ref, held, peaks, totals):
+    step, cols = held[0].shape
     per = step // LANES
     steps = points_ref.shape[0] // step
-
-    def product(block, held):
-        points = points_ref[pl.ds(pl.multiple_of(block * step, step), step), :]
+    chunks = cols // CHUNK
+    pots = pot_rows(pot_ref)
+
+    def product(at, chunk):
+        points = points_ref[at * step : (at + 1) * step, :]
+        lanes = slice(chunk * CHUNK, (chunk + 1) * CHUNK)
         tile = lax.dot_general(
-            points, tgt_ref[...], (((1,), (1,)), ((), ())), preferred_element_type=jnp.float32
+            points, tgt_ref[lanes, :], (((1,), (1,)), ((), ())), preferred_element_type=jnp.float32
         ) * (2.0 / UNIT)
-        held[...] = tile
+        held[at % 2][:, lanes] = tile
         for sub in range(per):
             part = slice(sub * LANES, (sub + 1) * LANES)
-            index = index_of(block * per + sub)
-            score_ref[pl.ds(pl.multiple_of(index * LANES, LANES), LANES), :] = tile[part]
-            sq_ref[pl.ds(index, 1), :] = squares(points[part])
-
-    def reduce(held):
-        pots = pot_rows(pot_ref)
-
-        def load(start):
-            return lambda first: held[start + first : start + first + SUB, :]
-
-        return [row_part(load(sub * LANES), pots) for sub in range(per)]
-
-    def keep(block, rows):
-        for sub, row in enumerate(rows):
-            rows_ref[pl.ds(index_of(block * per + sub), 1), :] = row
-
-    product(0, even)
-
-    if steps > 2:
-
-        @pl.loop(0, steps // 2 - 1)
-        def _(pair):
-            rows = reduce(even)
-            product(2 * pair + 1, odd)
-            keep(2 * pair, rows)
-            rows = reduce(odd)
-            product(2 * pair + 2, even)
-            keep(2 * pair + 1, rows)
-
-    rows = reduce(even)
-    product(steps - 1, odd)
-    keep(steps - 2, rows)
-    keep(steps - 1, reduce(odd))
+            index = index_of(at * per + sub)
+            score_ref[pl.ds(pl.multiple_of(index * LANES, LANES), LANES), lanes] = tile[part]
+            if chunk == sub:
+                sq_ref[pl.ds(index, 1), :] = squares(points[part])
+
+    def reduce(at, chunk):
+        size = step // chunks
+        for first in range(chunk * size, (chunk + 1) * size, SUB):
+            rows = slice(first, first + SUB)
+            tiles = [tile + pot for tile, pot in zip(lane_tiles(held[at % 2][rows, :]), pots)]
+            peak = tree(jnp.maximum, tiles)
+            peaks[at % 2][rows, :] = peak
+            totals[at % 2][rows, :] = power_sum(tiles, peak)
+
+    def finish(at):
+        for sub in range(per):
+            part = slice(sub * LANES, (sub + 1) * LANES)
+            row = merge(peaks[at % 2][part, :].T, totals[at % 2][part, :].T)
+            rows_ref[pl.ds(index_of(at * per + sub), 1), :] = row
+
+    for chunk in range(chunks):
+        product(0, chunk)
+    for at in range(steps):
+        for chunk in range(chunks):
+            if at + 1 < steps:
+                product(at + 1, chunk)
+            reduce(at, chunk)
+            if at and chunk == chunks // 2:
+                finish(at - 1)
+    finish(steps - 1)
 
 
 def row_index(lines):
@@ -185,15 +188,16 @@
     return index_of
 
 
-def own_kernel(points_ref, tgt_ref, pot_ref, score_ref, rows_ref, src_sq_ref, even, odd):
+def own_kernel(points_ref, tgt_ref, pot_ref, score_ref, rows_ref, src_sq_ref, *held):
     block_pipeline(
-        points_ref, row_index((0,)), tgt_ref, pot_ref, score_ref, rows_ref, src_sq_ref, even, odd
+        points_ref, row_index((0,)), tgt_ref, pot_ref, score_ref, rows_ref, src_sq_ref,
+        held[:2], held[2:4], held[4:],
     )
 
 
 def more_kernel(
     lines, score_in_ref, rows_in_ref, src_sq_in_ref, first_ref, second_ref, tgt_ref, pot_ref,
-    score_ref, part_ref, src_sq_ref, rows_ref, points, even, odd,
+    score_ref, part_ref, src_sq_ref, rows_ref, points, *held,
 ):
     rows_ref[...] = rows_in_ref[...]
     src_sq_ref[...] = src_sq_in_ref[...]
@@ -201,7 +205,8 @@
     points[:half, :] = first_ref[...]
     points[half:, :] = second_ref[...]
     block_pipeline(
-        points, row_index(lines), tgt_ref, pot_ref, score_ref, rows_ref, src_sq_ref, even, odd
+        points, row_index(lines), tgt_ref, pot_ref, score_ref, rows_ref, src_sq_ref,
+        held[:2], held[2:4], held[4:],
     )
     repeat(part_ref, rows_ref[...])
 
@@ -336,6 +341,13 @@
     )
 
 
+STEP = 256
+
+
+def step_scratch(cols):
+    return [scratch(STEP, cols)] * 2 + [scratch(STEP, LANES)] * 4
+
+
 def own_pass(points, targets, pot, rows):
     cols, width = targets.shape
     return pl.pallas_call(
@@ -343,7 +355,7 @@
         out_shape=(pltpu.VMEM((rows, cols), jnp.float32), vec(rows), vec(rows)),
         in_specs=[IN_VMEM] * 3,
         out_specs=(IN_VMEM,) * 3,
-        scratch_shapes=[scratch(256, cols)] * 2,
+        scratch_shapes=step_scratch(cols),
         cost_estimate=cost(points.shape[0], cols, width),
         compiler_params=params(),
         name="own_pass",
@@ -361,7 +373,7 @@
         in_specs=[IN_VMEM] * 7,
         out_specs=(IN_VMEM,) * 3,
         scratch_shapes=[scratch(rows // LANES, LANES), pltpu.VMEM((points, width), first.dtype)]
-        + [scratch(256, cols)] * 2,
+        + step_scratch(cols),
         input_output_aliases={0: 0},
         cost_estimate=cost(points, cols, width),
         compiler_params=params(),

time: 93.1 us -> 93.3 us (level)
  transfers between devices with their start and end apart: 13 -> 13, of which waited for: 1 -> 1; matrix products, arithmetic and copies ran while one was open for 0% -> 0% of each run, Pallas kernels for 8% -> 9%
where the time goes in v2:
time: 93.3 us; the launch traced here: 93 us
  blocking collectives  42.5 us (46%)
  Pallas kernels  24.6 us (26%)
  starting transfers between devices  23.4 us (25%)
  waiting for transfers between devices  1.58 us (2%)
    all_to_all x4, blocking collectives, exchange(): return lax.all_to_all(part, axis, 0, 0, tiled=True)  42.5 us
    ppermute x13, starting transfers between devices, move(): return lax.ppermute(block, ('src', 'tgt'), pairs)  23.4 us
    pallas_call x2, Pallas kernels, col_pass_call(): pl.pallas_call(functools.partial(col_kernel, count), out_shape=(vec(rows)...  8.93 us
    pallas_call x2, Pallas kernels, more_pass(): pl.pallas_call(functools.partial(more_kernel, lines), out_shape=(pltpu.VM...  6.44 us
    pallas_call x1, Pallas kernels, row_pass_call(): pl.pallas_call(functools.partial(row_kernel, count), out_shape=vecs(copie...  4.89 us
    pallas_call x1, Pallas kernels, own_pass(): pl.pallas_call(own_kernel, out_shape=(pltpu.VMEM((rows, cols), jnp.float3...  2.15 us
  transfers between devices with their start and end apart: 13, of which 1 were waited for; matrix products, arithmetic and copies ran while one was open for 0% of the time, Pallas kernels for 9%

profile of v2, /device:TPU:1, one launch (start us, length us, event | category | flops | bytes accessed | tf_op | source)
XLA Modules:
  0.0 93.0 jit_solution(3812987944756740378)
XLA Ops:
  0.6 1.5 %collective-permute-start.3 = (bf16[256,512]{1,0:T(8,128)(2,1)}, bf16[256,512]{1,0:T(8,128)(2,1)S(1)}, u32[]{:S(2)}, u32[]{:S(2)}) collective-permute-start(bf16[256,512]{1,0:T(8,128)(2,1)} %refs_1_.1), channel_id=1, source_target_pairs={{0,16},{1,17},{2,18},{3,19},{4,20},{5,21},{6,22},{7,23},{8,24},{9,... | collective-permute-start | bytes 786440 | tf_op jit(solution)/shard_map/ppermute | solution.py:433
  2.1 1.4 %collective-permute-start = (bf16[128,512]{1,0:T(8,128)(2,1)}, bf16[128,512]{1,0:T(8,128)(2,1)S(1)}, u32[]{:S(2)}, u32[]{:S(2)}) collective-permute-start(bf16[128,512]{1,0:T(8,128)(2,1)} %refs_0_.1), channel_id=1, source_target_pairs={{0,1},{1,2},{2,3},{3,0},{4,5},{5,6},{6,7},{7,4},{8,9},{9,10},{10,1... | collective-permute-start | bytes 393224 | tf_op jit(solution)/shard_map/ppermute | solution.py:433
  3.5 1.4 %collective-permute-start.1 = (bf16[128,512]{1,0:T(8,128)(2,1)}, bf16[128,512]{1,0:T(8,128)(2,1)S(1)}, u32[]{:S(2)}, u32[]{:S(2)}) collective-permute-start(bf16[128,512]{1,0:T(8,128)(2,1)} %refs_0_.1), channel_id=1, source_target_pairs={{0,3},{1,0},{2,1},{3,2},{4,7},{5,4},{6,5},{7,6},{8,11},{9,8},{10,9... | collective-permute-start | bytes 393224 | tf_op jit(solution)/shard_map/ppermute | solution.py:433
  5.0 1.6 %collective-permute-start.2 = (bf16[128,512]{1,0:T(8,128)(2,1)}, bf16[128,512]{1,0:T(8,128)(2,1)S(1)}, u32[]{:S(2)}, u32[]{:S(2)}) collective-permute-start(bf16[128,512]{1,0:T(8,128)(2,1)} %refs_0_.1), channel_id=1, source_target_pairs={{0,2},{1,3},{2,0},{3,1},{4,6},{5,7},{6,4},{7,5},{8,10},{9,11},{10,... | collective-permute-start | bytes 393224 | tf_op jit(solution)/shard_map/ppermute | solution.py:433
  6.6 3.8 %collective-permute-start.4 = (bf16[256,512]{1,0:T(8,128)(2,1)}, bf16[256,512]{1,0:T(8,128)(2,1)S(1)}, u32[]{:S(2)}, u32[]{:S(2)}) collective-permute-start(bf16[256,512]{1,0:T(8,128)(2,1)} %refs_1_.1), channel_id=1, source_target_pairs={{0,32},{1,33},{2,34},{3,35},{4,36},{5,37},{6,38},{7,39},{8,40},{9,... | collective-permute-start | bytes 786440 | tf_op jit(solution)/shard_map/ppermute | solution.py:433
  10.4 1.1 %bring.1 = (bf16[128,512]{1,0:T(8,128)(2,1)S(1)}, bf16[256,512]{1,0:T(8,128)(2,1)S(1)}, f32[16,128]{1,0:T(8,128)S(1)}) custom-call(bf16[128,512]{1,0:T(8,128)(2,1)} %refs_0_.1, bf16[256,512]{1,0:T(8,128)(2,1)} %refs_1_.1, f32[16,128]{1,0:T(8,128)} %bitcast.5), custom_call_target="tpu_custom_call" | custom-call | tf_op jit(solution)/shard_map/bring/pallas_call | solution.py:327
  11.4 0.0 collective-permute-done
  11.5 0.2 collective-permute-start.5
  11.7 0.0 collective-permute-done.2
  11.7 2.5 %collective-permute-start.10 = (bf16[512,512]{1,0:T(8,128)(2,1)S(1)}, bf16[512,512]{1,0:T(8,128)(2,1)S(1)}, u32[]{:S(2)}, u32[]{:S(2)}) collective-permute-start(bf16[512,512]{1,0:T(8,128)(2,1)S(1)} %constant_dynamic-update-slice_fusion.refs_1_.points_ref), channel_id=1, source_target_pairs={{0,12},{1,13},{2,14},{3,15},{4,0},{5,1},{6,2},{7,3},{8,4},{9,5},{1... | collective-permute-start | bytes 1572872 | tf_op jit(solution)/shard_map/ppermute | solution.py:433
  14.3 2.8 %collective-permute-start.6 = (bf16[256,512]{1,0:T(8,128)(2,1)S(1)}, bf16[256,512]{1,0:T(8,128)(2,1)S(1)}, u32[]{:S(2)}, u32[]{:S(2)}) collective-permute-start(bf16[256,512]{1,0:T(8,128)(2,1)S(1)} %after.1), channel_id=1, source_target_pairs={{0,32},{1,33},{2,34},{3,35},{4,36},{5,37},{6,38},{7,39},{8,40},{9,... | collective-permute-start | bytes 786440 | tf_op jit(solution)/shard_map/ppermute | solution.py:433
  17.1 0.0 collective-permute-done.5.side_other_ref
  17.1 1.7 %collective-permute-start.7 = (bf16[512,512]{1,0:T(8,128)(2,1)S(1)}, bf16[512,512]{1,0:T(8,128)(2,1)S(1)}, u32[]{:S(2)}, u32[]{:S(2)}) collective-permute-start(bf16[512,512]{1,0:T(8,128)(2,1)S(1)} %pad_maximum_fusion), channel_id=1, source_target_pairs={{0,16},{1,17},{2,18},{3,19},{4,20},{5,21},{6,22},{7,23},{8,24},{9,... | collective-permute-start | bytes 1572872 | tf_op jit(solution)/shard_map/ppermute | solution.py:433
  18.9 1.5 %collective-permute-done.6.far_ref = bf16[256,512]{1,0:T(8,128)(2,1)S(1)} collective-permute-done((bf16[256,512]{1,0:T(8,128)(2,1)S(1)}, bf16[256,512]{1,0:T(8,128)(2,1)S(1)}, u32[]{:S(2)}, u32[]{:S(2)}) %collective-permute-start.6) | collective-permute-done | bytes 262176 | tf_op jit(solution)/shard_map/ppermute | solution.py:433
  20.4 3.4 %collective-permute-start.8 = (bf16[256,512]{1,0:T(8,128)(2,1)S(1)}, bf16[256,512]{1,0:T(8,128)(2,1)S(1)}, u32[]{:S(2)}, u32[]{:S(2)}) collective-permute-start(bf16[256,512]{1,0:T(8,128)(2,1)S(1)} %collective-permute-done.6.far_ref), channel_id=1, source_target_pairs={{0,16},{1,17},{2,18},{3,19},{4,20},{5,21},{6,22},{7,23},{8,24},{9,... | collective-permute-start | bytes 786440 | tf_op jit(solution)/shard_map/ppermute | solution.py:433
  23.8 0.0 collective-permute-done.9.first_ref
  23.8 0.2 collective-permute-start.11
  24.0 0.0 collective-permute-done.10.second_ref
  24.1 2.8 %collective-permute-start.12 = (bf16[256,512]{1,0:T(8,128)(2,1)S(1)}, bf16[256,512]{1,0:T(8,128)(2,1)S(1)}, u32[]{:S(2)}, u32[]{:S(2)}) collective-permute-start(bf16[256,512]{1,0:T(8,128)(2,1)S(1)} %slice.9), channel_id=1, source_target_pairs={{0,12},{1,13},{2,14},{3,15},{4,0},{5,1},{6,2},{7,3},{8,4},{9,5},{1... | collective-permute-start | bytes 786440 | tf_op jit(solution)/shard_map/ppermute | solution.py:433
  26.9 0.5 place.1
  27.4 2.1 %own_pass.1 = (f32[2048,2048]{1,0:T(8,128)S(1)}, f32[16,128]{1,0:T(8,128)S(1)}, f32[16,128]{1,0:T(8,128)S(1)}) custom-call(bf16[512,512]{1,0:T(8,128)(2,1)S(1)} %constant_dynamic-update-slice_fusion.refs_1_.points_ref, bf16[2048,512]{1,0:T(8,128)(2,1)S(1)} %get-tuple-element.23.tgt_ref, f32[16,128]{1,0:T(8,128)S(1)} %get-tuple-element.24.pot_ref), custom_call_target="tpu_custom_call" | custom-call | flops 1073741824 | bytes 8388608 | tf_op jit(solution)/shard_map/own_pass/pallas_call | solution.py:353
  29.6 4.2 %more_pass.2 = (f32[2048,2048]{1,0:T(8,128)S(1)}, f32[1,16,128]{2,1,0:T(8,128)S(1)}, f32[16,128]{1,0:T(8,128)S(1)}) custom-call(f32[2048,2048]{1,0:T(8,128)S(1)} %get-tuple-element.25.score_in_ref, f32[16,128]{1,0:T(8,128)S(1)} %get-tuple-element.26.rows_in_ref, f32[16,128]{1,0:T(8,128)S(1)} %get-tuple-element.27.src_sq_in_ref, ...), custom_call_target="tpu_custom_call", output_to_operand_aliasing={{0}: (0, {})} | custom-call | flops 2147483648 | bytes 16777216 | tf_op jit(solution)/shard_map/more_pass/pallas_call | solution.py:370
  33.8 0.0 collective-permute-done.11.first_ref
  33.8 2.2 %more_pass.3 = (f32[2048,2048]{1,0:T(8,128)S(1)}, f32[16,16,128]{2,1,0:T(8,128)S(1)}, f32[16,128]{1,0:T(8,128)S(1)}) custom-call(f32[2048,2048]{1,0:T(8,128)S(1)} %get-tuple-element.28.score_in_ref, f32[16,128]{1,0:T(8,128)S(1)} %bitcast.4, f32[16,128]{1,0:T(8,128)S(1)} %get-tuple-element.30.src_sq_in_ref, ...), custom_call_target="tpu_custom_call", output_to_operand_aliasing={{0}: (0, {})} | custom-call | flops 1073741824 | bytes 8388608 | tf_op jit(solution)/shard_map/more_pass/pallas_call | solution.py:370
  36.0 11.0 %all_to_all.20.parts_ref = f32[16,16,128]{2,1,0:T(8,128)S(1)} all-to-all(f32[16,16,128]{2,1,0:T(8,128)S(1)} %get-tuple-element.32), channel_id=1, replica_groups=mesh['src'=8,'tgt'=16] {'tgt'}, dimensions={0} | all-to-all | bytes 262144 | tf_op jit(solution)/shard_map/all_to_all | solution.py:425
  47.0 4.5 %col_pass.2 = (f32[16,128]{1,0:T(8,128)}, f32[8,16,128]{2,1,0:T(8,128)S(1)}) custom-call(f32[2048,2048]{1,0:T(8,128)S(1)} %get-tuple-element.31.score_ref, f32[16,16,128]{2,1,0:T(8,128)S(1)} %all_to_all.20.parts_ref, f32[16,128]{1,0:T(8,128)S(1)} %get-tuple-element.33.sq_ref), custom_call_target="tpu_custom_call" | custom-call | tf_op jit(solution)/shard_map/col_pass/pallas_call | solution.py:400
  51.5 12.4 %all_to_all.21.parts_ref = f32[8,16,128]{2,1,0:T(8,128)S(1)} all-to-all(f32[8,16,128]{2,1,0:T(8,128)S(1)} %get-tuple-element.34), channel_id=1, replica_groups=mesh['src'=8,'tgt'=16] {'src'}, dimensions={0} | all-to-all | bytes 131072 | tf_op jit(solution)/shard_map/all_to_all | solution.py:425
  64.0 4.9 %row_pass.1 = f32[16,16,128]{2,1,0:T(8,128)S(1)} custom-call(f32[2048,2048]{1,0:T(8,128)S(1)} %get-tuple-element.31.score_ref, f32[8,16,128]{2,1,0:T(8,128)S(1)} %all_to_all.21.parts_ref), custom_call_target="tpu_custom_call" | custom-call | tf_op jit(solution)/shard_map/row_pass/pallas_call | solution.py:386
  68.8 9.7 %all_to_all.22.parts_ref = f32[16,16,128]{2,1,0:T(8,128)S(1)} all-to-all(f32[16,16,128]{2,1,0:T(8,128)S(1)} %row_pass.1), channel_id=1, replica_groups=mesh['src'=8,'tgt'=16] {'tgt'}, dimensions={0} | all-to-all | bytes 262144 | tf_op jit(solution)/shard_map/all_to_all | solution.py:425
  78.5 4.5 %col_pass.3 = (f32[16,128]{1,0:T(8,128)}, f32[8,16,128]{2,1,0:T(8,128)S(1)}) custom-call(f32[2048,2048]{1,0:T(8,128)S(1)} %get-tuple-element.31.score_ref, f32[16,16,128]{2,1,0:T(8,128)S(1)} %all_to_all.22.parts_ref, f32[16,128]{1,0:T(8,128)S(1)} %get-tuple-element.33.sq_ref), custom_call_target="tpu_custom_call" | custom-call | tf_op jit(solution)/shard_map/col_pass/pallas_call | solution.py:400
  83.0 9.4 %all_to_all.23.parts_ref = f32[8,16,128]{2,1,0:T(8,128)S(1)} all-to-all(f32[8,16,128]{2,1,0:T(8,128)S(1)} %get-tuple-element.36), channel_id=1, replica_groups=mesh['src'=8,'tgt'=16] {'src'}, dimensions={0} | all-to-all | bytes 131072 | tf_op jit(solution)/shard_map/all_to_all | solution.py:425
  92.4 0.6 last.1
  (16 shorter events, 0.2 us)
Async XLA Ops:
  0.6 10.8 %collective-permute-start.3 = (bf16[256,512]{1,0:T(8,128)(2,1)}, bf16[256,512]{1,0:T(8,128)(2,1)S(1)}, u32[]{:S(2)}, u32[]{:S(2)}) collective-permute-start(bf16[256,512]{1,0:T(8,128)(2,1)} %refs_1_.1), channel_id=1, source_target_pairs={{0,16},{1,17},{2,18},{3,19},{4,20},{5,21},{6,22},{7,23},{8,24},{9,... | collective-permute-start | bytes 786440 | tf_op jit(solution)/shard_map/ppermute | solution.py:433
  2.1 9.3 %collective-permute-start = (bf16[128,512]{1,0:T(8,128)(2,1)}, bf16[128,512]{1,0:T(8,128)(2,1)S(1)}, u32[]{:S(2)}, u32[]{:S(2)}) collective-permute-start(bf16[128,512]{1,0:T(8,128)(2,1)} %refs_0_.1), channel_id=1, source_target_pairs={{0,1},{1,2},{2,3},{3,0},{4,5},{5,6},{6,7},{7,4},{8,9},{9,10},{10,1... | collective-permute-start | bytes 393224 | tf_op jit(solution)/shard_map/ppermute | solution.py:433
  3.5 8.2 %collective-permute-start.1 = (bf16[128,512]{1,0:T(8,128)(2,1)}, bf16[128,512]{1,0:T(8,128)(2,1)S(1)}, u32[]{:S(2)}, u32[]{:S(2)}) collective-permute-start(bf16[128,512]{1,0:T(8,128)(2,1)} %refs_0_.1), channel_id=1, source_target_pairs={{0,3},{1,0},{2,1},{3,2},{4,7},{5,4},{6,5},{7,6},{8,11},{9,8},{10,9... | collective-permute-start | bytes 393224 | tf_op jit(solution)/shard_map/ppermute | solution.py:433
  5.0 6.8 %collective-permute-start.2 = (bf16[128,512]{1,0:T(8,128)(2,1)}, bf16[128,512]{1,0:T(8,128)(2,1)S(1)}, u32[]{:S(2)}, u32[]{:S(2)}) collective-permute-start(bf16[128,512]{1,0:T(8,128)(2,1)} %refs_0_.1), channel_id=1, source_target_pairs={{0,2},{1,3},{2,0},{3,1},{4,6},{5,7},{6,4},{7,5},{8,10},{9,11},{10,... | collective-permute-start | bytes 393224 | tf_op jit(solution)/shard_map/ppermute | solution.py:433
  6.6 7.7 %collective-permute-start.4 = (bf16[256,512]{1,0:T(8,128)(2,1)}, bf16[256,512]{1,0:T(8,128)(2,1)S(1)}, u32[]{:S(2)}, u32[]{:S(2)}) collective-permute-start(bf16[256,512]{1,0:T(8,128)(2,1)} %refs_1_.1), channel_id=1, source_target_pairs={{0,32},{1,33},{2,34},{3,35},{4,36},{5,37},{6,38},{7,39},{8,40},{9,... | collective-permute-start | bytes 786440 | tf_op jit(solution)/shard_map/ppermute | solution.py:433
  11.5 5.6 %collective-permute-start.5 = (bf16[256,512]{1,0:T(8,128)(2,1)S(1)}, bf16[256,512]{1,0:T(8,128)(2,1)S(1)}, u32[]{:S(2)}, u32[]{:S(2)}) collective-permute-start(bf16[256,512]{1,0:T(8,128)(2,1)S(1)} %collective-permute-done.3.other_ref), channel_id=1, source_target_pairs={{0,32},{1,33},{2,34},{3,35},{4,36},{5,37},{6,38},{7,39},{8,40},{9,... | collective-permute-start | bytes 786440 | tf_op jit(solution)/shard_map/ppermute | solution.py:433
  11.7 12.3 %collective-permute-start.10 = (bf16[512,512]{1,0:T(8,128)(2,1)S(1)}, bf16[512,512]{1,0:T(8,128)(2,1)S(1)}, u32[]{:S(2)}, u32[]{:S(2)}) collective-permute-start(bf16[512,512]{1,0:T(8,128)(2,1)S(1)} %constant_dynamic-update-slice_fusion.refs_1_.points_ref), channel_id=1, source_target_pairs={{0,12},{1,13},{2,14},{3,15},{4,0},{5,1},{6,2},{7,3},{8,4},{9,5},{1... | collective-permute-start | bytes 1572872 | tf_op jit(solution)/shard_map/ppermute | solution.py:433
  14.3 9.5 %collective-permute-start.9 = (bf16[512,512]{1,0:T(8,128)(2,1)S(1)}, bf16[512,512]{1,0:T(8,128)(2,1)S(1)}, u32[]{:S(2)}, u32[]{:S(2)}) collective-permute-start(bf16[512,512]{1,0:T(8,128)(2,1)S(1)} %constant_dynamic-update-slice_fusion.refs_1_.points_ref), channel_id=1, source_target_pairs={{0,4},{1,5},{2,6},{3,7},{4,8},{5,9},{6,10},{7,11},{8,12},{9,13},{1... | collective-permute-start | bytes 1572872 | tf_op jit(solution)/shard_map/ppermute | solution.py:433
  14.3 6.1 %collective-permute-start.6 = (bf16[256,512]{1,0:T(8,128)(2,1)S(1)}, bf16[256,512]{1,0:T(8,128)(2,1)S(1)}, u32[]{:S(2)}, u32[]{:S(2)}) collective-permute-start(bf16[256,512]{1,0:T(8,128)(2,1)S(1)} %after.1), channel_id=1, source_target_pairs={{0,32},{1,33},{2,34},{3,35},{4,36},{5,37},{6,38},{7,39},{8,40},{9,... | collective-permute-start | bytes 786440 | tf_op jit(solution)/shard_map/ppermute | solution.py:433
  17.1 9.7 %collective-permute-start.7 = (bf16[512,512]{1,0:T(8,128)(2,1)S(1)}, bf16[512,512]{1,0:T(8,128)(2,1)S(1)}, u32[]{:S(2)}, u32[]{:S(2)}) collective-permute-start(bf16[512,512]{1,0:T(8,128)(2,1)S(1)} %pad_maximum_fusion), channel_id=1, source_target_pairs={{0,16},{1,17},{2,18},{3,19},{4,20},{5,21},{6,22},{7,23},{8,24},{9,... | collective-permute-start | bytes 1572872 | tf_op jit(solution)/shard_map/ppermute | solution.py:433
  20.4 6.4 %collective-permute-start.8 = (bf16[256,512]{1,0:T(8,128)(2,1)S(1)}, bf16[256,512]{1,0:T(8,128)(2,1)S(1)}, u32[]{:S(2)}, u32[]{:S(2)}) collective-permute-start(bf16[256,512]{1,0:T(8,128)(2,1)S(1)} %collective-permute-done.6.far_ref), channel_id=1, source_target_pairs={{0,16},{1,17},{2,18},{3,19},{4,20},{5,21},{6,22},{7,23},{8,24},{9,... | collective-permute-start | bytes 786440 | tf_op jit(solution)/shard_map/ppermute | solution.py:433
  23.8 9.9 %collective-permute-start.11 = (bf16[256,512]{1,0:T(8,128)(2,1)S(1)}, bf16[256,512]{1,0:T(8,128)(2,1)S(1)}, u32[]{:S(2)}, u32[]{:S(2)}) collective-permute-start(bf16[256,512]{1,0:T(8,128)(2,1)S(1)} %slice.8), channel_id=1, source_target_pairs={{0,4},{1,5},{2,6},{3,7},{4,8},{5,9},{6,10},{7,11},{8,12},{9,13},{1... | collective-permute-start | bytes 786440 | tf_op jit(solution)/shard_map/ppermute | solution.py:433
  24.1 9.7 %collective-permute-start.12 = (bf16[256,512]{1,0:T(8,128)(2,1)S(1)}, bf16[256,512]{1,0:T(8,128)(2,1)S(1)}, u32[]{:S(2)}, u32[]{:S(2)}) collective-permute-start(bf16[256,512]{1,0:T(8,128)(2,1)S(1)} %slice.9), channel_id=1, source_target_pairs={{0,12},{1,13},{2,14},{3,15},{4,0},{5,1},{6,2},{7,3},{8,4},{9,5},{1... | collective-permute-start | bytes 786440 | tf_op jit(solution)/shard_map/ppermute | solution.py:433

commit v3 on v2

--- a/solution.py
+++ b/solution.py
@@ -13,7 +13,7 @@
 
 
 EPSILON = 0.05
-UNIT = EPSILON
+UNIT = EPSILON * math.log(2.0)
 
 LANES = 128
 SUB = 8
@@ -32,14 +32,14 @@
 
 def merge(peaks, totals):
     peak = jnp.max(peaks, axis=0, keepdims=True)
-    return peak + jnp.log(jnp.sum(totals * jnp.exp(peaks - peak), axis=0, keepdims=True))
+    return peak + jnp.log2(jnp.sum(totals * jnp.exp2(peaks - peak), axis=0, keepdims=True))
 
 
 def merge_parts(parts_ref, count, out_ref):
     parts = [parts_ref[i] for i in range(parts_ref.shape[0])]
     peak = tree(jnp.maximum, parts)
-    total = tree(jnp.add, [jnp.exp(part - peak) for part in parts])
-    out_ref[...] = math.log(count) - (peak + jnp.log(total))
+    total = tree(jnp.add, [jnp.exp2(part - peak) for part in parts])
+    out_ref[...] = math.log2(count) - (peak + jnp.log2(total))
 
 
 def repeat(part_ref, part):
@@ -47,31 +47,26 @@
         part_ref[copy] = part
 
 
-def stacked(first, second):
-    return jnp.concatenate([first, second], axis=0)
-
-
 def power_sum(tiles, peak):
-    both = [
-        jnp.exp(stacked(tiles[i] - peak, tiles[i + 1] - peak).astype(jnp.bfloat16))
-        for i in range(0, len(tiles), 2)
-    ]
-    total = tree(jnp.add, both).astype(jnp.float32)
-    return total[:SUB] + total[SUB:]
+    return tree(jnp.add, [jnp.exp2(tile - peak) for tile in tiles])
 
 
 def lane_tiles(rows):
     return [rows[:, k : k + LANES] for k in range(0, rows.shape[1], LANES)]
 
 
-def row_part(load, pots):
-    peaks, totals = [], []
-    for first in range(0, LANES, SUB):
-        tiles = [tile + pot for tile, pot in zip(lane_tiles(load(first)), pots)]
+def reduce_rows(score_ref, start, groups, pots, peaks, totals):
+    for group in groups:
+        rows = pl.ds(start + group * SUB, SUB)
+        tiles = [tile + pot for tile, pot in zip(lane_tiles(score_ref[rows, :]), pots)]
         peak = tree(jnp.maximum, tiles)
-        peaks.append(peak)
-        totals.append(power_sum(tiles, peak))
-    return merge(jnp.concatenate(peaks, axis=0).T, jnp.concatenate(totals, axis=0).T)
+        at = group * SUB
+        peaks[at : at + SUB, :] = peak
+        totals[at : at + SUB, :] = power_sum(tiles, peak)
+
+
+def merge_rows(peaks, totals):
+    return merge(peaks[...].T, totals[...].T)
 
 
 def pot_rows(pot_ref):
@@ -127,87 +122,76 @@
 CHUNK = 256
 
 
-def block_pipeline(points_ref, index_of, tgt_ref, pot_ref, score_ref, rows_ref, sq_ref, held, peaks, totals):
-    step, cols = held[0].shape
-    per = step // LANES
-    steps = points_ref.shape[0] // step
-    chunks = cols // CHUNK
+def row_index(block):
+    own, core = lax.axis_index("tgt"), lax.axis_index("src") % 2
+    y, x = own // 4, own % 4
+    line, place = y + core * (x - y), x + core * (y - x)
+    at = block % 4
+    by = at + 2 * (at % 2) * (1 - at // 2) - at // 2
+    to_line, to_place = (line + block // 4) % 4, (place + by) % 4
+    return to_line * (4 - 3 * core) + to_place * (1 + 3 * core)
+
+
+def block_pipeline(sources, tgt_ref, pot_ref, score_ref, rows_ref, sq_ref, peaks, totals):
+    per = STEP // LANES
+    chunks = tgt_ref.shape[0] // CHUNK
     pots = pot_rows(pot_ref)
 
     def product(at, chunk):
-        points = points_ref[at * step : (at + 1) * step, :]
+        ref, first, block = sources[at]
+        points = ref[first : first + STEP, :]
         lanes = slice(chunk * CHUNK, (chunk + 1) * CHUNK)
-        tile = lax.dot_general(
+        score_ref[block * LANES : (block + per) * LANES, lanes] = lax.dot_general(
             points, tgt_ref[lanes, :], (((1,), (1,)), ((), ())), preferred_element_type=jnp.float32
         ) * (2.0 / UNIT)
-        held[at % 2][:, lanes] = tile
-        for sub in range(per):
-            part = slice(sub * LANES, (sub + 1) * LANES)
-            index = index_of(at * per + sub)
-            score_ref[pl.ds(pl.multiple_of(index * LANES, LANES), LANES), lanes] = tile[part]
-            if chunk == sub:
-                sq_ref[pl.ds(index, 1), :] = squares(points[part])
+        if chunk < per:
+            row = squares(points[chunk * LANES : (chunk + 1) * LANES])
+            sq_ref[pl.ds(row_index(block + chunk), 1), :] = row
 
     def reduce(at, chunk):
-        size = step // chunks
-        for first in range(chunk * size, (chunk + 1) * size, SUB):
-            rows = slice(first, first + SUB)
-            tiles = [tile + pot for tile, pot in zip(lane_tiles(held[at % 2][rows, :]), pots)]
-            peak = tree(jnp.maximum, tiles)
-            peaks[at % 2][rows, :] = peak
-            totals[at % 2][rows, :] = power_sum(tiles, peak)
+        share = chunks // per
+        sub, part = chunk // share, chunk % share
+        held = at % 2 * per + sub
+        start = (sources[at][2] + sub) * LANES
+        size = LANES // SUB // share
+        groups = range(part * size, (part + 1) * size)
+        reduce_rows(score_ref, start, groups, pots, peaks[held], totals[held])
 
     def finish(at):
         for sub in range(per):
-            part = slice(sub * LANES, (sub + 1) * LANES)
-            row = merge(peaks[at % 2][part, :].T, totals[at % 2][part, :].T)
-            rows_ref[pl.ds(index_of(at * per + sub), 1), :] = row
+            held = at % 2 * per + sub
+            row = merge_rows(peaks[held], totals[held])
+            rows_ref[pl.ds(row_index(sources[at][2] + sub), 1), :] = row
 
     for chunk in range(chunks):
         product(0, chunk)
-    for at in range(steps):
+    for at in range(len(sources)):
         for chunk in range(chunks):
-            if at + 1 < steps:
+            if at + 1 < len(sources):
                 product(at + 1, chunk)
             reduce(at, chunk)
             if at and chunk == chunks // 2:
                 finish(at - 1)
-    finish(steps - 1)
-
-
-def row_index(lines):
-    own, core = lax.axis_index("tgt"), lax.axis_index("src") % 2
-    y, x = own // 4, own % 4
-    line, place = y + core * (x - y), x + core * (y - x)
-
-    def index_of(block):
-        shift = lines[0] if len(lines) == 1 else lines[0] + block // 4 * (lines[1] - lines[0])
-        to_line, to_place = (line + shift + 4) % 4, (place + block % 4 + 3) % 4
-        return to_line * (4 - 3 * core) + to_place * (1 + 3 * core)
-
-    return index_of
+    finish(len(sources) - 1)
 
 
 def own_kernel(points_ref, tgt_ref, pot_ref, score_ref, rows_ref, src_sq_ref, *held):
-    block_pipeline(
-        points_ref, row_index((0,)), tgt_ref, pot_ref, score_ref, rows_ref, src_sq_ref,
-        held[:2], held[2:4], held[4:],
-    )
+    sources = [(points_ref, 0, 0), (points_ref, STEP, 2)]
+    block_pipeline(sources, tgt_ref, pot_ref, score_ref, rows_ref, src_sq_ref, held[:4], held[4:])
 
 
 def more_kernel(
-    lines, score_in_ref, rows_in_ref, src_sq_in_ref, first_ref, second_ref, tgt_ref, pot_ref,
-    score_ref, part_ref, src_sq_ref, rows_ref, points, *held,
+    blocks, score_in_ref, rows_in_ref, src_sq_in_ref, first_ref, second_ref, tgt_ref, pot_ref,
+    score_ref, part_ref, src_sq_ref, rows_ref, *held,
 ):
     rows_ref[...] = rows_in_ref[...]
     src_sq_ref[...] = src_sq_in_ref[...]
-    half = first_ref.shape[0]
-    points[:half, :] = first_ref[...]
-    points[half:, :] = second_ref[...]
-    block_pipeline(
-        points, row_index(lines), tgt_ref, pot_ref, score_ref, rows_ref, src_sq_ref,
-        held[:2], held[2:4], held[4:],
-    )
+    sources = [
+        (ref, first, block + first // LANES)
+        for ref, block in zip((first_ref, second_ref), blocks)
+        for first in range(0, ref.shape[0], STEP)
+    ]
+    block_pipeline(sources, tgt_ref, pot_ref, score_ref, rows_ref, src_sq_ref, held[:4], held[4:])
     repeat(part_ref, rows_ref[...])
 
 
@@ -227,17 +211,11 @@
     even, odd = held[:2], held[2:]
 
     def reduce(block, into):
-        peaks, totals = into
         start = pl.multiple_of(block * LANES, LANES)
-        for first in range(0, LANES, SUB):
-            loaded = score_ref[pl.ds(start + first, SUB), :]
-            tiles = [tile + pot for tile, pot in zip(lane_tiles(loaded), pots)]
-            peak = tree(jnp.maximum, tiles)
-            peaks[first : first + SUB, :] = peak
-            totals[first : first + SUB, :] = power_sum(tiles, peak)
+        reduce_rows(score_ref, start, range(LANES // SUB), pots, *into)
 
     def finish(block, held):
-        rows_ref[pl.ds(block, 1), :] = merge(held[0][...].T, held[1][...].T)
+        rows_ref[pl.ds(row_index(block), 1), :] = merge_rows(*held)
 
     def step(block, is_even):
         finish(block - 1, odd if is_even else even)
@@ -258,7 +236,8 @@
     blocks = rows // LANES
 
     def widen(block, into):
-        into[...] = jnp.broadcast_to(pot_ref[pl.ds(block, 1), :], (LANES, LANES)).T
+        row = pot_ref[pl.ds(row_index(block), 1), :]
+        into[...] = jnp.broadcast_to(row, (LANES, LANES)).T
 
     def reduce(block, wide):
         here = pl.ds(pl.multiple_of(block * LANES, LANES), LANES)
@@ -344,8 +323,8 @@
 STEP = 256
 
 
-def step_scratch(cols):
-    return [scratch(STEP, cols)] * 2 + [scratch(STEP, LANES)] * 4
+def step_scratch():
+    return [scratch(LANES, LANES)] * 8
 
 
 def own_pass(points, targets, pot, rows):
@@ -355,25 +334,24 @@
         out_shape=(pltpu.VMEM((rows, cols), jnp.float32), vec(rows), vec(rows)),
         in_specs=[IN_VMEM] * 3,
         out_specs=(IN_VMEM,) * 3,
-        scratch_shapes=step_scratch(cols),
+        scratch_shapes=step_scratch(),
         cost_estimate=cost(points.shape[0], cols, width),
         compiler_params=params(),
         name="own_pass",
     )(points, targets, pot)
 
 
-def more_pass(state, first, second, lines, targets, pot, copies):
+def more_pass(state, first, second, blocks, targets, pot, copies):
     score, row_parts, src_sq = state
     (rows, cols), width = score.shape, targets.shape[1]
     points = 2 * first.shape[0]
     score = pltpu.with_memory_space_constraint(score, pltpu.VMEM)
     return pl.pallas_call(
-        functools.partial(more_kernel, lines),
+        functools.partial(more_kernel, blocks),
         out_shape=(pltpu.VMEM((rows, cols), jnp.float32), vecs(copies, rows), vec(rows)),
         in_specs=[IN_VMEM] * 7,
         out_specs=(IN_VMEM,) * 3,
-        scratch_shapes=[scratch(rows // LANES, LANES), pltpu.VMEM((points, width), first.dtype)]
-        + step_scratch(cols),
+        scratch_shapes=[scratch(rows // LANES, LANES)] + step_scratch(),
         input_output_aliases={0: 0},
         cost_estimate=cost(points, cols, width),
         compiler_params=params(),
@@ -481,16 +459,16 @@
     total_tgt = tgt_points.shape[0] * n_src * n_tgt
     held, tgt_held, start = bring(own, tgt_points, tgt_start.reshape(-1, LANES))
 
-    line = jnp.concatenate([along_line(own, 1), held, along_line(own, -1), along_line(own, 2)])
+    line = jnp.concatenate([held, along_line(own, 1), along_line(own, -1), along_line(own, 2)])
     before, behind = across_lines(line, 1), across_lines(line, -1)
     far_low, far_high = across_lines(before[: 2 * size], 1), across_lines(behind[2 * size :], -1)
 
     targets, tgt_sq, red_g = place(tgt_held, *gather_targets(tgt_points, line), start)
     targets = pltpu.with_memory_space_constraint(targets, pltpu.VMEM)
     state = own_pass(line, targets, red_g, size * n_tgt)
-    score, part, src_sq = more_pass(state, before, behind, (-1, 1), targets, red_g, 1)
+    score, part, src_sq = more_pass(state, before, behind, (12, 4), targets, red_g, 1)
     state = score, part[0], src_sq
-    score, part, src_sq = more_pass(state, far_low, far_high, (2,), targets, red_g, n_tgt)
+    score, part, src_sq = more_pass(state, far_low, far_high, (8, 10), targets, red_g, n_tgt)
     score = pltpu.with_memory_space_constraint(score, pltpu.VMEM)
     for step in range(ITERS):
         if step:

time: 93.3 us -> 92.9 us (level)
  Pallas kernels: 24.6 us -> 23.4 us
  transfers between devices with their start and end apart: 13 -> 13, of which waited for: 1 -> 1; matrix products, arithmetic and copies ran while one was open for 0% -> 0% of each run, Pallas kernels for 9% -> 8%
where the time goes in v3:
time: 92.9 us; the launch traced here: 92.6 us
  blocking collectives  43.4 us (47%)
  starting transfers between devices  23.4 us (25%)
  Pallas kernels  23.4 us (25%)
  waiting for transfers between devices  1.58 us (2%)
    all_to_all x4, blocking collectives, exchange(): return lax.all_to_all(part, axis, 0, 0, tiled=True)  43.4 us
    ppermute x13, starting transfers between devices, move(): return lax.ppermute(block, ('src', 'tgt'), pairs)  23.4 us
    pallas_call x2, Pallas kernels, col_pass_call(): pl.pallas_call(functools.partial(col_kernel, count), out_shape=(vec(rows)...  8.87 us
    pallas_call x2, Pallas kernels, more_pass(): pl.pallas_call(functools.partial(more_kernel, blocks), out_shape=(pltpu.V...  5.52 us
    pallas_call x1, Pallas kernels, row_pass_call(): pl.pallas_call(functools.partial(row_kernel, count), out_shape=vecs(copie...  4.83 us
    pallas_call x1, Pallas kernels, own_pass(): pl.pallas_call(own_kernel, out_shape=(pltpu.VMEM((rows, cols), jnp.float3...  1.92 us
  transfers between devices with their start and end apart: 13, of which 1 were waited for; matrix products, arithmetic and copies ran while one was open for 0% of the time, Pallas kernels for 8%

profile of v3, /device:TPU:1, one launch (start us, length us, event | category | flops | bytes accessed | tf_op | source)
XLA Modules:
  0.0 92.6 jit_solution(14231487846014634289)
XLA Ops:
  0.6 1.5 %collective-permute-start.3 = (bf16[256,512]{1,0:T(8,128)(2,1)}, bf16[256,512]{1,0:T(8,128)(2,1)S(1)}, u32[]{:S(2)}, u32[]{:S(2)}) collective-permute-start(bf16[256,512]{1,0:T(8,128)(2,1)} %refs_1_.1), channel_id=1, source_target_pairs={{0,16},{1,17},{2,18},{3,19},{4,20},{5,21},{6,22},{7,23},{8,24},{9,... | collective-permute-start | bytes 786440 | tf_op jit(solution)/shard_map/ppermute | solution.py:411
  2.1 1.4 %collective-permute-start = (bf16[128,512]{1,0:T(8,128)(2,1)}, bf16[128,512]{1,0:T(8,128)(2,1)S(1)}, u32[]{:S(2)}, u32[]{:S(2)}) collective-permute-start(bf16[128,512]{1,0:T(8,128)(2,1)} %refs_0_.1), channel_id=1, source_target_pairs={{0,1},{1,2},{2,3},{3,0},{4,5},{5,6},{6,7},{7,4},{8,9},{9,10},{10,1... | collective-permute-start | bytes 393224 | tf_op jit(solution)/shard_map/ppermute | solution.py:411
  3.5 1.4 %collective-permute-start.1 = (bf16[128,512]{1,0:T(8,128)(2,1)}, bf16[128,512]{1,0:T(8,128)(2,1)S(1)}, u32[]{:S(2)}, u32[]{:S(2)}) collective-permute-start(bf16[128,512]{1,0:T(8,128)(2,1)} %refs_0_.1), channel_id=1, source_target_pairs={{0,3},{1,0},{2,1},{3,2},{4,7},{5,4},{6,5},{7,6},{8,11},{9,8},{10,9... | collective-permute-start | bytes 393224 | tf_op jit(solution)/shard_map/ppermute | solution.py:411
  5.0 1.6 %collective-permute-start.2 = (bf16[128,512]{1,0:T(8,128)(2,1)}, bf16[128,512]{1,0:T(8,128)(2,1)S(1)}, u32[]{:S(2)}, u32[]{:S(2)}) collective-permute-start(bf16[128,512]{1,0:T(8,128)(2,1)} %refs_0_.1), channel_id=1, source_target_pairs={{0,2},{1,3},{2,0},{3,1},{4,6},{5,7},{6,4},{7,5},{8,10},{9,11},{10,... | collective-permute-start | bytes 393224 | tf_op jit(solution)/shard_map/ppermute | solution.py:411
  6.6 3.8 %collective-permute-start.4 = (bf16[256,512]{1,0:T(8,128)(2,1)}, bf16[256,512]{1,0:T(8,128)(2,1)S(1)}, u32[]{:S(2)}, u32[]{:S(2)}) collective-permute-start(bf16[256,512]{1,0:T(8,128)(2,1)} %refs_1_.1), channel_id=1, source_target_pairs={{0,32},{1,33},{2,34},{3,35},{4,36},{5,37},{6,38},{7,39},{8,40},{9,... | collective-permute-start | bytes 786440 | tf_op jit(solution)/shard_map/ppermute | solution.py:411
  10.4 1.1 %bring.1 = (bf16[128,512]{1,0:T(8,128)(2,1)S(1)}, bf16[256,512]{1,0:T(8,128)(2,1)S(1)}, f32[16,128]{1,0:T(8,128)S(1)}) custom-call(bf16[128,512]{1,0:T(8,128)(2,1)} %refs_0_.1, bf16[256,512]{1,0:T(8,128)(2,1)} %refs_1_.1, f32[16,128]{1,0:T(8,128)} %bitcast.5), custom_call_target="tpu_custom_call" | custom-call | tf_op jit(solution)/shard_map/bring/pallas_call | solution.py:306
  11.4 0.0 collective-permute-done.3.other_ref
  11.4 0.2 collective-permute-start.5
  11.7 0.0 collective-permute-done.2
  11.7 2.5 %collective-permute-start.10 = (bf16[512,512]{1,0:T(8,128)(2,1)S(1)}, bf16[512,512]{1,0:T(8,128)(2,1)S(1)}, u32[]{:S(2)}, u32[]{:S(2)}) collective-permute-start(bf16[512,512]{1,0:T(8,128)(2,1)S(1)} %constant_dynamic-update-slice_fusion.refs_1_.points_ref), channel_id=1, source_target_pairs={{0,12},{1,13},{2,14},{3,15},{4,0},{5,1},{6,2},{7,3},{8,4},{9,5},{1... | collective-permute-start | bytes 1572872 | tf_op jit(solution)/shard_map/ppermute | solution.py:411
  14.3 2.8 %collective-permute-start.6 = (bf16[256,512]{1,0:T(8,128)(2,1)S(1)}, bf16[256,512]{1,0:T(8,128)(2,1)S(1)}, u32[]{:S(2)}, u32[]{:S(2)}) collective-permute-start(bf16[256,512]{1,0:T(8,128)(2,1)S(1)} %after.1), channel_id=1, source_target_pairs={{0,32},{1,33},{2,34},{3,35},{4,36},{5,37},{6,38},{7,39},{8,40},{9,... | collective-permute-start | bytes 786440 | tf_op jit(solution)/shard_map/ppermute | solution.py:411
  17.1 0.0 collective-permute-done.5.side_other_ref
  17.1 1.7 %collective-permute-start.7 = (bf16[512,512]{1,0:T(8,128)(2,1)S(1)}, bf16[512,512]{1,0:T(8,128)(2,1)S(1)}, u32[]{:S(2)}, u32[]{:S(2)}) collective-permute-start(bf16[512,512]{1,0:T(8,128)(2,1)S(1)} %pad_maximum_fusion), channel_id=1, source_target_pairs={{0,16},{1,17},{2,18},{3,19},{4,20},{5,21},{6,22},{7,23},{8,24},{9,... | collective-permute-start | bytes 1572872 | tf_op jit(solution)/shard_map/ppermute | solution.py:411
  18.9 1.5 %collective-permute-done.6.far_ref = bf16[256,512]{1,0:T(8,128)(2,1)S(1)} collective-permute-done((bf16[256,512]{1,0:T(8,128)(2,1)S(1)}, bf16[256,512]{1,0:T(8,128)(2,1)S(1)}, u32[]{:S(2)}, u32[]{:S(2)}) %collective-permute-start.6) | collective-permute-done | bytes 262176 | tf_op jit(solution)/shard_map/ppermute | solution.py:411
  20.4 3.4 %collective-permute-start.8 = (bf16[256,512]{1,0:T(8,128)(2,1)S(1)}, bf16[256,512]{1,0:T(8,128)(2,1)S(1)}, u32[]{:S(2)}, u32[]{:S(2)}) collective-permute-start(bf16[256,512]{1,0:T(8,128)(2,1)S(1)} %collective-permute-done.6.far_ref), channel_id=1, source_target_pairs={{0,16},{1,17},{2,18},{3,19},{4,20},{5,21},{6,22},{7,23},{8,24},{9,... | collective-permute-start | bytes 786440 | tf_op jit(solution)/shard_map/ppermute | solution.py:411
  23.8 0.0 collective-permute-done.9.first_ref
  23.8 0.2 collective-permute-start.11
  24.0 0.0 collective-permute-done.10.second_ref
  24.1 2.8 %collective-permute-start.12 = (bf16[256,512]{1,0:T(8,128)(2,1)S(1)}, bf16[256,512]{1,0:T(8,128)(2,1)S(1)}, u32[]{:S(2)}, u32[]{:S(2)}) collective-permute-start(bf16[256,512]{1,0:T(8,128)(2,1)S(1)} %slice.9), channel_id=1, source_target_pairs={{0,12},{1,13},{2,14},{3,15},{4,0},{5,1},{6,2},{7,3},{8,4},{9,5},{1... | collective-permute-start | bytes 786440 | tf_op jit(solution)/shard_map/ppermute | solution.py:411
  26.9 0.0 collective-permute-done.8.theirs_far_ref
  26.9 0.5 place.1
  27.4 1.9 %own_pass.1 = (f32[2048,2048]{1,0:T(8,128)S(1)}, f32[16,128]{1,0:T(8,128)S(1)}, f32[16,128]{1,0:T(8,128)S(1)}) custom-call(bf16[512,512]{1,0:T(8,128)(2,1)S(1)} %constant_dynamic-update-slice_fusion.refs_1_.points_ref, bf16[2048,512]{1,0:T(8,128)(2,1)S(1)} %get-tuple-element.23.tgt_ref, f32[16,128]{1,0:T(8,128)S(1)} %get-tuple-element.24.pot_ref), custom_call_target="tpu_custom_call" | custom-call | flops 1073741824 | bytes 8388608 | tf_op jit(solution)/shard_map/own_pass/pallas_call | solution.py:332
  29.3 3.6 %more_pass.2 = (f32[2048,2048]{1,0:T(8,128)S(1)}, f32[1,16,128]{2,1,0:T(8,128)S(1)}, f32[16,128]{1,0:T(8,128)S(1)}) custom-call(f32[2048,2048]{1,0:T(8,128)S(1)} %get-tuple-element.25.score_in_ref, f32[16,128]{1,0:T(8,128)S(1)} %get-tuple-element.26.rows_in_ref, f32[16,128]{1,0:T(8,128)S(1)} %get-tuple-element.27.src_sq_in_ref, ...), custom_call_target="tpu_custom_call", output_to_operand_aliasing={{0}: (0, {})} | custom-call | flops 2147483648 | bytes 16777216 | tf_op jit(solution)/shard_map/more_pass/pallas_call | solution.py:349
  32.9 1.9 %more_pass.3 = (f32[2048,2048]{1,0:T(8,128)S(1)}, f32[16,16,128]{2,1,0:T(8,128)S(1)}, f32[16,128]{1,0:T(8,128)S(1)}) custom-call(f32[2048,2048]{1,0:T(8,128)S(1)} %get-tuple-element.28.score_in_ref, f32[16,128]{1,0:T(8,128)S(1)} %bitcast.4, f32[16,128]{1,0:T(8,128)S(1)} %get-tuple-element.30.src_sq_in_ref, ...), custom_call_target="tpu_custom_call", output_to_operand_aliasing={{0}: (0, {})} | custom-call | flops 1073741824 | bytes 8388608 | tf_op jit(solution)/shard_map/more_pass/pallas_call | solution.py:349
  34.9 11.4 %all_to_all.20.parts_ref = f32[16,16,128]{2,1,0:T(8,128)S(1)} all-to-all(f32[16,16,128]{2,1,0:T(8,128)S(1)} %get-tuple-element.32), channel_id=1, replica_groups=mesh['src'=8,'tgt'=16] {'tgt'}, dimensions={0} | all-to-all | bytes 262144 | tf_op jit(solution)/shard_map/all_to_all | solution.py:403
  46.2 4.4 %col_pass.2 = (f32[16,128]{1,0:T(8,128)}, f32[8,16,128]{2,1,0:T(8,128)S(1)}) custom-call(f32[2048,2048]{1,0:T(8,128)S(1)} %get-tuple-element.31.score_ref, f32[16,16,128]{2,1,0:T(8,128)S(1)} %all_to_all.20.parts_ref, f32[16,128]{1,0:T(8,128)S(1)} %get-tuple-element.33.sq_ref), custom_call_target="tpu_custom_call" | custom-call | tf_op jit(solution)/shard_map/col_pass/pallas_call | solution.py:378
  50.7 13.0 %all_to_all.21.parts_ref = f32[8,16,128]{2,1,0:T(8,128)S(1)} all-to-all(f32[8,16,128]{2,1,0:T(8,128)S(1)} %get-tuple-element.34), channel_id=1, replica_groups=mesh['src'=8,'tgt'=16] {'src'}, dimensions={0} | all-to-all | bytes 131072 | tf_op jit(solution)/shard_map/all_to_all | solution.py:403
  63.6 4.8 %row_pass.1 = f32[16,16,128]{2,1,0:T(8,128)S(1)} custom-call(f32[2048,2048]{1,0:T(8,128)S(1)} %get-tuple-element.31.score_ref, f32[8,16,128]{2,1,0:T(8,128)S(1)} %all_to_all.21.parts_ref), custom_call_target="tpu_custom_call" | custom-call | tf_op jit(solution)/shard_map/row_pass/pallas_call | solution.py:364
  68.5 9.7 %all_to_all.22.parts_ref = f32[16,16,128]{2,1,0:T(8,128)S(1)} all-to-all(f32[16,16,128]{2,1,0:T(8,128)S(1)} %row_pass.1), channel_id=1, replica_groups=mesh['src'=8,'tgt'=16] {'tgt'}, dimensions={0} | all-to-all | bytes 262144 | tf_op jit(solution)/shard_map/all_to_all | solution.py:403
  78.2 4.4 %col_pass.3 = (f32[16,128]{1,0:T(8,128)}, f32[8,16,128]{2,1,0:T(8,128)S(1)}) custom-call(f32[2048,2048]{1,0:T(8,128)S(1)} %get-tuple-element.31.score_ref, f32[16,16,128]{2,1,0:T(8,128)S(1)} %all_to_all.22.parts_ref, f32[16,128]{1,0:T(8,128)S(1)} %get-tuple-element.33.sq_ref), custom_call_target="tpu_custom_call" | custom-call | tf_op jit(solution)/shard_map/col_pass/pallas_call | solution.py:378
  82.6 9.4 %all_to_all.23.parts_ref = f32[8,16,128]{2,1,0:T(8,128)S(1)} all-to-all(f32[8,16,128]{2,1,0:T(8,128)S(1)} %get-tuple-element.36), channel_id=1, replica_groups=mesh['src'=8,'tgt'=16] {'src'}, dimensions={0} | all-to-all | bytes 131072 | tf_op jit(solution)/shard_map/all_to_all | solution.py:403
  92.0 0.6 last.1
  (16 shorter events, 0.2 us)
Async XLA Ops:
  0.6 10.8 %collective-permute-start.3 = (bf16[256,512]{1,0:T(8,128)(2,1)}, bf16[256,512]{1,0:T(8,128)(2,1)S(1)}, u32[]{:S(2)}, u32[]{:S(2)}) collective-permute-start(bf16[256,512]{1,0:T(8,128)(2,1)} %refs_1_.1), channel_id=1, source_target_pairs={{0,16},{1,17},{2,18},{3,19},{4,20},{5,21},{6,22},{7,23},{8,24},{9,... | collective-permute-start | bytes 786440 | tf_op jit(solution)/shard_map/ppermute | solution.py:411
  2.1 9.5 %collective-permute-start = (bf16[128,512]{1,0:T(8,128)(2,1)}, bf16[128,512]{1,0:T(8,128)(2,1)S(1)}, u32[]{:S(2)}, u32[]{:S(2)}) collective-permute-start(bf16[128,512]{1,0:T(8,128)(2,1)} %refs_0_.1), channel_id=1, source_target_pairs={{0,1},{1,2},{2,3},{3,0},{4,5},{5,6},{6,7},{7,4},{8,9},{9,10},{10,1... | collective-permute-start | bytes 393224 | tf_op jit(solution)/shard_map/ppermute | solution.py:411
  3.5 8.1 %collective-permute-start.1 = (bf16[128,512]{1,0:T(8,128)(2,1)}, bf16[128,512]{1,0:T(8,128)(2,1)S(1)}, u32[]{:S(2)}, u32[]{:S(2)}) collective-permute-start(bf16[128,512]{1,0:T(8,128)(2,1)} %refs_0_.1), channel_id=1, source_target_pairs={{0,3},{1,0},{2,1},{3,2},{4,7},{5,4},{6,5},{7,6},{8,11},{9,8},{10,9... | collective-permute-start | bytes 393224 | tf_op jit(solution)/shard_map/ppermute | solution.py:411
  5.0 6.7 %collective-permute-start.2 = (bf16[128,512]{1,0:T(8,128)(2,1)}, bf16[128,512]{1,0:T(8,128)(2,1)S(1)}, u32[]{:S(2)}, u32[]{:S(2)}) collective-permute-start(bf16[128,512]{1,0:T(8,128)(2,1)} %refs_0_.1), channel_id=1, source_target_pairs={{0,2},{1,3},{2,0},{3,1},{4,6},{5,7},{6,4},{7,5},{8,10},{9,11},{10,... | collective-permute-start | bytes 393224 | tf_op jit(solution)/shard_map/ppermute | solution.py:411
  6.6 7.7 %collective-permute-start.4 = (bf16[256,512]{1,0:T(8,128)(2,1)}, bf16[256,512]{1,0:T(8,128)(2,1)S(1)}, u32[]{:S(2)}, u32[]{:S(2)}) collective-permute-start(bf16[256,512]{1,0:T(8,128)(2,1)} %refs_1_.1), channel_id=1, source_target_pairs={{0,32},{1,33},{2,34},{3,35},{4,36},{5,37},{6,38},{7,39},{8,40},{9,... | collective-permute-start | bytes 786440 | tf_op jit(solution)/shard_map/ppermute | solution.py:411
  11.4 5.7 %collective-permute-start.5 = (bf16[256,512]{1,0:T(8,128)(2,1)S(1)}, bf16[256,512]{1,0:T(8,128)(2,1)S(1)}, u32[]{:S(2)}, u32[]{:S(2)}) collective-permute-start(bf16[256,512]{1,0:T(8,128)(2,1)S(1)} %collective-permute-done.3.other_ref), channel_id=1, source_target_pairs={{0,32},{1,33},{2,34},{3,35},{4,36},{5,37},{6,38},{7,39},{8,40},{9,... | collective-permute-start | bytes 786440 | tf_op jit(solution)/shard_map/ppermute | solution.py:411
  11.7 12.3 %collective-permute-start.10 = (bf16[512,512]{1,0:T(8,128)(2,1)S(1)}, bf16[512,512]{1,0:T(8,128)(2,1)S(1)}, u32[]{:S(2)}, u32[]{:S(2)}) collective-permute-start(bf16[512,512]{1,0:T(8,128)(2,1)S(1)} %constant_dynamic-update-slice_fusion.refs_1_.points_ref), channel_id=1, source_target_pairs={{0,12},{1,13},{2,14},{3,15},{4,0},{5,1},{6,2},{7,3},{8,4},{9,5},{1... | collective-permute-start | bytes 1572872 | tf_op jit(solution)/shard_map/ppermute | solution.py:411
  14.3 9.6 %collective-permute-start.9 = (bf16[512,512]{1,0:T(8,128)(2,1)S(1)}, bf16[512,512]{1,0:T(8,128)(2,1)S(1)}, u32[]{:S(2)}, u32[]{:S(2)}) collective-permute-start(bf16[512,512]{1,0:T(8,128)(2,1)S(1)} %constant_dynamic-update-slice_fusion.refs_1_.points_ref), channel_id=1, source_target_pairs={{0,4},{1,5},{2,6},{3,7},{4,8},{5,9},{6,10},{7,11},{8,12},{9,13},{1... | collective-permute-start | bytes 1572872 | tf_op jit(solution)/shard_map/ppermute | solution.py:411
  14.3 6.1 %collective-permute-start.6 = (bf16[256,512]{1,0:T(8,128)(2,1)S(1)}, bf16[256,512]{1,0:T(8,128)(2,1)S(1)}, u32[]{:S(2)}, u32[]{:S(2)}) collective-permute-start(bf16[256,512]{1,0:T(8,128)(2,1)S(1)} %after.1), channel_id=1, source_target_pairs={{0,32},{1,33},{2,34},{3,35},{4,36},{5,37},{6,38},{7,39},{8,40},{9,... | collective-permute-start | bytes 786440 | tf_op jit(solution)/shard_map/ppermute | solution.py:411
  17.1 9.7 %collective-permute-start.7 = (bf16[512,512]{1,0:T(8,128)(2,1)S(1)}, bf16[512,512]{1,0:T(8,128)(2,1)S(1)}, u32[]{:S(2)}, u32[]{:S(2)}) collective-permute-start(bf16[512,512]{1,0:T(8,128)(2,1)S(1)} %pad_maximum_fusion), channel_id=1, source_target_pairs={{0,16},{1,17},{2,18},{3,19},{4,20},{5,21},{6,22},{7,23},{8,24},{9,... | collective-permute-start | bytes 1572872 | tf_op jit(solution)/shard_map/ppermute | solution.py:411
  20.4 6.4 %collective-permute-start.8 = (bf16[256,512]{1,0:T(8,128)(2,1)S(1)}, bf16[256,512]{1,0:T(8,128)(2,1)S(1)}, u32[]{:S(2)}, u32[]{:S(2)}) collective-permute-start(bf16[256,512]{1,0:T(8,128)(2,1)S(1)} %collective-permute-done.6.far_ref), channel_id=1, source_target_pairs={{0,16},{1,17},{2,18},{3,19},{4,20},{5,21},{6,22},{7,23},{8,24},{9,... | collective-permute-start | bytes 786440 | tf_op jit(solution)/shard_map/ppermute | solution.py:411
  23.8 9.1 %collective-permute-start.11 = (bf16[256,512]{1,0:T(8,128)(2,1)S(1)}, bf16[256,512]{1,0:T(8,128)(2,1)S(1)}, u32[]{:S(2)}, u32[]{:S(2)}) collective-permute-start(bf16[256,512]{1,0:T(8,128)(2,1)S(1)} %slice.8), channel_id=1, source_target_pairs={{0,4},{1,5},{2,6},{3,7},{4,8},{5,9},{6,10},{7,11},{8,12},{9,13},{1... | collective-permute-start | bytes 786440 | tf_op jit(solution)/shard_map/ppermute | solution.py:411
  24.1 8.8 %collective-permute-start.12 = (bf16[256,512]{1,0:T(8,128)(2,1)S(1)}, bf16[256,512]{1,0:T(8,128)(2,1)S(1)}, u32[]{:S(2)}, u32[]{:S(2)}) collective-permute-start(bf16[256,512]{1,0:T(8,128)(2,1)S(1)} %slice.9), channel_id=1, source_target_pairs={{0,12},{1,13},{2,14},{3,15},{4,0},{5,1},{6,2},{7,3},{8,4},{9,5},{1... | collective-permute-start | bytes 786440 | tf_op jit(solution)/shard_map/ppermute | solution.py:411

commit v4 on v3

--- a/solution.py
+++ b/solution.py
@@ -181,14 +181,15 @@
 
 
 def more_kernel(
-    blocks, score_in_ref, rows_in_ref, src_sq_in_ref, first_ref, second_ref, tgt_ref, pot_ref,
-    score_ref, part_ref, src_sq_ref, rows_ref, *held,
+    blocks, score_in_ref, rows_in_ref, src_sq_in_ref, tgt_ref, pot_ref, *refs
 ):
+    point_refs, refs = refs[: len(blocks)], refs[len(blocks) :]
+    score_ref, part_ref, src_sq_ref, rows_ref, *held = refs
     rows_ref[...] = rows_in_ref[...]
     src_sq_ref[...] = src_sq_in_ref[...]
     sources = [
         (ref, first, block + first // LANES)
-        for ref, block in zip((first_ref, second_ref), blocks)
+        for ref, block in zip(point_refs, blocks)
         for first in range(0, ref.shape[0], STEP)
     ]
     block_pipeline(sources, tgt_ref, pot_ref, score_ref, rows_ref, src_sq_ref, held[:4], held[4:])
@@ -228,10 +229,9 @@
 
 
 def col_kernel(
-    count, score_ref, parts_ref, sq_ref, pot_out_ref, part_ref, pot_ref, peaks, totals, even, odd
+    count, score_ref, parts_ref, pot_ref, part_ref, peaks, totals, even, odd
 ):
     merge_parts(parts_ref, count, pot_ref)
-    pot_out_ref[...] = pot_ref[...] * UNIT + sq_ref[...]
     rows, cols = score_ref.shape
     blocks = rows // LANES
 
@@ -260,13 +260,14 @@
     reduce(blocks - 1, odd)
     for k in range(cols // LANES):
         lanes = slice(k * LANES, (k + 1) * LANES)
-        pot_ref[k : k + 1, :] = merge(peaks[:, lanes], totals[:, lanes])
-    repeat(part_ref, pot_ref[...])
-
-
-def last_kernel(count, parts_ref, sq_ref, out_ref):
-    merge_parts(parts_ref, count, out_ref)
-    out_ref[...] = out_ref[...] * UNIT + sq_ref[...]
+        part_ref[0, k : k + 1, :] = merge(peaks[:, lanes], totals[:, lanes])
+    repeat(part_ref, part_ref[0])
+
+
+def last_kernel(count, parts_ref, pot_f_ref, src_sq_ref, tgt_sq_ref, out_f_ref, out_g_ref):
+    out_f_ref[...] = pot_f_ref[...] * UNIT + src_sq_ref[...]
+    merge_parts(parts_ref, count, out_g_ref)
+    out_g_ref[...] = out_g_ref[...] * UNIT + tgt_sq_ref[...]
 
 
 def params():
@@ -341,22 +342,22 @@
     )(points, targets, pot)
 
 
-def more_pass(state, first, second, blocks, targets, pot, copies):
+def more_pass(state, points, blocks, targets, pot, copies):
     score, row_parts, src_sq = state
     (rows, cols), width = score.shape, targets.shape[1]
-    points = 2 * first.shape[0]
+    added = sum(array.shape[0] for array in points)
     score = pltpu.with_memory_space_constraint(score, pltpu.VMEM)
     return pl.pallas_call(
         functools.partial(more_kernel, blocks),
         out_shape=(pltpu.VMEM((rows, cols), jnp.float32), vecs(copies, rows), vec(rows)),
-        in_specs=[IN_VMEM] * 7,
+        in_specs=[IN_VMEM] * (5 + len(points)),
         out_specs=(IN_VMEM,) * 3,
         scratch_shapes=[scratch(rows // LANES, LANES)] + step_scratch(),
         input_output_aliases={0: 0},
-        cost_estimate=cost(points, cols, width),
+        cost_estimate=cost(added, cols, width),
         compiler_params=params(),
         name="more_pass",
-    )(score, row_parts, src_sq, first, second, targets, pot)
+    )(score, row_parts, src_sq, targets, pot, *points)
 
 
 def row_pass_call(score, parts, count, copies):
@@ -373,30 +374,28 @@
     )(score, parts)
 
 
-def col_pass_call(score, parts, sq, count, copies):
+def col_pass_call(score, parts, count, copies):
     rows, cols = score.shape
     return pl.pallas_call(
         functools.partial(col_kernel, count),
-        out_shape=(vec(rows), vecs(copies, cols)),
-        in_specs=[IN_VMEM] * 3,
+        out_shape=(pltpu.VMEM((rows // LANES, LANES), jnp.float32), vecs(copies, cols)),
+        in_specs=[IN_VMEM] * 2,
         out_specs=(IN_VMEM, IN_VMEM),
-        scratch_shapes=[scratch(max(rows, cols) // LANES, LANES)]
-        + [scratch(rows // LANES * SUB, cols)] * 2
-        + [scratch(LANES, LANES)] * 2,
+        scratch_shapes=[scratch(rows // LANES * SUB, cols)] * 2 + [scratch(LANES, LANES)] * 2,
         compiler_params=params(),
         name="col_pass",
-    )(score, parts, sq)
-
-
-def last_call(parts, sq, count):
+    )(score, parts)
+
+
+def last_call(parts, pot_f, src_sq, tgt_sq, count):
     return pl.pallas_call(
         functools.partial(last_kernel, count),
-        out_shape=jax.ShapeDtypeStruct(sq.shape, jnp.float32),
-        in_specs=[IN_VMEM] * 2,
-        out_specs=IN_VMEM,
+        out_shape=(vec(src_sq.size), vec(tgt_sq.size)),
+        in_specs=[IN_VMEM] * 4,
+        out_specs=(IN_VMEM, IN_VMEM),
         compiler_params=params(),
         name="last",
-    )(parts, sq)
+    )(parts, pltpu.with_memory_space_constraint(pot_f, pltpu.VMEM), src_sq, tgt_sq)
 
 
 def exchange(part, axis):
@@ -461,22 +460,22 @@
 
     line = jnp.concatenate([held, along_line(own, 1), along_line(own, -1), along_line(own, 2)])
     before, behind = across_lines(line, 1), across_lines(line, -1)
-    far_low, far_high = across_lines(before[: 2 * size], 1), across_lines(behind[2 * size :], -1)
+    far = across_lines(before, 1)
 
     targets, tgt_sq, red_g = place(tgt_held, *gather_targets(tgt_points, line), start)
     targets = pltpu.with_memory_space_constraint(targets, pltpu.VMEM)
     state = own_pass(line, targets, red_g, size * n_tgt)
-    score, part, src_sq = more_pass(state, before, behind, (12, 4), targets, red_g, 1)
+    score, part, src_sq = more_pass(state, (before, behind), (12, 4), targets, red_g, 1)
     state = score, part[0], src_sq
-    score, part, src_sq = more_pass(state, far_low, far_high, (8, 10), targets, red_g, n_tgt)
+    score, part, src_sq = more_pass(state, (far,), (8,), targets, red_g, n_tgt)
     score = pltpu.with_memory_space_constraint(score, pltpu.VMEM)
     for step in range(ITERS):
         if step:
             part = row_pass_call(score, parts, total_src, n_tgt)
         parts = exchange(part, "tgt")
-        pot_f, part = col_pass_call(score, parts, src_sq, total_tgt, n_src)
+        red_f, part = col_pass_call(score, parts, total_tgt, n_src)
         parts = exchange(part, "src")
-    pot_g = last_call(parts, tgt_sq, total_src)
+    pot_f, pot_g = last_call(parts, red_f, src_sq, tgt_sq, total_src)
     return (pot_f.reshape(-1), pot_g.reshape(-1))
 
 

time: 92.9 us -> 89.7 us (0.966)
  blocking collectives: 43.4 us -> 40.1 us
  waiting for transfers between devices: 1.58 us -> 4.83 us
  starting transfers between devices: 23.4 us -> 20.4 us
    all_to_all x4, blocking collectives: 43.4 us -> 40.1 us  [exchange(): return lax.all_to_all(part, axis, 0, 0, tiled=True)]
    ppermute x13 -> x12, waiting for transfers between devices: 1.58 us -> 4.83 us  [move(): return lax.ppermute(block, ('src', 'tgt'), pairs)]
    ppermute x13 -> x12, starting transfers between devices: 23.4 us -> 20.4 us  [move(): return lax.ppermute(block, ('src', 'tgt'), pairs)]
  transfers between devices with their start and end apart: 13 -> 12, of which waited for: 1 -> 4; matrix products, arithmetic and copies ran while one was open for 0% -> 0% of each run, Pallas kernels for 8% -> 8%
where the time goes in v4:
time: 89.7 us; the launch traced here: 89.4 us
  blocking collectives  40.1 us (45%)
  Pallas kernels  23.2 us (26%)
  starting transfers between devices  20.4 us (23%)
  waiting for transfers between devices  4.83 us (5%)
    all_to_all x4, blocking collectives, exchange(): return lax.all_to_all(part, axis, 0, 0, tiled=True)  40.1 us
    ppermute x12, starting transfers between devices, move(): return lax.ppermute(block, ('src', 'tgt'), pairs)  20.4 us
    pallas_call x2, Pallas kernels, col_pass_call(): pl.pallas_call(functools.partial(col_kernel, count), out_shape=(pltpu.VME...  8.7 us
    pallas_call x2, Pallas kernels, more_pass(): pl.pallas_call(functools.partial(more_kernel, blocks), out_shape=(pltpu.V...  5.5 us
    pallas_call x1, Pallas kernels, row_pass_call(): pl.pallas_call(functools.partial(row_kernel, count), out_shape=vecs(copie...  4.83 us
    ppermute x12, waiting for transfers between devices, move(): return lax.ppermute(block, ('src', 'tgt'), pairs)  4.83 us
    pallas_call x1, Pallas kernels, own_pass(): pl.pallas_call(own_kernel, out_shape=(pltpu.VMEM((rows, cols), jnp.float3...  1.92 us
  transfers between devices with their start and end apart: 12, of which 4 were waited for; matrix products, arithmetic and copies ran while one was open for 0% of the time, Pallas kernels for 8%

profile of v4, /device:TPU:1, one launch (start us, length us, event | category | flops | bytes accessed | tf_op | source)
XLA Modules:
  0.0 89.4 jit_solution(1874791282009868532)
XLA Ops:
  0.6 1.5 %collective-permute-start.3 = (bf16[256,512]{1,0:T(8,128)(2,1)}, bf16[256,512]{1,0:T(8,128)(2,1)S(1)}, u32[]{:S(2)}, u32[]{:S(2)}) collective-permute-start(bf16[256,512]{1,0:T(8,128)(2,1)} %refs_1_.1), channel_id=1, source_target_pairs={{0,16},{1,17},{2,18},{3,19},{4,20},{5,21},{6,22},{7,23},{8,24},{9,... | collective-permute-start | bytes 786440 | tf_op jit(solution)/shard_map/ppermute | solution.py:410
  2.1 1.4 %collective-permute-start = (bf16[128,512]{1,0:T(8,128)(2,1)}, bf16[128,512]{1,0:T(8,128)(2,1)S(1)}, u32[]{:S(2)}, u32[]{:S(2)}) collective-permute-start(bf16[128,512]{1,0:T(8,128)(2,1)} %refs_0_.1), channel_id=1, source_target_pairs={{0,1},{1,2},{2,3},{3,0},{4,5},{5,6},{6,7},{7,4},{8,9},{9,10},{10,1... | collective-permute-start | bytes 393224 | tf_op jit(solution)/shard_map/ppermute | solution.py:410
  3.5 1.4 %collective-permute-start.1 = (bf16[128,512]{1,0:T(8,128)(2,1)}, bf16[128,512]{1,0:T(8,128)(2,1)S(1)}, u32[]{:S(2)}, u32[]{:S(2)}) collective-permute-start(bf16[128,512]{1,0:T(8,128)(2,1)} %refs_0_.1), channel_id=1, source_target_pairs={{0,3},{1,0},{2,1},{3,2},{4,7},{5,4},{6,5},{7,6},{8,11},{9,8},{10,9... | collective-permute-start | bytes 393224 | tf_op jit(solution)/shard_map/ppermute | solution.py:410
  5.0 1.6 %collective-permute-start.2 = (bf16[128,512]{1,0:T(8,128)(2,1)}, bf16[128,512]{1,0:T(8,128)(2,1)S(1)}, u32[]{:S(2)}, u32[]{:S(2)}) collective-permute-start(bf16[128,512]{1,0:T(8,128)(2,1)} %refs_0_.1), channel_id=1, source_target_pairs={{0,2},{1,3},{2,0},{3,1},{4,6},{5,7},{6,4},{7,5},{8,10},{9,11},{10,... | collective-permute-start | bytes 393224 | tf_op jit(solution)/shard_map/ppermute | solution.py:410
  6.6 3.8 %collective-permute-start.4 = (bf16[256,512]{1,0:T(8,128)(2,1)}, bf16[256,512]{1,0:T(8,128)(2,1)S(1)}, u32[]{:S(2)}, u32[]{:S(2)}) collective-permute-start(bf16[256,512]{1,0:T(8,128)(2,1)} %refs_1_.1), channel_id=1, source_target_pairs={{0,32},{1,33},{2,34},{3,35},{4,36},{5,37},{6,38},{7,39},{8,40},{9,... | collective-permute-start | bytes 786440 | tf_op jit(solution)/shard_map/ppermute | solution.py:410
  10.4 1.1 %bring.1 = (bf16[128,512]{1,0:T(8,128)(2,1)S(1)}, bf16[256,512]{1,0:T(8,128)(2,1)S(1)}, f32[16,128]{1,0:T(8,128)S(1)}) custom-call(bf16[128,512]{1,0:T(8,128)(2,1)} %refs_0_.1, bf16[256,512]{1,0:T(8,128)(2,1)} %refs_1_.1, f32[16,128]{1,0:T(8,128)} %bitcast.5), custom_call_target="tpu_custom_call" | custom-call | tf_op jit(solution)/shard_map/bring/pallas_call | solution.py:307
  11.4 0.0 collective-permute-done
  11.5 0.0 collective-permute-done.3.other_ref
  11.5 0.2 collective-permute-start.5
  11.7 0.0 collective-permute-done.1
  11.7 1.3 %collective-permute-start.9 = (bf16[512,512]{1,0:T(8,128)(2,1)S(1)}, bf16[512,512]{1,0:T(8,128)(2,1)S(1)}, u32[]{:S(2)}, u32[]{:S(2)}) collective-permute-start(bf16[512,512]{1,0:T(8,128)(2,1)S(1)} %constant_dynamic-update-slice_fusion.refs_1_.points_ref), channel_id=1, source_target_pairs={{0,4},{1,5},{2,6},{3,7},{4,8},{5,9},{6,10},{7,11},{8,12},{9,13},{1... | collective-permute-start | bytes 1572872 | tf_op jit(solution)/shard_map/ppermute | solution.py:410
  13.0 1.0 %collective-permute-done.4.side_ref = bf16[256,512]{1,0:T(8,128)(2,1)S(1)} collective-permute-done((bf16[256,512]{1,0:T(8,128)(2,1)}, bf16[256,512]{1,0:T(8,128)(2,1)S(1)}, u32[]{:S(2)}, u32[]{:S(2)}) %collective-permute-start.4) | collective-permute-done | bytes 262176 | tf_op jit(solution)/shard_map/ppermute | solution.py:410
  14.0 3.1 %collective-permute-start.6 = (bf16[256,512]{1,0:T(8,128)(2,1)S(1)}, bf16[256,512]{1,0:T(8,128)(2,1)S(1)}, u32[]{:S(2)}, u32[]{:S(2)}) collective-permute-start(bf16[256,512]{1,0:T(8,128)(2,1)S(1)} %after.1), channel_id=1, source_target_pairs={{0,32},{1,33},{2,34},{3,35},{4,36},{5,37},{6,38},{7,39},{8,40},{9,... | collective-permute-start | bytes 786440 | tf_op jit(solution)/shard_map/ppermute | solution.py:410
  17.1 1.7 %collective-permute-start.7 = (bf16[512,512]{1,0:T(8,128)(2,1)S(1)}, bf16[512,512]{1,0:T(8,128)(2,1)S(1)}, u32[]{:S(2)}, u32[]{:S(2)}) collective-permute-start(bf16[512,512]{1,0:T(8,128)(2,1)S(1)} %pad_maximum_fusion), channel_id=1, source_target_pairs={{0,16},{1,17},{2,18},{3,19},{4,20},{5,21},{6,22},{7,23},{8,24},{9,... | collective-permute-start | bytes 1572872 | tf_op jit(solution)/shard_map/ppermute | solution.py:410
  18.9 0.9 %collective-permute-start.10 = (bf16[512,512]{1,0:T(8,128)(2,1)S(1)}, bf16[512,512]{1,0:T(8,128)(2,1)S(1)}, u32[]{:S(2)}, u32[]{:S(2)}) collective-permute-start(bf16[512,512]{1,0:T(8,128)(2,1)S(1)} %constant_dynamic-update-slice_fusion.refs_1_.points_ref), channel_id=1, source_target_pairs={{0,12},{1,13},{2,14},{3,15},{4,0},{5,1},{6,2},{7,3},{8,4},{9,5},{1... | collective-permute-start | bytes 1572872 | tf_op jit(solution)/shard_map/ppermute | solution.py:410
  19.8 0.6 collective-permute-done.6.far_ref
  20.4 3.2 %collective-permute-start.8 = (bf16[256,512]{1,0:T(8,128)(2,1)S(1)}, bf16[256,512]{1,0:T(8,128)(2,1)S(1)}, u32[]{:S(2)}, u32[]{:S(2)}) collective-permute-start(bf16[256,512]{1,0:T(8,128)(2,1)S(1)} %collective-permute-done.6.far_ref), channel_id=1, source_target_pairs={{0,16},{1,17},{2,18},{3,19},{4,20},{5,21},{6,22},{7,23},{8,24},{9,... | collective-permute-start | bytes 786440 | tf_op jit(solution)/shard_map/ppermute | solution.py:410
  23.6 0.3 collective-permute-start.11
  23.9 0.8 collective-permute-done.8.theirs_far_ref
  24.8 0.5 place.1
  25.3 1.9 %own_pass.1 = (f32[2048,2048]{1,0:T(8,128)S(1)}, f32[16,128]{1,0:T(8,128)S(1)}, f32[16,128]{1,0:T(8,128)S(1)}) custom-call(bf16[512,512]{1,0:T(8,128)(2,1)S(1)} %constant_dynamic-update-slice_fusion.refs_1_.points_ref, bf16[2048,512]{1,0:T(8,128)(2,1)S(1)} %get-tuple-element.25.tgt_ref, f32[16,128]{1,0:T(8,128)S(1)} %get-tuple-element.26.pot_ref), custom_call_target="tpu_custom_call" | custom-call | flops 1073741824 | bytes 8388608 | tf_op jit(solution)/shard_map/own_pass/pallas_call | solution.py:333
  27.3 3.6 %more_pass.2 = (f32[2048,2048]{1,0:T(8,128)S(1)}, f32[1,16,128]{2,1,0:T(8,128)S(1)}, f32[16,128]{1,0:T(8,128)S(1)}) custom-call(f32[2048,2048]{1,0:T(8,128)S(1)} %get-tuple-element.27.score_in_ref, f32[16,128]{1,0:T(8,128)S(1)} %get-tuple-element.28.rows_in_ref, f32[16,128]{1,0:T(8,128)S(1)} %get-tuple-element.29.src_sq_in_ref, ...), custom_call_target="tpu_custom_call", output_to_operand_aliasing={{0}: (0, {})} | custom-call | flops 2147483648 | bytes 16777216 | tf_op jit(solution)/shard_map/more_pass/pallas_call | solution.py:350
  30.8 2.3 %collective-permute-done.11.refs_0_ = bf16[512,512]{1,0:T(8,128)(2,1)S(1)} collective-permute-done((bf16[512,512]{1,0:T(8,128)(2,1)S(1)}, bf16[512,512]{1,0:T(8,128)(2,1)S(1)}, u32[]{:S(2)}, u32[]{:S(2)}) %collective-permute-start.11) | collective-permute-done | bytes 524320 | tf_op jit(solution)/shard_map/ppermute | solution.py:410
  33.2 1.9 %more_pass.3 = (f32[2048,2048]{1,0:T(8,128)S(1)}, f32[16,16,128]{2,1,0:T(8,128)S(1)}, f32[16,128]{1,0:T(8,128)S(1)}) custom-call(f32[2048,2048]{1,0:T(8,128)S(1)} %get-tuple-element.30.score_in_ref, f32[16,128]{1,0:T(8,128)S(1)} %bitcast.4, f32[16,128]{1,0:T(8,128)S(1)} %get-tuple-element.32.src_sq_in_ref, ...), custom_call_target="tpu_custom_call", output_to_operand_aliasing={{0}: (0, {})} | custom-call | flops 1073741824 | bytes 8388608 | tf_op jit(solution)/shard_map/more_pass/pallas_call | solution.py:350
  35.1 10.9 %all_to_all.20.parts_ref = f32[16,16,128]{2,1,0:T(8,128)S(1)} all-to-all(f32[16,16,128]{2,1,0:T(8,128)S(1)} %get-tuple-element.34), channel_id=1, replica_groups=mesh['src'=8,'tgt'=16] {'tgt'}, dimensions={0} | all-to-all | bytes 262144 | tf_op jit(solution)/shard_map/all_to_all | solution.py:402
  46.0 4.4 %col_pass.2 = (f32[16,128]{1,0:T(8,128)}, f32[8,16,128]{2,1,0:T(8,128)S(1)}) custom-call(f32[2048,2048]{1,0:T(8,128)S(1)} %get-tuple-element.33.score_ref, f32[16,16,128]{2,1,0:T(8,128)S(1)} %all_to_all.20.parts_ref), custom_call_target="tpu_custom_call" | custom-call | tf_op jit(solution)/shard_map/col_pass/pallas_call | solution.py:379
  50.4 10.2 %all_to_all.21.parts_ref = f32[8,16,128]{2,1,0:T(8,128)S(1)} all-to-all(f32[8,16,128]{2,1,0:T(8,128)S(1)} %get-tuple-element.35), channel_id=1, replica_groups=mesh['src'=8,'tgt'=16] {'src'}, dimensions={0} | all-to-all | bytes 131072 | tf_op jit(solution)/shard_map/all_to_all | solution.py:402
  60.6 4.8 %row_pass.1 = f32[16,16,128]{2,1,0:T(8,128)S(1)} custom-call(f32[2048,2048]{1,0:T(8,128)S(1)} %get-tuple-element.33.score_ref, f32[8,16,128]{2,1,0:T(8,128)S(1)} %all_to_all.21.parts_ref), custom_call_target="tpu_custom_call" | custom-call | tf_op jit(solution)/shard_map/row_pass/pallas_call | solution.py:365
  65.4 9.7 %all_to_all.22.parts_ref = f32[16,16,128]{2,1,0:T(8,128)S(1)} all-to-all(f32[16,16,128]{2,1,0:T(8,128)S(1)} %row_pass.1), channel_id=1, replica_groups=mesh['src'=8,'tgt'=16] {'tgt'}, dimensions={0} | all-to-all | bytes 262144 | tf_op jit(solution)/shard_map/all_to_all | solution.py:402
  75.1 4.3 %col_pass.3 = (f32[16,128]{1,0:T(8,128)S(1)}, f32[8,16,128]{2,1,0:T(8,128)S(1)}) custom-call(f32[2048,2048]{1,0:T(8,128)S(1)} %get-tuple-element.33.score_ref, f32[16,16,128]{2,1,0:T(8,128)S(1)} %all_to_all.22.parts_ref), custom_call_target="tpu_custom_call" | custom-call | tf_op jit(solution)/shard_map/col_pass/pallas_call | solution.py:379
  79.4 9.4 %all_to_all.23.parts_ref = f32[8,16,128]{2,1,0:T(8,128)S(1)} all-to-all(f32[8,16,128]{2,1,0:T(8,128)S(1)} %get-tuple-element.36), channel_id=1, replica_groups=mesh['src'=8,'tgt'=16] {'src'}, dimensions={0} | all-to-all | bytes 131072 | tf_op jit(solution)/shard_map/all_to_all | solution.py:402
  88.8 0.6 last.1
  (12 shorter events, 0.1 us)
Async XLA Ops:
  0.6 10.8 %collective-permute-start.3 = (bf16[256,512]{1,0:T(8,128)(2,1)}, bf16[256,512]{1,0:T(8,128)(2,1)S(1)}, u32[]{:S(2)}, u32[]{:S(2)}) collective-permute-start(bf16[256,512]{1,0:T(8,128)(2,1)} %refs_1_.1), channel_id=1, source_target_pairs={{0,16},{1,17},{2,18},{3,19},{4,20},{5,21},{6,22},{7,23},{8,24},{9,... | collective-permute-start | bytes 786440 | tf_op jit(solution)/shard_map/ppermute | solution.py:410
  2.1 9.3 %collective-permute-start = (bf16[128,512]{1,0:T(8,128)(2,1)}, bf16[128,512]{1,0:T(8,128)(2,1)S(1)}, u32[]{:S(2)}, u32[]{:S(2)}) collective-permute-start(bf16[128,512]{1,0:T(8,128)(2,1)} %refs_0_.1), channel_id=1, source_target_pairs={{0,1},{1,2},{2,3},{3,0},{4,5},{5,6},{6,7},{7,4},{8,9},{9,10},{10,1... | collective-permute-start | bytes 393224 | tf_op jit(solution)/shard_map/ppermute | solution.py:410
  3.5 8.2 %collective-permute-start.1 = (bf16[128,512]{1,0:T(8,128)(2,1)}, bf16[128,512]{1,0:T(8,128)(2,1)S(1)}, u32[]{:S(2)}, u32[]{:S(2)}) collective-permute-start(bf16[128,512]{1,0:T(8,128)(2,1)} %refs_0_.1), channel_id=1, source_target_pairs={{0,3},{1,0},{2,1},{3,2},{4,7},{5,4},{6,5},{7,6},{8,11},{9,8},{10,9... | collective-permute-start | bytes 393224 | tf_op jit(solution)/shard_map/ppermute | solution.py:410
  5.0 6.7 %collective-permute-start.2 = (bf16[128,512]{1,0:T(8,128)(2,1)}, bf16[128,512]{1,0:T(8,128)(2,1)S(1)}, u32[]{:S(2)}, u32[]{:S(2)}) collective-permute-start(bf16[128,512]{1,0:T(8,128)(2,1)} %refs_0_.1), channel_id=1, source_target_pairs={{0,2},{1,3},{2,0},{3,1},{4,6},{5,7},{6,4},{7,5},{8,10},{9,11},{10,... | collective-permute-start | bytes 393224 | tf_op jit(solution)/shard_map/ppermute | solution.py:410
  6.6 7.4 %collective-permute-start.4 = (bf16[256,512]{1,0:T(8,128)(2,1)}, bf16[256,512]{1,0:T(8,128)(2,1)S(1)}, u32[]{:S(2)}, u32[]{:S(2)}) collective-permute-start(bf16[256,512]{1,0:T(8,128)(2,1)} %refs_1_.1), channel_id=1, source_target_pairs={{0,32},{1,33},{2,34},{3,35},{4,36},{5,37},{6,38},{7,39},{8,40},{9,... | collective-permute-start | bytes 786440 | tf_op jit(solution)/shard_map/ppermute | solution.py:410
  11.5 5.6 %collective-permute-start.5 = (bf16[256,512]{1,0:T(8,128)(2,1)S(1)}, bf16[256,512]{1,0:T(8,128)(2,1)S(1)}, u32[]{:S(2)}, u32[]{:S(2)}) collective-permute-start(bf16[256,512]{1,0:T(8,128)(2,1)S(1)} %collective-permute-done.3.other_ref), channel_id=1, source_target_pairs={{0,32},{1,33},{2,34},{3,35},{4,36},{5,37},{6,38},{7,39},{8,40},{9,... | collective-permute-start | bytes 786440 | tf_op jit(solution)/shard_map/ppermute | solution.py:410
  11.7 11.9 %collective-permute-start.9 = (bf16[512,512]{1,0:T(8,128)(2,1)S(1)}, bf16[512,512]{1,0:T(8,128)(2,1)S(1)}, u32[]{:S(2)}, u32[]{:S(2)}) collective-permute-start(bf16[512,512]{1,0:T(8,128)(2,1)S(1)} %constant_dynamic-update-slice_fusion.refs_1_.points_ref), channel_id=1, source_target_pairs={{0,4},{1,5},{2,6},{3,7},{4,8},{5,9},{6,10},{7,11},{8,12},{9,13},{1... | collective-permute-start | bytes 1572872 | tf_op jit(solution)/shard_map/ppermute | solution.py:410
  14.0 6.4 %collective-permute-start.6 = (bf16[256,512]{1,0:T(8,128)(2,1)S(1)}, bf16[256,512]{1,0:T(8,128)(2,1)S(1)}, u32[]{:S(2)}, u32[]{:S(2)}) collective-permute-start(bf16[256,512]{1,0:T(8,128)(2,1)S(1)} %after.1), channel_id=1, source_target_pairs={{0,32},{1,33},{2,34},{3,35},{4,36},{5,37},{6,38},{7,39},{8,40},{9,... | collective-permute-start | bytes 786440 | tf_op jit(solution)/shard_map/ppermute | solution.py:410
  17.1 7.7 %collective-permute-start.7 = (bf16[512,512]{1,0:T(8,128)(2,1)S(1)}, bf16[512,512]{1,0:T(8,128)(2,1)S(1)}, u32[]{:S(2)}, u32[]{:S(2)}) collective-permute-start(bf16[512,512]{1,0:T(8,128)(2,1)S(1)} %pad_maximum_fusion), channel_id=1, source_target_pairs={{0,16},{1,17},{2,18},{3,19},{4,20},{5,21},{6,22},{7,23},{8,24},{9,... | collective-permute-start | bytes 1572872 | tf_op jit(solution)/shard_map/ppermute | solution.py:410
  18.9 8.4 %collective-permute-start.10 = (bf16[512,512]{1,0:T(8,128)(2,1)S(1)}, bf16[512,512]{1,0:T(8,128)(2,1)S(1)}, u32[]{:S(2)}, u32[]{:S(2)}) collective-permute-start(bf16[512,512]{1,0:T(8,128)(2,1)S(1)} %constant_dynamic-update-slice_fusion.refs_1_.points_ref), channel_id=1, source_target_pairs={{0,12},{1,13},{2,14},{3,15},{4,0},{5,1},{6,2},{7,3},{8,4},{9,5},{1... | collective-permute-start | bytes 1572872 | tf_op jit(solution)/shard_map/ppermute | solution.py:410
  20.4 4.4 %collective-permute-start.8 = (bf16[256,512]{1,0:T(8,128)(2,1)S(1)}, bf16[256,512]{1,0:T(8,128)(2,1)S(1)}, u32[]{:S(2)}, u32[]{:S(2)}) collective-permute-start(bf16[256,512]{1,0:T(8,128)(2,1)S(1)} %collective-permute-done.6.far_ref), channel_id=1, source_target_pairs={{0,16},{1,17},{2,18},{3,19},{4,20},{5,21},{6,22},{7,23},{8,24},{9,... | collective-permute-start | bytes 786440 | tf_op jit(solution)/shard_map/ppermute | solution.py:410
  23.6 9.5 %collective-permute-start.11 = (bf16[512,512]{1,0:T(8,128)(2,1)S(1)}, bf16[512,512]{1,0:T(8,128)(2,1)S(1)}, u32[]{:S(2)}, u32[]{:S(2)}) collective-permute-start(bf16[512,512]{1,0:T(8,128)(2,1)S(1)} %collective-permute-done.9.refs_0_), channel_id=1, source_target_pairs={{0,4},{1,5},{2,6},{3,7},{4,8},{5,9},{6,10},{7,11},{8,12},{9,13},{1... | collective-permute-start | bytes 1572872 | tf_op jit(solution)/shard_map/ppermute | solution.py:410

commit v5 on v4

--- a/solution.py
+++ b/solution.py
@@ -127,7 +127,7 @@
     y, x = own // 4, own % 4
     line, place = y + core * (x - y), x + core * (y - x)
     at = block % 4
-    by = at + 2 * (at % 2) * (1 - at // 2) - at // 2
+    by = at + (at + 3) // 4 + at // 3
     to_line, to_place = (line + block // 4) % 4, (place + by) % 4
     return to_line * (4 - 3 * core) + to_place * (1 + 3 * core)
 
@@ -458,15 +458,16 @@
     total_tgt = tgt_points.shape[0] * n_src * n_tgt
     held, tgt_held, start = bring(own, tgt_points, tgt_start.reshape(-1, LANES))
 
-    line = jnp.concatenate([held, along_line(own, 1), along_line(own, -1), along_line(own, 2)])
+    line = jnp.concatenate([held, along_line(own, 2), along_line(own, 1), along_line(own, -1)])
     before, behind = across_lines(line, 1), across_lines(line, -1)
     far = across_lines(before, 1)
 
     targets, tgt_sq, red_g = place(tgt_held, *gather_targets(tgt_points, line), start)
     targets = pltpu.with_memory_space_constraint(targets, pltpu.VMEM)
     state = own_pass(line, targets, red_g, size * n_tgt)
-    score, part, src_sq = more_pass(state, (before, behind), (12, 4), targets, red_g, 1)
-    state = score, part[0], src_sq
+    for points, block in ((before, 12), (behind, 4)):
+        score, part, src_sq = more_pass(state, (points,), (block,), targets, red_g, 1)
+        state = score, part[0], src_sq
     score, part, src_sq = more_pass(state, (far,), (8,), targets, red_g, n_tgt)
     score = pltpu.with_memory_space_constraint(score, pltpu.VMEM)
     for step in range(ITERS):

time: 89.7 us -> 90.2 us (level)
    ppermute x12, starting transfers between devices: 20.4 us -> 21.3 us  [move(): return lax.ppermute(block, ('src', 'tgt'), pairs)]
    pallas_call x2 -> x3, Pallas kernels: 5.5 us -> 5.76 us  [more_pass(): pl.pallas_call(functools.partial(more_kernel, blocks), out_shape=(pltpu.V...]
where the time goes in v5:
time: 90.2 us; the launch traced here: 89.9 us
  blocking collectives  40 us (44%)
  Pallas kernels  22.8 us (25%)
  starting transfers between devices  21.3 us (24%)
  waiting for transfers between devices  4.88 us (5%)
    all_to_all x4, blocking collectives, exchange(): return lax.all_to_all(part, axis, 0, 0, tiled=True)  40 us
    ppermute x12, starting transfers between devices, move(): return lax.ppermute(block, ('src', 'tgt'), pairs)  21.3 us
    pallas_call x2, Pallas kernels, col_pass_call(): pl.pallas_call(functools.partial(col_kernel, count), out_shape=(pltpu.VME...  8.35 us
    pallas_call x3, Pallas kernels, more_pass(): pl.pallas_call(functools.partial(more_kernel, blocks), out_shape=(pltpu.V...  5.76 us
    ppermute x12, waiting for transfers between devices, move(): return lax.ppermute(block, ('src', 'tgt'), pairs)  4.88 us
    pallas_call x1, Pallas kernels, row_pass_call(): pl.pallas_call(functools.partial(row_kernel, count), out_shape=vecs(copie...  4.57 us
    pallas_call x1, Pallas kernels, own_pass(): pl.pallas_call(own_kernel, out_shape=(pltpu.VMEM((rows, cols), jnp.float3...  1.91 us
  transfers between devices with their start and end apart: 12, of which 4 were waited for; matrix products, arithmetic and copies ran while one was open for 0% of the time, Pallas kernels for 8%

profile of v5, /device:TPU:1, one launch (start us, length us, event | category | flops | bytes accessed | tf_op | source)
XLA Modules:
  0.0 89.9 jit_solution(4706654338123972844)
XLA Ops:
  0.6 1.5 %collective-permute-start.3 = (bf16[256,512]{1,0:T(8,128)(2,1)}, bf16[256,512]{1,0:T(8,128)(2,1)S(1)}, u32[]{:S(2)}, u32[]{:S(2)}) collective-permute-start(bf16[256,512]{1,0:T(8,128)(2,1)} %refs_1_.1), channel_id=1, source_target_pairs={{0,16},{1,17},{2,18},{3,19},{4,20},{5,21},{6,22},{7,23},{8,24},{9,... | collective-permute-start | bytes 786440 | tf_op jit(solution)/shard_map/ppermute | solution.py:410
  2.1 3.0 %collective-permute-start = (bf16[128,512]{1,0:T(8,128)(2,1)}, bf16[128,512]{1,0:T(8,128)(2,1)S(1)}, u32[]{:S(2)}, u32[]{:S(2)}) collective-permute-start(bf16[128,512]{1,0:T(8,128)(2,1)} %refs_0_.1), channel_id=1, source_target_pairs={{0,2},{1,3},{2,0},{3,1},{4,6},{5,7},{6,4},{7,5},{8,10},{9,11},{10,... | collective-permute-start | bytes 393224 | tf_op jit(solution)/shard_map/ppermute | solution.py:410
  5.1 0.4 collective-permute-start.1
  5.5 2.3 %collective-permute-start.2 = (bf16[128,512]{1,0:T(8,128)(2,1)}, bf16[128,512]{1,0:T(8,128)(2,1)S(1)}, u32[]{:S(2)}, u32[]{:S(2)}) collective-permute-start(bf16[128,512]{1,0:T(8,128)(2,1)} %refs_0_.1), channel_id=1, source_target_pairs={{0,3},{1,0},{2,1},{3,2},{4,7},{5,4},{6,5},{7,6},{8,11},{9,8},{10,9... | collective-permute-start | bytes 393224 | tf_op jit(solution)/shard_map/ppermute | solution.py:410
  7.8 3.8 %collective-permute-start.4 = (bf16[256,512]{1,0:T(8,128)(2,1)}, bf16[256,512]{1,0:T(8,128)(2,1)S(1)}, u32[]{:S(2)}, u32[]{:S(2)}) collective-permute-start(bf16[256,512]{1,0:T(8,128)(2,1)} %refs_1_.1), channel_id=1, source_target_pairs={{0,32},{1,33},{2,34},{3,35},{4,36},{5,37},{6,38},{7,39},{8,40},{9,... | collective-permute-start | bytes 786440 | tf_op jit(solution)/shard_map/ppermute | solution.py:410
  11.6 1.1 %bring.1 = (bf16[128,512]{1,0:T(8,128)(2,1)S(1)}, bf16[256,512]{1,0:T(8,128)(2,1)S(1)}, f32[16,128]{1,0:T(8,128)S(1)}) custom-call(bf16[128,512]{1,0:T(8,128)(2,1)} %refs_0_.1, bf16[256,512]{1,0:T(8,128)(2,1)} %refs_1_.1, f32[16,128]{1,0:T(8,128)} %bitcast.7), custom_call_target="tpu_custom_call" | custom-call | tf_op jit(solution)/shard_map/bring/pallas_call | solution.py:307
  12.7 0.0 collective-permute-done.3.other_ref
  12.7 0.2 collective-permute-start.5
  12.9 1.3 %collective-permute-start.9 = (bf16[512,512]{1,0:T(8,128)(2,1)S(1)}, bf16[512,512]{1,0:T(8,128)(2,1)S(1)}, u32[]{:S(2)}, u32[]{:S(2)}) collective-permute-start(bf16[512,512]{1,0:T(8,128)(2,1)S(1)} %constant_dynamic-update-slice_fusion.refs_1_.points_ref), channel_id=1, source_target_pairs={{0,4},{1,5},{2,6},{3,7},{4,8},{5,9},{6,10},{7,11},{8,12},{9,13},{1... | collective-permute-start | bytes 1572872 | tf_op jit(solution)/shard_map/ppermute | solution.py:410
  14.2 1.0 %collective-permute-done.4.side_ref = bf16[256,512]{1,0:T(8,128)(2,1)S(1)} collective-permute-done((bf16[256,512]{1,0:T(8,128)(2,1)}, bf16[256,512]{1,0:T(8,128)(2,1)S(1)}, u32[]{:S(2)}, u32[]{:S(2)}) %collective-permute-start.4) | collective-permute-done | bytes 262176 | tf_op jit(solution)/shard_map/ppermute | solution.py:410
  15.2 3.1 %collective-permute-start.6 = (bf16[256,512]{1,0:T(8,128)(2,1)S(1)}, bf16[256,512]{1,0:T(8,128)(2,1)S(1)}, u32[]{:S(2)}, u32[]{:S(2)}) collective-permute-start(bf16[256,512]{1,0:T(8,128)(2,1)S(1)} %after.1), channel_id=1, source_target_pairs={{0,32},{1,33},{2,34},{3,35},{4,36},{5,37},{6,38},{7,39},{8,40},{9,... | collective-permute-start | bytes 786440 | tf_op jit(solution)/shard_map/ppermute | solution.py:410
  18.3 0.0 collective-permute-done.5.side_other_ref
  18.4 1.7 %collective-permute-start.7 = (bf16[512,512]{1,0:T(8,128)(2,1)S(1)}, bf16[512,512]{1,0:T(8,128)(2,1)S(1)}, u32[]{:S(2)}, u32[]{:S(2)}) collective-permute-start(bf16[512,512]{1,0:T(8,128)(2,1)S(1)} %pad_maximum_fusion), channel_id=1, source_target_pairs={{0,16},{1,17},{2,18},{3,19},{4,20},{5,21},{6,22},{7,23},{8,24},{9,... | collective-permute-start | bytes 1572872 | tf_op jit(solution)/shard_map/ppermute | solution.py:410
  20.1 0.9 collective-permute-start.10
  21.0 0.6 collective-permute-done.6.far_ref
  21.6 3.2 %collective-permute-start.8 = (bf16[256,512]{1,0:T(8,128)(2,1)S(1)}, bf16[256,512]{1,0:T(8,128)(2,1)S(1)}, u32[]{:S(2)}, u32[]{:S(2)}) collective-permute-start(bf16[256,512]{1,0:T(8,128)(2,1)S(1)} %collective-permute-done.6.far_ref), channel_id=1, source_target_pairs={{0,16},{1,17},{2,18},{3,19},{4,20},{5,21},{6,22},{7,23},{8,24},{9,... | collective-permute-start | bytes 786440 | tf_op jit(solution)/shard_map/ppermute | solution.py:410
  24.9 0.0 collective-permute-done.9.refs_0_
  24.9 1.2 %collective-permute-done.8.theirs_far_ref = bf16[256,512]{1,0:T(8,128)(2,1)S(1)} collective-permute-done((bf16[256,512]{1,0:T(8,128)(2,1)S(1)}, bf16[256,512]{1,0:T(8,128)(2,1)S(1)}, u32[]{:S(2)}, u32[]{:S(2)}) %collective-permute-start.8) | collective-permute-done | bytes 262176 | tf_op jit(solution)/shard_map/ppermute | solution.py:410
  26.0 0.5 place.1
  26.6 1.9 %own_pass.1 = (f32[2048,2048]{1,0:T(8,128)S(1)}, f32[16,128]{1,0:T(8,128)S(1)}, f32[16,128]{1,0:T(8,128)S(1)}) custom-call(bf16[512,512]{1,0:T(8,128)(2,1)S(1)} %constant_dynamic-update-slice_fusion.refs_1_.points_ref, bf16[2048,512]{1,0:T(8,128)(2,1)S(1)} %get-tuple-element.28.tgt_ref, f32[16,128]{1,0:T(8,128)S(1)} %get-tuple-element.29.pot_ref), custom_call_target="tpu_custom_call" | custom-call | flops 1073741824 | bytes 8388608 | tf_op jit(solution)/shard_map/own_pass/pallas_call | solution.py:333
  28.5 1.9 %more_pass.3 = (f32[2048,2048]{1,0:T(8,128)S(1)}, f32[1,16,128]{2,1,0:T(8,128)S(1)}, f32[16,128]{1,0:T(8,128)S(1)}) custom-call(f32[2048,2048]{1,0:T(8,128)S(1)} %get-tuple-element.30.score_in_ref, f32[16,128]{1,0:T(8,128)S(1)} %get-tuple-element.31.rows_in_ref, f32[16,128]{1,0:T(8,128)S(1)} %get-tuple-element.32.src_sq_in_ref, ...), custom_call_target="tpu_custom_call", output_to_operand_aliasing={{0}: (0, {})} | custom-call | flops 1073741824 | bytes 8388608 | tf_op jit(solution)/shard_map/more_pass/pallas_call | solution.py:350
  30.4 1.9 %more_pass.4 = (f32[2048,2048]{1,0:T(8,128)S(1)}, f32[1,16,128]{2,1,0:T(8,128)S(1)}, f32[16,128]{1,0:T(8,128)S(1)}) custom-call(f32[2048,2048]{1,0:T(8,128)S(1)} %get-tuple-element.33.score_in_ref, f32[16,128]{1,0:T(8,128)S(1)} %bitcast.6, f32[16,128]{1,0:T(8,128)S(1)} %get-tuple-element.35.src_sq_in_ref, ...), custom_call_target="tpu_custom_call", output_to_operand_aliasing={{0}: (0, {})} | custom-call | flops 1073741824 | bytes 8388608 | tf_op jit(solution)/shard_map/more_pass/pallas_call | solution.py:350
  32.3 2.1 %collective-permute-done.11.refs_0_ = bf16[512,512]{1,0:T(8,128)(2,1)S(1)} collective-permute-done((bf16[512,512]{1,0:T(8,128)(2,1)S(1)}, bf16[512,512]{1,0:T(8,128)(2,1)S(1)}, u32[]{:S(2)}, u32[]{:S(2)}) %collective-permute-start.11) | collective-permute-done | bytes 524320 | tf_op jit(solution)/shard_map/ppermute | solution.py:410
  34.4 1.9 %more_pass.5 = (f32[2048,2048]{1,0:T(8,128)S(1)}, f32[16,16,128]{2,1,0:T(8,128)S(1)}, f32[16,128]{1,0:T(8,128)S(1)}) custom-call(f32[2048,2048]{1,0:T(8,128)S(1)} %get-tuple-element.36.score_in_ref, f32[16,128]{1,0:T(8,128)S(1)} %bitcast.5, f32[16,128]{1,0:T(8,128)S(1)} %get-tuple-element.38.src_sq_in_ref, ...), custom_call_target="tpu_custom_call", output_to_operand_aliasing={{0}: (0, {})} | custom-call | flops 1073741824 | bytes 8388608 | tf_op jit(solution)/shard_map/more_pass/pallas_call | solution.py:350
  36.3 11.2 %all_to_all.20.parts_ref = f32[16,16,128]{2,1,0:T(8,128)S(1)} all-to-all(f32[16,16,128]{2,1,0:T(8,128)S(1)} %get-tuple-element.40), channel_id=1, replica_groups=mesh['src'=8,'tgt'=16] {'tgt'}, dimensions={0} | all-to-all | bytes 262144 | tf_op jit(solution)/shard_map/all_to_all | solution.py:402
  47.5 4.2 %col_pass.2 = (f32[16,128]{1,0:T(8,128)}, f32[8,16,128]{2,1,0:T(8,128)S(1)}) custom-call(f32[2048,2048]{1,0:T(8,128)S(1)} %get-tuple-element.39.score_ref, f32[16,16,128]{2,1,0:T(8,128)S(1)} %all_to_all.20.parts_ref), custom_call_target="tpu_custom_call" | custom-call | tf_op jit(solution)/shard_map/col_pass/pallas_call | solution.py:379
  51.7 9.8 %all_to_all.21.parts_ref = f32[8,16,128]{2,1,0:T(8,128)S(1)} all-to-all(f32[8,16,128]{2,1,0:T(8,128)S(1)} %get-tuple-element.41), channel_id=1, replica_groups=mesh['src'=8,'tgt'=16] {'src'}, dimensions={0} | all-to-all | bytes 131072 | tf_op jit(solution)/shard_map/all_to_all | solution.py:402
  61.5 4.6 %row_pass.1 = f32[16,16,128]{2,1,0:T(8,128)S(1)} custom-call(f32[2048,2048]{1,0:T(8,128)S(1)} %get-tuple-element.39.score_ref, f32[8,16,128]{2,1,0:T(8,128)S(1)} %all_to_all.21.parts_ref), custom_call_target="tpu_custom_call" | custom-call | tf_op jit(solution)/shard_map/row_pass/pallas_call | solution.py:365
  66.1 9.7 %all_to_all.22.parts_ref = f32[16,16,128]{2,1,0:T(8,128)S(1)} all-to-all(f32[16,16,128]{2,1,0:T(8,128)S(1)} %row_pass.1), channel_id=1, replica_groups=mesh['src'=8,'tgt'=16] {'tgt'}, dimensions={0} | all-to-all | bytes 262144 | tf_op jit(solution)/shard_map/all_to_all | solution.py:402
  75.8 4.1 %col_pass.3 = (f32[16,128]{1,0:T(8,128)S(1)}, f32[8,16,128]{2,1,0:T(8,128)S(1)}) custom-call(f32[2048,2048]{1,0:T(8,128)S(1)} %get-tuple-element.39.score_ref, f32[16,16,128]{2,1,0:T(8,128)S(1)} %all_to_all.22.parts_ref), custom_call_target="tpu_custom_call" | custom-call | tf_op jit(solution)/shard_map/col_pass/pallas_call | solution.py:379
  79.9 9.4 %all_to_all.23.parts_ref = f32[8,16,128]{2,1,0:T(8,128)S(1)} all-to-all(f32[8,16,128]{2,1,0:T(8,128)S(1)} %get-tuple-element.42), channel_id=1, replica_groups=mesh['src'=8,'tgt'=16] {'src'}, dimensions={0} | all-to-all | bytes 131072 | tf_op jit(solution)/shard_map/all_to_all | solution.py:402
  89.2 0.6 last.1
  (13 shorter events, 0.1 us)
Async XLA Ops:
  0.6 12.1 %collective-permute-start.3 = (bf16[256,512]{1,0:T(8,128)(2,1)}, bf16[256,512]{1,0:T(8,128)(2,1)S(1)}, u32[]{:S(2)}, u32[]{:S(2)}) collective-permute-start(bf16[256,512]{1,0:T(8,128)(2,1)} %refs_1_.1), channel_id=1, source_target_pairs={{0,16},{1,17},{2,18},{3,19},{4,20},{5,21},{6,22},{7,23},{8,24},{9,... | collective-permute-start | bytes 786440 | tf_op jit(solution)/shard_map/ppermute | solution.py:410
  2.1 10.5 %collective-permute-start = (bf16[128,512]{1,0:T(8,128)(2,1)}, bf16[128,512]{1,0:T(8,128)(2,1)S(1)}, u32[]{:S(2)}, u32[]{:S(2)}) collective-permute-start(bf16[128,512]{1,0:T(8,128)(2,1)} %refs_0_.1), channel_id=1, source_target_pairs={{0,2},{1,3},{2,0},{3,1},{4,6},{5,7},{6,4},{7,5},{8,10},{9,11},{10,... | collective-permute-start | bytes 393224 | tf_op jit(solution)/shard_map/ppermute | solution.py:410
  5.1 7.8 %collective-permute-start.1 = (bf16[128,512]{1,0:T(8,128)(2,1)}, bf16[128,512]{1,0:T(8,128)(2,1)S(1)}, u32[]{:S(2)}, u32[]{:S(2)}) collective-permute-start(bf16[128,512]{1,0:T(8,128)(2,1)} %refs_0_.1), channel_id=1, source_target_pairs={{0,1},{1,2},{2,3},{3,0},{4,5},{5,6},{6,7},{7,4},{8,9},{9,10},{10,1... | collective-permute-start | bytes 393224 | tf_op jit(solution)/shard_map/ppermute | solution.py:410
  5.5 7.4 %collective-permute-start.2 = (bf16[128,512]{1,0:T(8,128)(2,1)}, bf16[128,512]{1,0:T(8,128)(2,1)S(1)}, u32[]{:S(2)}, u32[]{:S(2)}) collective-permute-start(bf16[128,512]{1,0:T(8,128)(2,1)} %refs_0_.1), channel_id=1, source_target_pairs={{0,3},{1,0},{2,1},{3,2},{4,7},{5,4},{6,5},{7,6},{8,11},{9,8},{10,9... | collective-permute-start | bytes 393224 | tf_op jit(solution)/shard_map/ppermute | solution.py:410
  7.8 7.4 %collective-permute-start.4 = (bf16[256,512]{1,0:T(8,128)(2,1)}, bf16[256,512]{1,0:T(8,128)(2,1)S(1)}, u32[]{:S(2)}, u32[]{:S(2)}) collective-permute-start(bf16[256,512]{1,0:T(8,128)(2,1)} %refs_1_.1), channel_id=1, source_target_pairs={{0,32},{1,33},{2,34},{3,35},{4,36},{5,37},{6,38},{7,39},{8,40},{9,... | collective-permute-start | bytes 786440 | tf_op jit(solution)/shard_map/ppermute | solution.py:410
  12.7 5.6 %collective-permute-start.5 = (bf16[256,512]{1,0:T(8,128)(2,1)S(1)}, bf16[256,512]{1,0:T(8,128)(2,1)S(1)}, u32[]{:S(2)}, u32[]{:S(2)}) collective-permute-start(bf16[256,512]{1,0:T(8,128)(2,1)S(1)} %collective-permute-done.3.other_ref), channel_id=1, source_target_pairs={{0,32},{1,33},{2,34},{3,35},{4,36},{5,37},{6,38},{7,39},{8,40},{9,... | collective-permute-start | bytes 786440 | tf_op jit(solution)/shard_map/ppermute | solution.py:410
  12.9 11.9 %collective-permute-start.9 = (bf16[512,512]{1,0:T(8,128)(2,1)S(1)}, bf16[512,512]{1,0:T(8,128)(2,1)S(1)}, u32[]{:S(2)}, u32[]{:S(2)}) collective-permute-start(bf16[512,512]{1,0:T(8,128)(2,1)S(1)} %constant_dynamic-update-slice_fusion.refs_1_.points_ref), channel_id=1, source_target_pairs={{0,4},{1,5},{2,6},{3,7},{4,8},{5,9},{6,10},{7,11},{8,12},{9,13},{1... | collective-permute-start | bytes 1572872 | tf_op jit(solution)/shard_map/ppermute | solution.py:410
  15.2 6.4 %collective-permute-start.6 = (bf16[256,512]{1,0:T(8,128)(2,1)S(1)}, bf16[256,512]{1,0:T(8,128)(2,1)S(1)}, u32[]{:S(2)}, u32[]{:S(2)}) collective-permute-start(bf16[256,512]{1,0:T(8,128)(2,1)S(1)} %after.1), channel_id=1, source_target_pairs={{0,32},{1,33},{2,34},{3,35},{4,36},{5,37},{6,38},{7,39},{8,40},{9,... | collective-permute-start | bytes 786440 | tf_op jit(solution)/shard_map/ppermute | solution.py:410
  18.4 7.7 %collective-permute-start.7 = (bf16[512,512]{1,0:T(8,128)(2,1)S(1)}, bf16[512,512]{1,0:T(8,128)(2,1)S(1)}, u32[]{:S(2)}, u32[]{:S(2)}) collective-permute-start(bf16[512,512]{1,0:T(8,128)(2,1)S(1)} %pad_maximum_fusion), channel_id=1, source_target_pairs={{0,16},{1,17},{2,18},{3,19},{4,20},{5,21},{6,22},{7,23},{8,24},{9,... | collective-permute-start | bytes 1572872 | tf_op jit(solution)/shard_map/ppermute | solution.py:410
  20.1 10.3 %collective-permute-start.10 = (bf16[512,512]{1,0:T(8,128)(2,1)S(1)}, bf16[512,512]{1,0:T(8,128)(2,1)S(1)}, u32[]{:S(2)}, u32[]{:S(2)}) collective-permute-start(bf16[512,512]{1,0:T(8,128)(2,1)S(1)} %constant_dynamic-update-slice_fusion.refs_1_.points_ref), channel_id=1, source_target_pairs={{0,12},{1,13},{2,14},{3,15},{4,0},{5,1},{6,2},{7,3},{8,4},{9,5},{1... | collective-permute-start | bytes 1572872 | tf_op jit(solution)/shard_map/ppermute | solution.py:410
  21.6 4.4 %collective-permute-start.8 = (bf16[256,512]{1,0:T(8,128)(2,1)S(1)}, bf16[256,512]{1,0:T(8,128)(2,1)S(1)}, u32[]{:S(2)}, u32[]{:S(2)}) collective-permute-start(bf16[256,512]{1,0:T(8,128)(2,1)S(1)} %collective-permute-done.6.far_ref), channel_id=1, source_target_pairs={{0,16},{1,17},{2,18},{3,19},{4,20},{5,21},{6,22},{7,23},{8,24},{9,... | collective-permute-start | bytes 786440 | tf_op jit(solution)/shard_map/ppermute | solution.py:410
  24.9 9.5 %collective-permute-start.11 = (bf16[512,512]{1,0:T(8,128)(2,1)S(1)}, bf16[512,512]{1,0:T(8,128)(2,1)S(1)}, u32[]{:S(2)}, u32[]{:S(2)}) collective-permute-start(bf16[512,512]{1,0:T(8,128)(2,1)S(1)} %collective-permute-done.9.refs_0_), channel_id=1, source_target_pairs={{0,4},{1,5},{2,6},{3,7},{4,8},{5,9},{6,10},{7,11},{8,12},{9,13},{1... | collective-permute-start | bytes 1572872 | tf_op jit(solution)/shard_map/ppermute | solution.py:410

commit v6 on v5

--- a/solution.py
+++ b/solution.py
@@ -86,11 +86,11 @@
     own = lax.axis_index("src")
     core = own % 2
     size = own_ref.shape[0]
-    chips = targets.shape[0] // (2 * size)
+    chips = targets.shape[1] // (2 * size)
 
     def put(points, chip, core):
         index = (own // 2 + chip + chips) % chips * 2 + core
-        targets[pl.ds(pl.multiple_of(index * size, size), size), :] = points
+        targets[:, pl.ds(pl.multiple_of(index * size, size), size)] = points.T
         per = size // LANES
         for sub in range(per):
             row = squares(points[sub * LANES : (sub + 1) * LANES])
@@ -134,7 +134,7 @@
 
 def block_pipeline(sources, tgt_ref, pot_ref, score_ref, rows_ref, sq_ref, peaks, totals):
     per = STEP // LANES
-    chunks = tgt_ref.shape[0] // CHUNK
+    chunks = tgt_ref.shape[1] // CHUNK
     pots = pot_rows(pot_ref)
 
     def product(at, chunk):
@@ -142,7 +142,7 @@
         points = ref[first : first + STEP, :]
         lanes = slice(chunk * CHUNK, (chunk + 1) * CHUNK)
         score_ref[block * LANES : (block + per) * LANES, lanes] = lax.dot_general(
-            points, tgt_ref[lanes, :], (((1,), (1,)), ((), ())), preferred_element_type=jnp.float32
+            points, tgt_ref[:, lanes], (((1,), (0,)), ((), ())), preferred_element_type=jnp.float32
         ) * (2.0 / UNIT)
         if chunk < per:
             row = squares(points[chunk * LANES : (chunk + 1) * LANES])
@@ -294,7 +294,7 @@
     rows, width = 8 * own.shape[0], own.shape[1]
     return pl.pallas_call(
         place_kernel,
-        out_shape=(pltpu.VMEM((rows, width), own.dtype), vec(rows), vec(rows)),
+        out_shape=(pltpu.VMEM((width, rows), own.dtype), vec(rows), vec(rows)),
         in_specs=[IN_VMEM] * 8,
         out_specs=(IN_VMEM,) * 3,
         cost_estimate=cost(rows, width, 1),
@@ -329,7 +329,7 @@
 
 
 def own_pass(points, targets, pot, rows):
-    cols, width = targets.shape
+    width, cols = targets.shape
     return pl.pallas_call(
         own_kernel,
         out_shape=(pltpu.VMEM((rows, cols), jnp.float32), vec(rows), vec(rows)),
@@ -344,7 +344,7 @@
 
 def more_pass(state, points, blocks, targets, pot, copies):
     score, row_parts, src_sq = state
-    (rows, cols), width = score.shape, targets.shape[1]
+    (rows, cols), width = score.shape, targets.shape[0]
     added = sum(array.shape[0] for array in points)
     score = pltpu.with_memory_space_constraint(score, pltpu.VMEM)
     return pl.pallas_call(

time: 90.2 us -> 90 us (level)
  transfers between devices with their start and end apart: 12 -> 12, of which waited for: 4 -> 4; matrix products, arithmetic and copies ran while one was open for 0% -> 0% of each run, Pallas kernels for 8% -> 9%
where the time goes in v6:
time: 90 us; the launch traced here: 89.7 us
  blocking collectives  39.8 us (44%)
  Pallas kernels  23.4 us (26%)
  starting transfers between devices  21.3 us (24%)
  waiting for transfers between devices  4.33 us (5%)
    all_to_all x4, blocking collectives, exchange(): return lax.all_to_all(part, axis, 0, 0, tiled=True)  39.8 us
    ppermute x12, starting transfers between devices, move(): return lax.ppermute(block, ('src', 'tgt'), pairs)  21.3 us
    pallas_call x2, Pallas kernels, col_pass_call(): pl.pallas_call(functools.partial(col_kernel, count), out_shape=(pltpu.VME...  8.35 us
    pallas_call x3, Pallas kernels, more_pass(): pl.pallas_call(functools.partial(more_kernel, blocks), out_shape=(pltpu.V...  5.81 us
    pallas_call x1, Pallas kernels, row_pass_call(): pl.pallas_call(functools.partial(row_kernel, count), out_shape=vecs(copie...  4.57 us
    ppermute x12, waiting for transfers between devices, move(): return lax.ppermute(block, ('src', 'tgt'), pairs)  4.33 us
    pallas_call x1, Pallas kernels, own_pass(): pl.pallas_call(own_kernel, out_shape=(pltpu.VMEM((rows, cols), jnp.float3...  1.91 us
  transfers between devices with their start and end apart: 12, of which 4 were waited for; matrix products, arithmetic and copies ran while one was open for 0% of the time, Pallas kernels for 9%

profile of v6, /device:TPU:1, one launch (start us, length us, event | category | flops | bytes accessed | tf_op | source)
XLA Modules:
  0.0 89.7 jit_solution(3568457451256904491)
XLA Ops:
  0.6 1.5 %collective-permute-start.3 = (bf16[256,512]{1,0:T(8,128)(2,1)}, bf16[256,512]{1,0:T(8,128)(2,1)S(1)}, u32[]{:S(2)}, u32[]{:S(2)}) collective-permute-start(bf16[256,512]{1,0:T(8,128)(2,1)} %refs_1_.1), channel_id=1, source_target_pairs={{0,16},{1,17},{2,18},{3,19},{4,20},{5,21},{6,22},{7,23},{8,24},{9,... | collective-permute-start | bytes 786440 | tf_op jit(solution)/shard_map/ppermute | solution.py:410
  2.1 3.0 %collective-permute-start = (bf16[128,512]{1,0:T(8,128)(2,1)}, bf16[128,512]{1,0:T(8,128)(2,1)S(1)}, u32[]{:S(2)}, u32[]{:S(2)}) collective-permute-start(bf16[128,512]{1,0:T(8,128)(2,1)} %refs_0_.1), channel_id=1, source_target_pairs={{0,2},{1,3},{2,0},{3,1},{4,6},{5,7},{6,4},{7,5},{8,10},{9,11},{10,... | collective-permute-start | bytes 393224 | tf_op jit(solution)/shard_map/ppermute | solution.py:410
  5.1 0.4 collective-permute-start.1
  5.5 2.3 %collective-permute-start.2 = (bf16[128,512]{1,0:T(8,128)(2,1)}, bf16[128,512]{1,0:T(8,128)(2,1)S(1)}, u32[]{:S(2)}, u32[]{:S(2)}) collective-permute-start(bf16[128,512]{1,0:T(8,128)(2,1)} %refs_0_.1), channel_id=1, source_target_pairs={{0,3},{1,0},{2,1},{3,2},{4,7},{5,4},{6,5},{7,6},{8,11},{9,8},{10,9... | collective-permute-start | bytes 393224 | tf_op jit(solution)/shard_map/ppermute | solution.py:410
  7.8 3.8 %collective-permute-start.4 = (bf16[256,512]{1,0:T(8,128)(2,1)}, bf16[256,512]{1,0:T(8,128)(2,1)S(1)}, u32[]{:S(2)}, u32[]{:S(2)}) collective-permute-start(bf16[256,512]{1,0:T(8,128)(2,1)} %refs_1_.1), channel_id=1, source_target_pairs={{0,32},{1,33},{2,34},{3,35},{4,36},{5,37},{6,38},{7,39},{8,40},{9,... | collective-permute-start | bytes 786440 | tf_op jit(solution)/shard_map/ppermute | solution.py:410
  11.6 1.1 %bring.1 = (bf16[128,512]{1,0:T(8,128)(2,1)S(1)}, bf16[256,512]{1,0:T(8,128)(2,1)S(1)}, f32[16,128]{1,0:T(8,128)S(1)}) custom-call(bf16[128,512]{1,0:T(8,128)(2,1)} %refs_0_.1, bf16[256,512]{1,0:T(8,128)(2,1)} %refs_1_.1, f32[16,128]{1,0:T(8,128)} %bitcast.7), custom_call_target="tpu_custom_call" | custom-call | tf_op jit(solution)/shard_map/bring/pallas_call | solution.py:307
  12.7 0.0 collective-permute-done.3.other_ref
  12.7 0.2 collective-permute-start.5
  12.9 1.3 %collective-permute-start.9 = (bf16[512,512]{1,0:T(8,128)(2,1)S(1)}, bf16[512,512]{1,0:T(8,128)(2,1)S(1)}, u32[]{:S(2)}, u32[]{:S(2)}) collective-permute-start(bf16[512,512]{1,0:T(8,128)(2,1)S(1)} %constant_dynamic-update-slice_fusion.refs_1_.points_ref), channel_id=1, source_target_pairs={{0,4},{1,5},{2,6},{3,7},{4,8},{5,9},{6,10},{7,11},{8,12},{9,13},{1... | collective-permute-start | bytes 1572872 | tf_op jit(solution)/shard_map/ppermute | solution.py:410
  14.2 1.0 %collective-permute-done.4.side_ref = bf16[256,512]{1,0:T(8,128)(2,1)S(1)} collective-permute-done((bf16[256,512]{1,0:T(8,128)(2,1)}, bf16[256,512]{1,0:T(8,128)(2,1)S(1)}, u32[]{:S(2)}, u32[]{:S(2)}) %collective-permute-start.4) | collective-permute-done | bytes 262176 | tf_op jit(solution)/shard_map/ppermute | solution.py:410
  15.2 3.1 %collective-permute-start.6 = (bf16[256,512]{1,0:T(8,128)(2,1)S(1)}, bf16[256,512]{1,0:T(8,128)(2,1)S(1)}, u32[]{:S(2)}, u32[]{:S(2)}) collective-permute-start(bf16[256,512]{1,0:T(8,128)(2,1)S(1)} %after.1), channel_id=1, source_target_pairs={{0,32},{1,33},{2,34},{3,35},{4,36},{5,37},{6,38},{7,39},{8,40},{9,... | collective-permute-start | bytes 786440 | tf_op jit(solution)/shard_map/ppermute | solution.py:410
  18.3 0.0 collective-permute-done.5.side_other_ref
  18.4 1.7 %collective-permute-start.7 = (bf16[512,512]{1,0:T(8,128)(2,1)S(1)}, bf16[512,512]{1,0:T(8,128)(2,1)S(1)}, u32[]{:S(2)}, u32[]{:S(2)}) collective-permute-start(bf16[512,512]{1,0:T(8,128)(2,1)S(1)} %pad_maximum_fusion), channel_id=1, source_target_pairs={{0,16},{1,17},{2,18},{3,19},{4,20},{5,21},{6,22},{7,23},{8,24},{9,... | collective-permute-start | bytes 1572872 | tf_op jit(solution)/shard_map/ppermute | solution.py:410
  20.1 0.9 %collective-permute-start.10 = (bf16[512,512]{1,0:T(8,128)(2,1)S(1)}, bf16[512,512]{1,0:T(8,128)(2,1)S(1)}, u32[]{:S(2)}, u32[]{:S(2)}) collective-permute-start(bf16[512,512]{1,0:T(8,128)(2,1)S(1)} %constant_dynamic-update-slice_fusion.refs_1_.points_ref), channel_id=1, source_target_pairs={{0,12},{1,13},{2,14},{3,15},{4,0},{5,1},{6,2},{7,3},{8,4},{9,5},{1... | collective-permute-start | bytes 1572872 | tf_op jit(solution)/shard_map/ppermute | solution.py:410
  21.0 0.6 collective-permute-done.6.far_ref
  21.6 3.2 %collective-permute-start.8 = (bf16[256,512]{1,0:T(8,128)(2,1)S(1)}, bf16[256,512]{1,0:T(8,128)(2,1)S(1)}, u32[]{:S(2)}, u32[]{:S(2)}) collective-permute-start(bf16[256,512]{1,0:T(8,128)(2,1)S(1)} %collective-permute-done.6.far_ref), channel_id=1, source_target_pairs={{0,16},{1,17},{2,18},{3,19},{4,20},{5,21},{6,22},{7,23},{8,24},{9,... | collective-permute-start | bytes 786440 | tf_op jit(solution)/shard_map/ppermute | solution.py:410
  24.9 0.0 collective-permute-start.11
  24.9 1.2 %collective-permute-done.8.theirs_far_ref = bf16[256,512]{1,0:T(8,128)(2,1)S(1)} collective-permute-done((bf16[256,512]{1,0:T(8,128)(2,1)S(1)}, bf16[256,512]{1,0:T(8,128)(2,1)S(1)}, u32[]{:S(2)}, u32[]{:S(2)}) %collective-permute-start.8) | collective-permute-done | bytes 262176 | tf_op jit(solution)/shard_map/ppermute | solution.py:410
  26.0 1.1 %place.1 = (bf16[512,2048]{1,0:T(8,128)(2,1)S(1)}, f32[16,128]{1,0:T(8,128)S(1)}, f32[16,128]{1,0:T(8,128)S(1)}) custom-call(bf16[256,512]{1,0:T(8,128)(2,1)S(1)} %get-tuple-element.26.own_ref, bf16[256,512]{1,0:T(8,128)(2,1)S(1)} %collective-permute-done.3.other_ref, bf16[256,512]{1,0:T(8,128)(2,1)S(1)} %collective-permute-done.4.side_ref, ...), custom_call_target="tpu_custom_call" | custom-call | flops 2097152 | bytes 8388608 | tf_op jit(solution)/shard_map/place/pallas_call | solution.py:295
  27.1 1.9 %own_pass.1 = (f32[2048,2048]{1,0:T(8,128)S(1)}, f32[16,128]{1,0:T(8,128)S(1)}, f32[16,128]{1,0:T(8,128)S(1)}) custom-call(bf16[512,512]{1,0:T(8,128)(2,1)S(1)} %constant_dynamic-update-slice_fusion.refs_1_.points_ref, bf16[512,2048]{1,0:T(8,128)(2,1)S(1)} %get-tuple-element.28.tgt_ref, f32[16,128]{1,0:T(8,128)S(1)} %get-tuple-element.29.pot_ref), custom_call_target="tpu_custom_call" | custom-call | flops 1073741824 | bytes 8388608 | tf_op jit(solution)/shard_map/own_pass/pallas_call | solution.py:333
  29.0 1.9 %more_pass.3 = (f32[2048,2048]{1,0:T(8,128)S(1)}, f32[1,16,128]{2,1,0:T(8,128)S(1)}, f32[16,128]{1,0:T(8,128)S(1)}) custom-call(f32[2048,2048]{1,0:T(8,128)S(1)} %get-tuple-element.30.score_in_ref, f32[16,128]{1,0:T(8,128)S(1)} %get-tuple-element.31.rows_in_ref, f32[16,128]{1,0:T(8,128)S(1)} %get-tuple-element.32.src_sq_in_ref, ...), custom_call_target="tpu_custom_call", output_to_operand_aliasing={{0}: (0, {})} | custom-call | flops 1073741824 | bytes 8388608 | tf_op jit(solution)/shard_map/more_pass/pallas_call | solution.py:350
  30.9 1.9 %more_pass.4 = (f32[2048,2048]{1,0:T(8,128)S(1)}, f32[1,16,128]{2,1,0:T(8,128)S(1)}, f32[16,128]{1,0:T(8,128)S(1)}) custom-call(f32[2048,2048]{1,0:T(8,128)S(1)} %get-tuple-element.33.score_in_ref, f32[16,128]{1,0:T(8,128)S(1)} %bitcast.6, f32[16,128]{1,0:T(8,128)S(1)} %get-tuple-element.35.src_sq_in_ref, ...), custom_call_target="tpu_custom_call", output_to_operand_aliasing={{0}: (0, {})} | custom-call | flops 1073741824 | bytes 8388608 | tf_op jit(solution)/shard_map/more_pass/pallas_call | solution.py:350
  32.9 1.5 %collective-permute-done.11.refs_0_ = bf16[512,512]{1,0:T(8,128)(2,1)S(1)} collective-permute-done((bf16[512,512]{1,0:T(8,128)(2,1)S(1)}, bf16[512,512]{1,0:T(8,128)(2,1)S(1)}, u32[]{:S(2)}, u32[]{:S(2)}) %collective-permute-start.11) | collective-permute-done | bytes 524320 | tf_op jit(solution)/shard_map/ppermute | solution.py:410
  34.4 1.9 %more_pass.5 = (f32[2048,2048]{1,0:T(8,128)S(1)}, f32[16,16,128]{2,1,0:T(8,128)S(1)}, f32[16,128]{1,0:T(8,128)S(1)}) custom-call(f32[2048,2048]{1,0:T(8,128)S(1)} %get-tuple-element.36.score_in_ref, f32[16,128]{1,0:T(8,128)S(1)} %bitcast.5, f32[16,128]{1,0:T(8,128)S(1)} %get-tuple-element.38.src_sq_in_ref, ...), custom_call_target="tpu_custom_call", output_to_operand_aliasing={{0}: (0, {})} | custom-call | flops 1073741824 | bytes 8388608 | tf_op jit(solution)/shard_map/more_pass/pallas_call | solution.py:350
  36.3 11.0 %all_to_all.20.parts_ref = f32[16,16,128]{2,1,0:T(8,128)S(1)} all-to-all(f32[16,16,128]{2,1,0:T(8,128)S(1)} %get-tuple-element.40), channel_id=1, replica_groups=mesh['src'=8,'tgt'=16] {'tgt'}, dimensions={0} | all-to-all | bytes 262144 | tf_op jit(solution)/shard_map/all_to_all | solution.py:402
  47.4 4.2 %col_pass.2 = (f32[16,128]{1,0:T(8,128)}, f32[8,16,128]{2,1,0:T(8,128)S(1)}) custom-call(f32[2048,2048]{1,0:T(8,128)S(1)} %get-tuple-element.39.score_ref, f32[16,16,128]{2,1,0:T(8,128)S(1)} %all_to_all.20.parts_ref), custom_call_target="tpu_custom_call" | custom-call | tf_op jit(solution)/shard_map/col_pass/pallas_call | solution.py:379
  51.6 9.7 %all_to_all.21.parts_ref = f32[8,16,128]{2,1,0:T(8,128)S(1)} all-to-all(f32[8,16,128]{2,1,0:T(8,128)S(1)} %get-tuple-element.41), channel_id=1, replica_groups=mesh['src'=8,'tgt'=16] {'src'}, dimensions={0} | all-to-all | bytes 131072 | tf_op jit(solution)/shard_map/all_to_all | solution.py:402
  61.3 4.6 %row_pass.1 = f32[16,16,128]{2,1,0:T(8,128)S(1)} custom-call(f32[2048,2048]{1,0:T(8,128)S(1)} %get-tuple-element.39.score_ref, f32[8,16,128]{2,1,0:T(8,128)S(1)} %all_to_all.21.parts_ref), custom_call_target="tpu_custom_call" | custom-call | tf_op jit(solution)/shard_map/row_pass/pallas_call | solution.py:365
  65.9 9.7 %all_to_all.22.parts_ref = f32[16,16,128]{2,1,0:T(8,128)S(1)} all-to-all(f32[16,16,128]{2,1,0:T(8,128)S(1)} %row_pass.1), channel_id=1, replica_groups=mesh['src'=8,'tgt'=16] {'tgt'}, dimensions={0} | all-to-all | bytes 262144 | tf_op jit(solution)/shard_map/all_to_all | solution.py:402
  75.6 4.1 %col_pass.3 = (f32[16,128]{1,0:T(8,128)S(1)}, f32[8,16,128]{2,1,0:T(8,128)S(1)}) custom-call(f32[2048,2048]{1,0:T(8,128)S(1)} %get-tuple-element.39.score_ref, f32[16,16,128]{2,1,0:T(8,128)S(1)} %all_to_all.22.parts_ref), custom_call_target="tpu_custom_call" | custom-call | tf_op jit(solution)/shard_map/col_pass/pallas_call | solution.py:379
  79.7 9.4 %all_to_all.23.parts_ref = f32[8,16,128]{2,1,0:T(8,128)S(1)} all-to-all(f32[8,16,128]{2,1,0:T(8,128)S(1)} %get-tuple-element.42), channel_id=1, replica_groups=mesh['src'=8,'tgt'=16] {'src'}, dimensions={0} | all-to-all | bytes 131072 | tf_op jit(solution)/shard_map/all_to_all | solution.py:402
  89.1 0.6 last.1
  (13 shorter events, 0.1 us)
Async XLA Ops:
  0.6 12.1 %collective-permute-start.3 = (bf16[256,512]{1,0:T(8,128)(2,1)}, bf16[256,512]{1,0:T(8,128)(2,1)S(1)}, u32[]{:S(2)}, u32[]{:S(2)}) collective-permute-start(bf16[256,512]{1,0:T(8,128)(2,1)} %refs_1_.1), channel_id=1, source_target_pairs={{0,16},{1,17},{2,18},{3,19},{4,20},{5,21},{6,22},{7,23},{8,24},{9,... | collective-permute-start | bytes 786440 | tf_op jit(solution)/shard_map/ppermute | solution.py:410
  2.1 10.5 %collective-permute-start = (bf16[128,512]{1,0:T(8,128)(2,1)}, bf16[128,512]{1,0:T(8,128)(2,1)S(1)}, u32[]{:S(2)}, u32[]{:S(2)}) collective-permute-start(bf16[128,512]{1,0:T(8,128)(2,1)} %refs_0_.1), channel_id=1, source_target_pairs={{0,2},{1,3},{2,0},{3,1},{4,6},{5,7},{6,4},{7,5},{8,10},{9,11},{10,... | collective-permute-start | bytes 393224 | tf_op jit(solution)/shard_map/ppermute | solution.py:410
  5.1 7.8 %collective-permute-start.1 = (bf16[128,512]{1,0:T(8,128)(2,1)}, bf16[128,512]{1,0:T(8,128)(2,1)S(1)}, u32[]{:S(2)}, u32[]{:S(2)}) collective-permute-start(bf16[128,512]{1,0:T(8,128)(2,1)} %refs_0_.1), channel_id=1, source_target_pairs={{0,1},{1,2},{2,3},{3,0},{4,5},{5,6},{6,7},{7,4},{8,9},{9,10},{10,1... | collective-permute-start | bytes 393224 | tf_op jit(solution)/shard_map/ppermute | solution.py:410
  5.5 7.4 %collective-permute-start.2 = (bf16[128,512]{1,0:T(8,128)(2,1)}, bf16[128,512]{1,0:T(8,128)(2,1)S(1)}, u32[]{:S(2)}, u32[]{:S(2)}) collective-permute-start(bf16[128,512]{1,0:T(8,128)(2,1)} %refs_0_.1), channel_id=1, source_target_pairs={{0,3},{1,0},{2,1},{3,2},{4,7},{5,4},{6,5},{7,6},{8,11},{9,8},{10,9... | collective-permute-start | bytes 393224 | tf_op jit(solution)/shard_map/ppermute | solution.py:410
  7.8 7.4 %collective-permute-start.4 = (bf16[256,512]{1,0:T(8,128)(2,1)}, bf16[256,512]{1,0:T(8,128)(2,1)S(1)}, u32[]{:S(2)}, u32[]{:S(2)}) collective-permute-start(bf16[256,512]{1,0:T(8,128)(2,1)} %refs_1_.1), channel_id=1, source_target_pairs={{0,32},{1,33},{2,34},{3,35},{4,36},{5,37},{6,38},{7,39},{8,40},{9,... | collective-permute-start | bytes 786440 | tf_op jit(solution)/shard_map/ppermute | solution.py:410
  12.7 5.6 %collective-permute-start.5 = (bf16[256,512]{1,0:T(8,128)(2,1)S(1)}, bf16[256,512]{1,0:T(8,128)(2,1)S(1)}, u32[]{:S(2)}, u32[]{:S(2)}) collective-permute-start(bf16[256,512]{1,0:T(8,128)(2,1)S(1)} %collective-permute-done.3.other_ref), channel_id=1, source_target_pairs={{0,32},{1,33},{2,34},{3,35},{4,36},{5,37},{6,38},{7,39},{8,40},{9,... | collective-permute-start | bytes 786440 | tf_op jit(solution)/shard_map/ppermute | solution.py:410
  12.9 11.9 %collective-permute-start.9 = (bf16[512,512]{1,0:T(8,128)(2,1)S(1)}, bf16[512,512]{1,0:T(8,128)(2,1)S(1)}, u32[]{:S(2)}, u32[]{:S(2)}) collective-permute-start(bf16[512,512]{1,0:T(8,128)(2,1)S(1)} %constant_dynamic-update-slice_fusion.refs_1_.points_ref), channel_id=1, source_target_pairs={{0,4},{1,5},{2,6},{3,7},{4,8},{5,9},{6,10},{7,11},{8,12},{9,13},{1... | collective-permute-start | bytes 1572872 | tf_op jit(solution)/shard_map/ppermute | solution.py:410
  15.2 6.4 %collective-permute-start.6 = (bf16[256,512]{1,0:T(8,128)(2,1)S(1)}, bf16[256,512]{1,0:T(8,128)(2,1)S(1)}, u32[]{:S(2)}, u32[]{:S(2)}) collective-permute-start(bf16[256,512]{1,0:T(8,128)(2,1)S(1)} %after.1), channel_id=1, source_target_pairs={{0,32},{1,33},{2,34},{3,35},{4,36},{5,37},{6,38},{7,39},{8,40},{9,... | collective-permute-start | bytes 786440 | tf_op jit(solution)/shard_map/ppermute | solution.py:410
  18.4 7.7 %collective-permute-start.7 = (bf16[512,512]{1,0:T(8,128)(2,1)S(1)}, bf16[512,512]{1,0:T(8,128)(2,1)S(1)}, u32[]{:S(2)}, u32[]{:S(2)}) collective-permute-start(bf16[512,512]{1,0:T(8,128)(2,1)S(1)} %pad_maximum_fusion), channel_id=1, source_target_pairs={{0,16},{1,17},{2,18},{3,19},{4,20},{5,21},{6,22},{7,23},{8,24},{9,... | collective-permute-start | bytes 1572872 | tf_op jit(solution)/shard_map/ppermute | solution.py:410
  20.1 10.8 %collective-permute-start.10 = (bf16[512,512]{1,0:T(8,128)(2,1)S(1)}, bf16[512,512]{1,0:T(8,128)(2,1)S(1)}, u32[]{:S(2)}, u32[]{:S(2)}) collective-permute-start(bf16[512,512]{1,0:T(8,128)(2,1)S(1)} %constant_dynamic-update-slice_fusion.refs_1_.points_ref), channel_id=1, source_target_pairs={{0,12},{1,13},{2,14},{3,15},{4,0},{5,1},{6,2},{7,3},{8,4},{9,5},{1... | collective-permute-start | bytes 1572872 | tf_op jit(solution)/shard_map/ppermute | solution.py:410
  21.6 4.4 %collective-permute-start.8 = (bf16[256,512]{1,0:T(8,128)(2,1)S(1)}, bf16[256,512]{1,0:T(8,128)(2,1)S(1)}, u32[]{:S(2)}, u32[]{:S(2)}) collective-permute-start(bf16[256,512]{1,0:T(8,128)(2,1)S(1)} %collective-permute-done.6.far_ref), channel_id=1, source_target_pairs={{0,16},{1,17},{2,18},{3,19},{4,20},{5,21},{6,22},{7,23},{8,24},{9,... | collective-permute-start | bytes 786440 | tf_op jit(solution)/shard_map/ppermute | solution.py:410
  24.9 9.5 %collective-permute-start.11 = (bf16[512,512]{1,0:T(8,128)(2,1)S(1)}, bf16[512,512]{1,0:T(8,128)(2,1)S(1)}, u32[]{:S(2)}, u32[]{:S(2)}) collective-permute-start(bf16[512,512]{1,0:T(8,128)(2,1)S(1)} %collective-permute-done.9.refs_0_), channel_id=1, source_target_pairs={{0,4},{1,5},{2,6},{3,7},{4,8},{5,9},{6,10},{7,11},{8,12},{9,13},{1... | collective-permute-start | bytes 1572872 | tf_op jit(solution)/shard_map/ppermute | solution.py:410

commit v7 on v5

--- a/solution.py
+++ b/solution.py
@@ -119,7 +119,7 @@
         copy.wait()
 
 
-CHUNK = 256
+CHUNK = 1024
 
 
 def row_index(block):

time: 90.2 us -> 90 us (level)
  no operation moved by 1% of the time
where the time goes in v7:
time: 90 us; the launch traced here: 89.8 us
  blocking collectives  39.8 us (44%)
  Pallas kernels  23 us (26%)
  starting transfers between devices  21.3 us (24%)
  waiting for transfers between devices  4.73 us (5%)
    all_to_all x4, blocking collectives, exchange(): return lax.all_to_all(part, axis, 0, 0, tiled=True)  39.8 us
    ppermute x12, starting transfers between devices, move(): return lax.ppermute(block, ('src', 'tgt'), pairs)  21.3 us
    pallas_call x2, Pallas kernels, col_pass_call(): pl.pallas_call(functools.partial(col_kernel, count), out_shape=(pltpu.VME...  8.35 us
    pallas_call x3, Pallas kernels, more_pass(): pl.pallas_call(functools.partial(more_kernel, blocks), out_shape=(pltpu.V...  5.91 us
    ppermute x12, waiting for transfers between devices, move(): return lax.ppermute(block, ('src', 'tgt'), pairs)  4.73 us
    pallas_call x1, Pallas kernels, row_pass_call(): pl.pallas_call(functools.partial(row_kernel, count), out_shape=vecs(copie...  4.57 us
    pallas_call x1, Pallas kernels, own_pass(): pl.pallas_call(own_kernel, out_shape=(pltpu.VMEM((rows, cols), jnp.float3...  1.95 us
  transfers between devices with their start and end apart: 12, of which 4 were waited for; matrix products, arithmetic and copies ran while one was open for 0% of the time, Pallas kernels for 8%

profile of v7, /device:TPU:1, one launch (start us, length us, event | category | flops | bytes accessed | tf_op | source)
XLA Modules:
  0.0 89.8 jit_solution(13707763024026853793)
XLA Ops:
  0.6 1.5 %collective-permute-start.3 = (bf16[256,512]{1,0:T(8,128)(2,1)}, bf16[256,512]{1,0:T(8,128)(2,1)S(1)}, u32[]{:S(2)}, u32[]{:S(2)}) collective-permute-start(bf16[256,512]{1,0:T(8,128)(2,1)} %refs_1_.1), channel_id=1, source_target_pairs={{0,16},{1,17},{2,18},{3,19},{4,20},{5,21},{6,22},{7,23},{8,24},{9,... | collective-permute-start | bytes 786440 | tf_op jit(solution)/shard_map/ppermute | solution.py:410
  2.1 3.0 %collective-permute-start = (bf16[128,512]{1,0:T(8,128)(2,1)}, bf16[128,512]{1,0:T(8,128)(2,1)S(1)}, u32[]{:S(2)}, u32[]{:S(2)}) collective-permute-start(bf16[128,512]{1,0:T(8,128)(2,1)} %refs_0_.1), channel_id=1, source_target_pairs={{0,2},{1,3},{2,0},{3,1},{4,6},{5,7},{6,4},{7,5},{8,10},{9,11},{10,... | collective-permute-start | bytes 393224 | tf_op jit(solution)/shard_map/ppermute | solution.py:410
  5.1 0.4 collective-permute-start.1
  5.5 2.3 %collective-permute-start.2 = (bf16[128,512]{1,0:T(8,128)(2,1)}, bf16[128,512]{1,0:T(8,128)(2,1)S(1)}, u32[]{:S(2)}, u32[]{:S(2)}) collective-permute-start(bf16[128,512]{1,0:T(8,128)(2,1)} %refs_0_.1), channel_id=1, source_target_pairs={{0,3},{1,0},{2,1},{3,2},{4,7},{5,4},{6,5},{7,6},{8,11},{9,8},{10,9... | collective-permute-start | bytes 393224 | tf_op jit(solution)/shard_map/ppermute | solution.py:410
  7.8 3.8 %collective-permute-start.4 = (bf16[256,512]{1,0:T(8,128)(2,1)}, bf16[256,512]{1,0:T(8,128)(2,1)S(1)}, u32[]{:S(2)}, u32[]{:S(2)}) collective-permute-start(bf16[256,512]{1,0:T(8,128)(2,1)} %refs_1_.1), channel_id=1, source_target_pairs={{0,32},{1,33},{2,34},{3,35},{4,36},{5,37},{6,38},{7,39},{8,40},{9,... | collective-permute-start | bytes 786440 | tf_op jit(solution)/shard_map/ppermute | solution.py:410
  11.6 1.1 %bring.1 = (bf16[128,512]{1,0:T(8,128)(2,1)S(1)}, bf16[256,512]{1,0:T(8,128)(2,1)S(1)}, f32[16,128]{1,0:T(8,128)S(1)}) custom-call(bf16[128,512]{1,0:T(8,128)(2,1)} %refs_0_.1, bf16[256,512]{1,0:T(8,128)(2,1)} %refs_1_.1, f32[16,128]{1,0:T(8,128)} %bitcast.7), custom_call_target="tpu_custom_call" | custom-call | tf_op jit(solution)/shard_map/bring/pallas_call | solution.py:307
  12.7 0.0 collective-permute-done.3.other_ref
  12.7 0.2 collective-permute-start.5
  12.9 1.3 %collective-permute-start.9 = (bf16[512,512]{1,0:T(8,128)(2,1)S(1)}, bf16[512,512]{1,0:T(8,128)(2,1)S(1)}, u32[]{:S(2)}, u32[]{:S(2)}) collective-permute-start(bf16[512,512]{1,0:T(8,128)(2,1)S(1)} %constant_dynamic-update-slice_fusion.refs_1_.points_ref), channel_id=1, source_target_pairs={{0,4},{1,5},{2,6},{3,7},{4,8},{5,9},{6,10},{7,11},{8,12},{9,13},{1... | collective-permute-start | bytes 1572872 | tf_op jit(solution)/shard_map/ppermute | solution.py:410
  14.2 1.0 %collective-permute-done.4.side_ref = bf16[256,512]{1,0:T(8,128)(2,1)S(1)} collective-permute-done((bf16[256,512]{1,0:T(8,128)(2,1)}, bf16[256,512]{1,0:T(8,128)(2,1)S(1)}, u32[]{:S(2)}, u32[]{:S(2)}) %collective-permute-start.4) | collective-permute-done | bytes 262176 | tf_op jit(solution)/shard_map/ppermute | solution.py:410
  15.2 3.1 %collective-permute-start.6 = (bf16[256,512]{1,0:T(8,128)(2,1)S(1)}, bf16[256,512]{1,0:T(8,128)(2,1)S(1)}, u32[]{:S(2)}, u32[]{:S(2)}) collective-permute-start(bf16[256,512]{1,0:T(8,128)(2,1)S(1)} %after.1), channel_id=1, source_target_pairs={{0,32},{1,33},{2,34},{3,35},{4,36},{5,37},{6,38},{7,39},{8,40},{9,... | collective-permute-start | bytes 786440 | tf_op jit(solution)/shard_map/ppermute | solution.py:410
  18.3 0.0 collective-permute-done.5.side_other_ref
  18.4 1.7 %collective-permute-start.7 = (bf16[512,512]{1,0:T(8,128)(2,1)S(1)}, bf16[512,512]{1,0:T(8,128)(2,1)S(1)}, u32[]{:S(2)}, u32[]{:S(2)}) collective-permute-start(bf16[512,512]{1,0:T(8,128)(2,1)S(1)} %pad_maximum_fusion), channel_id=1, source_target_pairs={{0,16},{1,17},{2,18},{3,19},{4,20},{5,21},{6,22},{7,23},{8,24},{9,... | collective-permute-start | bytes 1572872 | tf_op jit(solution)/shard_map/ppermute | solution.py:410
  20.1 0.9 %collective-permute-start.10 = (bf16[512,512]{1,0:T(8,128)(2,1)S(1)}, bf16[512,512]{1,0:T(8,128)(2,1)S(1)}, u32[]{:S(2)}, u32[]{:S(2)}) collective-permute-start(bf16[512,512]{1,0:T(8,128)(2,1)S(1)} %constant_dynamic-update-slice_fusion.refs_1_.points_ref), channel_id=1, source_target_pairs={{0,12},{1,13},{2,14},{3,15},{4,0},{5,1},{6,2},{7,3},{8,4},{9,5},{1... | collective-permute-start | bytes 1572872 | tf_op jit(solution)/shard_map/ppermute | solution.py:410
  21.0 0.6 collective-permute-done.6.far_ref
  21.6 3.2 %collective-permute-start.8 = (bf16[256,512]{1,0:T(8,128)(2,1)S(1)}, bf16[256,512]{1,0:T(8,128)(2,1)S(1)}, u32[]{:S(2)}, u32[]{:S(2)}) collective-permute-start(bf16[256,512]{1,0:T(8,128)(2,1)S(1)} %collective-permute-done.6.far_ref), channel_id=1, source_target_pairs={{0,16},{1,17},{2,18},{3,19},{4,20},{5,21},{6,22},{7,23},{8,24},{9,... | collective-permute-start | bytes 786440 | tf_op jit(solution)/shard_map/ppermute | solution.py:410
  24.9 0.0 collective-permute-start.11
  24.9 1.2 %collective-permute-done.8.theirs_far_ref = bf16[256,512]{1,0:T(8,128)(2,1)S(1)} collective-permute-done((bf16[256,512]{1,0:T(8,128)(2,1)S(1)}, bf16[256,512]{1,0:T(8,128)(2,1)S(1)}, u32[]{:S(2)}, u32[]{:S(2)}) %collective-permute-start.8) | collective-permute-done | bytes 262176 | tf_op jit(solution)/shard_map/ppermute | solution.py:410
  26.0 0.5 place.1
  26.6 2.0 %own_pass.1 = (f32[2048,2048]{1,0:T(8,128)S(1)}, f32[16,128]{1,0:T(8,128)S(1)}, f32[16,128]{1,0:T(8,128)S(1)}) custom-call(bf16[512,512]{1,0:T(8,128)(2,1)S(1)} %constant_dynamic-update-slice_fusion.refs_1_.points_ref, bf16[2048,512]{1,0:T(8,128)(2,1)S(1)} %get-tuple-element.28.tgt_ref, f32[16,128]{1,0:T(8,128)S(1)} %get-tuple-element.29.pot_ref), custom_call_target="tpu_custom_call" | custom-call | flops 1073741824 | bytes 8388608 | tf_op jit(solution)/shard_map/own_pass/pallas_call | solution.py:333
  28.5 2.0 %more_pass.3 = (f32[2048,2048]{1,0:T(8,128)S(1)}, f32[1,16,128]{2,1,0:T(8,128)S(1)}, f32[16,128]{1,0:T(8,128)S(1)}) custom-call(f32[2048,2048]{1,0:T(8,128)S(1)} %get-tuple-element.30.score_in_ref, f32[16,128]{1,0:T(8,128)S(1)} %get-tuple-element.31.rows_in_ref, f32[16,128]{1,0:T(8,128)S(1)} %get-tuple-element.32.src_sq_in_ref, ...), custom_call_target="tpu_custom_call", output_to_operand_aliasing={{0}: (0, {})} | custom-call | flops 1073741824 | bytes 8388608 | tf_op jit(solution)/shard_map/more_pass/pallas_call | solution.py:350
  30.5 2.0 %more_pass.4 = (f32[2048,2048]{1,0:T(8,128)S(1)}, f32[1,16,128]{2,1,0:T(8,128)S(1)}, f32[16,128]{1,0:T(8,128)S(1)}) custom-call(f32[2048,2048]{1,0:T(8,128)S(1)} %get-tuple-element.33.score_in_ref, f32[16,128]{1,0:T(8,128)S(1)} %bitcast.6, f32[16,128]{1,0:T(8,128)S(1)} %get-tuple-element.35.src_sq_in_ref, ...), custom_call_target="tpu_custom_call", output_to_operand_aliasing={{0}: (0, {})} | custom-call | flops 1073741824 | bytes 8388608 | tf_op jit(solution)/shard_map/more_pass/pallas_call | solution.py:350
  32.5 1.9 %collective-permute-done.11.refs_0_ = bf16[512,512]{1,0:T(8,128)(2,1)S(1)} collective-permute-done((bf16[512,512]{1,0:T(8,128)(2,1)S(1)}, bf16[512,512]{1,0:T(8,128)(2,1)S(1)}, u32[]{:S(2)}, u32[]{:S(2)}) %collective-permute-start.11) | collective-permute-done | bytes 524320 | tf_op jit(solution)/shard_map/ppermute | solution.py:410
  34.4 2.0 %more_pass.5 = (f32[2048,2048]{1,0:T(8,128)S(1)}, f32[16,16,128]{2,1,0:T(8,128)S(1)}, f32[16,128]{1,0:T(8,128)S(1)}) custom-call(f32[2048,2048]{1,0:T(8,128)S(1)} %get-tuple-element.36.score_in_ref, f32[16,128]{1,0:T(8,128)S(1)} %bitcast.5, f32[16,128]{1,0:T(8,128)S(1)} %get-tuple-element.38.src_sq_in_ref, ...), custom_call_target="tpu_custom_call", output_to_operand_aliasing={{0}: (0, {})} | custom-call | flops 1073741824 | bytes 8388608 | tf_op jit(solution)/shard_map/more_pass/pallas_call | solution.py:350
  36.4 11.0 %all_to_all.20.parts_ref = f32[16,16,128]{2,1,0:T(8,128)S(1)} all-to-all(f32[16,16,128]{2,1,0:T(8,128)S(1)} %get-tuple-element.40), channel_id=1, replica_groups=mesh['src'=8,'tgt'=16] {'tgt'}, dimensions={0} | all-to-all | bytes 262144 | tf_op jit(solution)/shard_map/all_to_all | solution.py:402
  47.4 4.2 %col_pass.2 = (f32[16,128]{1,0:T(8,128)}, f32[8,16,128]{2,1,0:T(8,128)S(1)}) custom-call(f32[2048,2048]{1,0:T(8,128)S(1)} %get-tuple-element.39.score_ref, f32[16,16,128]{2,1,0:T(8,128)S(1)} %all_to_all.20.parts_ref), custom_call_target="tpu_custom_call" | custom-call | tf_op jit(solution)/shard_map/col_pass/pallas_call | solution.py:379
  51.6 9.8 %all_to_all.21.parts_ref = f32[8,16,128]{2,1,0:T(8,128)S(1)} all-to-all(f32[8,16,128]{2,1,0:T(8,128)S(1)} %get-tuple-element.41), channel_id=1, replica_groups=mesh['src'=8,'tgt'=16] {'src'}, dimensions={0} | all-to-all | bytes 131072 | tf_op jit(solution)/shard_map/all_to_all | solution.py:402
  61.4 4.6 %row_pass.1 = f32[16,16,128]{2,1,0:T(8,128)S(1)} custom-call(f32[2048,2048]{1,0:T(8,128)S(1)} %get-tuple-element.39.score_ref, f32[8,16,128]{2,1,0:T(8,128)S(1)} %all_to_all.21.parts_ref), custom_call_target="tpu_custom_call" | custom-call | tf_op jit(solution)/shard_map/row_pass/pallas_call | solution.py:365
  65.9 9.7 %all_to_all.22.parts_ref = f32[16,16,128]{2,1,0:T(8,128)S(1)} all-to-all(f32[16,16,128]{2,1,0:T(8,128)S(1)} %row_pass.1), channel_id=1, replica_groups=mesh['src'=8,'tgt'=16] {'tgt'}, dimensions={0} | all-to-all | bytes 262144 | tf_op jit(solution)/shard_map/all_to_all | solution.py:402
  75.6 4.1 %col_pass.3 = (f32[16,128]{1,0:T(8,128)S(1)}, f32[8,16,128]{2,1,0:T(8,128)S(1)}) custom-call(f32[2048,2048]{1,0:T(8,128)S(1)} %get-tuple-element.39.score_ref, f32[16,16,128]{2,1,0:T(8,128)S(1)} %all_to_all.22.parts_ref), custom_call_target="tpu_custom_call" | custom-call | tf_op jit(solution)/shard_map/col_pass/pallas_call | solution.py:379
  79.7 9.4 %all_to_all.23.parts_ref = f32[8,16,128]{2,1,0:T(8,128)S(1)} all-to-all(f32[8,16,128]{2,1,0:T(8,128)S(1)} %get-tuple-element.42), channel_id=1, replica_groups=mesh['src'=8,'tgt'=16] {'src'}, dimensions={0} | all-to-all | bytes 131072 | tf_op jit(solution)/shard_map/all_to_all | solution.py:402
  89.1 0.6 last.1
  (13 shorter events, 0.1 us)
Async XLA Ops:
  0.6 12.1 %collective-permute-start.3 = (bf16[256,512]{1,0:T(8,128)(2,1)}, bf16[256,512]{1,0:T(8,128)(2,1)S(1)}, u32[]{:S(2)}, u32[]{:S(2)}) collective-permute-start(bf16[256,512]{1,0:T(8,128)(2,1)} %refs_1_.1), channel_id=1, source_target_pairs={{0,16},{1,17},{2,18},{3,19},{4,20},{5,21},{6,22},{7,23},{8,24},{9,... | collective-permute-start | bytes 786440 | tf_op jit(solution)/shard_map/ppermute | solution.py:410
  2.1 10.5 %collective-permute-start = (bf16[128,512]{1,0:T(8,128)(2,1)}, bf16[128,512]{1,0:T(8,128)(2,1)S(1)}, u32[]{:S(2)}, u32[]{:S(2)}) collective-permute-start(bf16[128,512]{1,0:T(8,128)(2,1)} %refs_0_.1), channel_id=1, source_target_pairs={{0,2},{1,3},{2,0},{3,1},{4,6},{5,7},{6,4},{7,5},{8,10},{9,11},{10,... | collective-permute-start | bytes 393224 | tf_op jit(solution)/shard_map/ppermute | solution.py:410
  5.1 7.8 %collective-permute-start.1 = (bf16[128,512]{1,0:T(8,128)(2,1)}, bf16[128,512]{1,0:T(8,128)(2,1)S(1)}, u32[]{:S(2)}, u32[]{:S(2)}) collective-permute-start(bf16[128,512]{1,0:T(8,128)(2,1)} %refs_0_.1), channel_id=1, source_target_pairs={{0,1},{1,2},{2,3},{3,0},{4,5},{5,6},{6,7},{7,4},{8,9},{9,10},{10,1... | collective-permute-start | bytes 393224 | tf_op jit(solution)/shard_map/ppermute | solution.py:410
  5.5 7.4 %collective-permute-start.2 = (bf16[128,512]{1,0:T(8,128)(2,1)}, bf16[128,512]{1,0:T(8,128)(2,1)S(1)}, u32[]{:S(2)}, u32[]{:S(2)}) collective-permute-start(bf16[128,512]{1,0:T(8,128)(2,1)} %refs_0_.1), channel_id=1, source_target_pairs={{0,3},{1,0},{2,1},{3,2},{4,7},{5,4},{6,5},{7,6},{8,11},{9,8},{10,9... | collective-permute-start | bytes 393224 | tf_op jit(solution)/shard_map/ppermute | solution.py:410
  7.8 7.4 %collective-permute-start.4 = (bf16[256,512]{1,0:T(8,128)(2,1)}, bf16[256,512]{1,0:T(8,128)(2,1)S(1)}, u32[]{:S(2)}, u32[]{:S(2)}) collective-permute-start(bf16[256,512]{1,0:T(8,128)(2,1)} %refs_1_.1), channel_id=1, source_target_pairs={{0,32},{1,33},{2,34},{3,35},{4,36},{5,37},{6,38},{7,39},{8,40},{9,... | collective-permute-start | bytes 786440 | tf_op jit(solution)/shard_map/ppermute | solution.py:410
  12.7 5.6 %collective-permute-start.5 = (bf16[256,512]{1,0:T(8,128)(2,1)S(1)}, bf16[256,512]{1,0:T(8,128)(2,1)S(1)}, u32[]{:S(2)}, u32[]{:S(2)}) collective-permute-start(bf16[256,512]{1,0:T(8,128)(2,1)S(1)} %collective-permute-done.3.other_ref), channel_id=1, source_target_pairs={{0,32},{1,33},{2,34},{3,35},{4,36},{5,37},{6,38},{7,39},{8,40},{9,... | collective-permute-start | bytes 786440 | tf_op jit(solution)/shard_map/ppermute | solution.py:410
  12.9 11.9 %collective-permute-start.9 = (bf16[512,512]{1,0:T(8,128)(2,1)S(1)}, bf16[512,512]{1,0:T(8,128)(2,1)S(1)}, u32[]{:S(2)}, u32[]{:S(2)}) collective-permute-start(bf16[512,512]{1,0:T(8,128)(2,1)S(1)} %constant_dynamic-update-slice_fusion.refs_1_.points_ref), channel_id=1, source_target_pairs={{0,4},{1,5},{2,6},{3,7},{4,8},{5,9},{6,10},{7,11},{8,12},{9,13},{1... | collective-permute-start | bytes 1572872 | tf_op jit(solution)/shard_map/ppermute | solution.py:410
  15.2 6.4 %collective-permute-start.6 = (bf16[256,512]{1,0:T(8,128)(2,1)S(1)}, bf16[256,512]{1,0:T(8,128)(2,1)S(1)}, u32[]{:S(2)}, u32[]{:S(2)}) collective-permute-start(bf16[256,512]{1,0:T(8,128)(2,1)S(1)} %after.1), channel_id=1, source_target_pairs={{0,32},{1,33},{2,34},{3,35},{4,36},{5,37},{6,38},{7,39},{8,40},{9,... | collective-permute-start | bytes 786440 | tf_op jit(solution)/shard_map/ppermute | solution.py:410
  18.4 7.7 %collective-permute-start.7 = (bf16[512,512]{1,0:T(8,128)(2,1)S(1)}, bf16[512,512]{1,0:T(8,128)(2,1)S(1)}, u32[]{:S(2)}, u32[]{:S(2)}) collective-permute-start(bf16[512,512]{1,0:T(8,128)(2,1)S(1)} %pad_maximum_fusion), channel_id=1, source_target_pairs={{0,16},{1,17},{2,18},{3,19},{4,20},{5,21},{6,22},{7,23},{8,24},{9,... | collective-permute-start | bytes 1572872 | tf_op jit(solution)/shard_map/ppermute | solution.py:410
  20.1 10.4 %collective-permute-start.10 = (bf16[512,512]{1,0:T(8,128)(2,1)S(1)}, bf16[512,512]{1,0:T(8,128)(2,1)S(1)}, u32[]{:S(2)}, u32[]{:S(2)}) collective-permute-start(bf16[512,512]{1,0:T(8,128)(2,1)S(1)} %constant_dynamic-update-slice_fusion.refs_1_.points_ref), channel_id=1, source_target_pairs={{0,12},{1,13},{2,14},{3,15},{4,0},{5,1},{6,2},{7,3},{8,4},{9,5},{1... | collective-permute-start | bytes 1572872 | tf_op jit(solution)/shard_map/ppermute | solution.py:410
  21.6 4.4 %collective-permute-start.8 = (bf16[256,512]{1,0:T(8,128)(2,1)S(1)}, bf16[256,512]{1,0:T(8,128)(2,1)S(1)}, u32[]{:S(2)}, u32[]{:S(2)}) collective-permute-start(bf16[256,512]{1,0:T(8,128)(2,1)S(1)} %collective-permute-done.6.far_ref), channel_id=1, source_target_pairs={{0,16},{1,17},{2,18},{3,19},{4,20},{5,21},{6,22},{7,23},{8,24},{9,... | collective-permute-start | bytes 786440 | tf_op jit(solution)/shard_map/ppermute | solution.py:410
  24.9 9.5 %collective-permute-start.11 = (bf16[512,512]{1,0:T(8,128)(2,1)S(1)}, bf16[512,512]{1,0:T(8,128)(2,1)S(1)}, u32[]{:S(2)}, u32[]{:S(2)}) collective-permute-start(bf16[512,512]{1,0:T(8,128)(2,1)S(1)} %collective-permute-done.9.refs_0_), channel_id=1, source_target_pairs={{0,4},{1,5},{2,6},{3,7},{4,8},{5,9},{6,10},{7,11},{8,12},{9,13},{1... | collective-permute-start | bytes 1572872 | tf_op jit(solution)/shard_map/ppermute | solution.py:410

commit v8 on v7

--- a/solution.py
+++ b/solution.py
@@ -9,15 +9,12 @@
 from jax.experimental.pallas import tpu as pltpu
 from jax.sharding import PartitionSpec as P
 
-ITERS = 2
-
-
 EPSILON = 0.05
 UNIT = EPSILON * math.log(2.0)
 
 LANES = 128
 SUB = 8
-VMEM_LIMIT = 16 * 1024 * 1024
+VMEM_LIMIT = 12 * 1024 * 1024
 
 
 def tree(op, values):
@@ -228,39 +225,92 @@
     repeat(part_ref, rows_ref[...])
 
 
-def col_kernel(
-    count, score_ref, parts_ref, pot_ref, part_ref, peaks, totals, even, odd
-):
-    merge_parts(parts_ref, count, pot_ref)
-    rows, cols = score_ref.shape
-    blocks = rows // LANES
-
+def by_row_blocks(pot_ref, blocks, reduce, even, odd):
     def widen(block, into):
         row = pot_ref[pl.ds(row_index(block), 1), :]
         into[...] = jnp.broadcast_to(row, (LANES, LANES)).T
 
-    def reduce(block, wide):
+    def run(block, wide):
         here = pl.ds(pl.multiple_of(block * LANES, LANES), LANES)
         there = pl.ds(pl.multiple_of(block * SUB, SUB), SUB)
-        pots = wide[...]
-        for k in range(cols // LANES):
-            lanes = slice(k * LANES, (k + 1) * LANES)
-            tile = score_ref[here, lanes] + pots
-            tiles = [tile[i : i + SUB] for i in range(0, LANES, SUB)]
-            peak = tree(jnp.maximum, tiles)
-            peaks[there, lanes] = peak
-            totals[there, lanes] = power_sum(tiles, peak)
+        reduce(here, there, wide[...])
 
     def step(block, is_even):
         widen(block, even if is_even else odd)
-        reduce(block - 1, odd if is_even else even)
+        run(block - 1, odd if is_even else even)
 
     widen(0, even)
     two_by_two(blocks, step)
-    reduce(blocks - 1, odd)
-    for k in range(cols // LANES):
-        lanes = slice(k * LANES, (k + 1) * LANES)
+    run(blocks - 1, odd)
+
+
+def column_tiles(cols):
+    return [slice(k, k + LANES) for k in range(0, cols, LANES)]
+
+
+def row_groups(tile):
+    return [tile[i : i + SUB] for i in range(0, LANES, SUB)]
+
+
+def exact_columns(score_ref, pot_ref, part_ref, peaks, totals, even, odd, table_ref=None):
+    rows, cols = score_ref.shape
+
+    def reduce(here, there, pots):
+        for lanes in column_tiles(cols):
+            tiles = row_groups(score_ref[here, lanes] + pots)
+            peak = tree(jnp.maximum, tiles)
+            powers = [jnp.exp2(tile - peak) for tile in tiles]
+            peaks[there, lanes] = peak
+            totals[there, lanes] = tree(jnp.add, powers)
+            if table_ref is not None:
+                table_ref[here, lanes] = jnp.concatenate(powers, axis=0).astype(jnp.bfloat16)
+
+    by_row_blocks(pot_ref, rows // LANES, reduce, even, odd)
+    for k, lanes in enumerate(column_tiles(cols)):
         part_ref[0, k : k + 1, :] = merge(peaks[:, lanes], totals[:, lanes])
+
+
+def col_kernel(
+    count, score_ref, parts_ref, pot_ref, part_ref, table_ref, peaks, totals, even, odd
+):
+    merge_parts(parts_ref, count, pot_ref)
+    exact_columns(score_ref, pot_ref, part_ref, peaks, totals, even, odd, table_ref)
+    repeat(part_ref, part_ref[0])
+
+
+FLOOR = 1e-28
+LARGEST = 1e30
+
+
+def last_col_kernel(
+    count, score_ref, parts_ref, table_ref, kept_ref, before_ref, pot_ref, part_ref,
+    ratio_ref, peaks, totals, even, odd,
+):
+    merge_parts(parts_ref, count, pot_ref)
+    ratio = jnp.exp2(pot_ref[...] - before_ref[...])
+    ratio_ref[...] = ratio
+    rows, cols = score_ref.shape
+
+    def reduce(here, there, weights):
+        for lanes in column_tiles(cols):
+            tile = table_ref[here, lanes].astype(jnp.float32) * weights
+            totals[there, lanes] = tree(jnp.add, row_groups(tile))
+
+    by_row_blocks(ratio_ref, rows // LANES, reduce, even, odd)
+    sums = []
+    for k, lanes in enumerate(column_tiles(cols)):
+        peak = jnp.max(kept_ref[:, lanes], axis=0, keepdims=True)
+        scaled = totals[:, lanes] * jnp.exp2(kept_ref[:, lanes] - peak)
+        sums.append(jnp.sum(scaled, axis=0, keepdims=True))
+        part_ref[0, k : k + 1, :] = peak + jnp.log2(sums[-1])
+
+    largest, least = jnp.max(ratio), jnp.min(tree(jnp.minimum, sums))
+    whole = (largest <= LARGEST) & (least >= FLOOR * jnp.maximum(largest, 1.0))
+
+    @pl.when(jnp.logical_not(whole))
+    def _():
+        exact_columns(score_ref, pot_ref, part_ref, peaks, totals, even, odd)
+
     repeat(part_ref, part_ref[0])
 
 
@@ -374,17 +424,43 @@
     )(score, parts)
 
 
+def in_vmem(*arrays):
+    return [pltpu.with_memory_space_constraint(array, pltpu.VMEM) for array in arrays]
+
+
 def col_pass_call(score, parts, count, copies):
     rows, cols = score.shape
-    return pl.pallas_call(
+    kept = (rows // LANES * SUB, cols)
+    red_f, part, *table = pl.pallas_call(
         functools.partial(col_kernel, count),
+        out_shape=(
+            pltpu.VMEM((rows // LANES, LANES), jnp.float32),
+            vecs(copies, cols),
+            pltpu.VMEM((rows, cols), jnp.bfloat16),
+            pltpu.VMEM(kept, jnp.float32),
+        ),
+        in_specs=[IN_VMEM] * 2,
+        out_specs=(IN_VMEM,) * 4,
+        scratch_shapes=[scratch(*kept)] + [scratch(LANES, LANES)] * 2,
+        compiler_params=params(),
+        name="col_pass",
+    )(*in_vmem(score), parts)
+    return red_f, part, table
+
+
+def last_col_call(score, parts, table, before, count, copies):
+    rows, cols = score.shape
+    return pl.pallas_call(
+        functools.partial(last_col_kernel, count),
         out_shape=(pltpu.VMEM((rows // LANES, LANES), jnp.float32), vecs(copies, cols)),
-        in_specs=[IN_VMEM] * 2,
+        in_specs=[IN_VMEM] * 5,
         out_specs=(IN_VMEM, IN_VMEM),
-        scratch_shapes=[scratch(rows // LANES * SUB, cols)] * 2 + [scratch(LANES, LANES)] * 2,
-        compiler_params=params(),
-        name="col_pass",
-    )(score, parts)
+        scratch_shapes=[scratch(rows // LANES, LANES)]
+        + [scratch(rows // LANES * SUB, cols)] * 2
+        + [scratch(LANES, LANES)] * 2,
+        compiler_params=params(),
+        name="last_col_pass",
+    )(*in_vmem(score), parts, *in_vmem(*table, before))
 
 
 def last_call(parts, pot_f, src_sq, tgt_sq, count):
@@ -470,12 +546,13 @@
         state = score, part[0], src_sq
     score, part, src_sq = more_pass(state, (far,), (8,), targets, red_g, n_tgt)
     score = pltpu.with_memory_space_constraint(score, pltpu.VMEM)
-    for step in range(ITERS):
-        if step:
-            part = row_pass_call(score, parts, total_src, n_tgt)
-        parts = exchange(part, "tgt")
-        red_f, part = col_pass_call(score, parts, total_tgt, n_src)
-        parts = exchange(part, "src")
+    parts = exchange(part, "tgt")
+    first_f, part, table = col_pass_call(score, parts, total_tgt, n_src)
+    parts = exchange(part, "src")
+    part = row_pass_call(score, parts, total_src, n_tgt)
+    parts = exchange(part, "tgt")
+    red_f, part = last_col_call(score, parts, table, first_f, total_tgt, n_src)
+    parts = exchange(part, "src")
     pot_f, pot_g = last_call(parts, red_f, src_sq, tgt_sq, total_src)
     return (pot_f.reshape(-1), pot_g.reshape(-1))
 

time: 90 us -> 88.6 us (0.984)
  Pallas kernels: 23 us -> 21.6 us
    pallas_call x2 -> x1, Pallas kernels: 8.35 us -> 4.39 us  [col_pass_call(): pl.pallas_call(functools.partial(col_kernel, count), out_shape=(pltpu.VME...]
    pallas_call x0 -> x1, Pallas kernels: none -> 2.52 us  [last_col_call(): pl.pallas_call(functools.partial(last_col_kernel, count), out_shape=(pltp...]
where the time goes in v8:
time: 88.6 us; the launch traced here: 88.3 us
  blocking collectives  39.8 us (45%)
  Pallas kernels  21.6 us (24%)
  starting transfers between devices  21.3 us (24%)
  waiting for transfers between devices  4.74 us (5%)
    all_to_all x4, blocking collectives, exchange(): return lax.all_to_all(part, axis, 0, 0, tiled=True)  39.8 us
    ppermute x12, starting transfers between devices, move(): return lax.ppermute(block, ('src', 'tgt'), pairs)  21.3 us
    pallas_call x3, Pallas kernels, more_pass(): pl.pallas_call(functools.partial(more_kernel, blocks), out_shape=(pltpu.V...  5.9 us
    ppermute x12, waiting for transfers between devices, move(): return lax.ppermute(block, ('src', 'tgt'), pairs)  4.74 us
    pallas_call x1, Pallas kernels, row_pass_call(): pl.pallas_call(functools.partial(row_kernel, count), out_shape=vecs(copie...  4.57 us
    pallas_call x1, Pallas kernels, col_pass_call(): pl.pallas_call(functools.partial(col_kernel, count), out_shape=(pltpu.VME...  4.39 us
    pallas_call x1, Pallas kernels, last_col_call(): pl.pallas_call(functools.partial(last_col_kernel, count), out_shape=(pltp...  2.52 us
    pallas_call x1, Pallas kernels, own_pass(): pl.pallas_call(own_kernel, out_shape=(pltpu.VMEM((rows, cols), jnp.float3...  1.95 us
  transfers between devices with their start and end apart: 12, of which 4 were waited for; matrix products, arithmetic and copies ran while one was open for 0% of the time, Pallas kernels for 8%

profile of v8, /device:TPU:1, one launch (start us, length us, event | category | flops | bytes accessed | tf_op | source)
XLA Modules:
  0.0 88.3 jit_solution(1846080305975526135)
XLA Ops:
  0.6 1.5 %collective-permute-start.3 = (bf16[256,512]{1,0:T(8,128)(2,1)}, bf16[256,512]{1,0:T(8,128)(2,1)S(1)}, u32[]{:S(2)}, u32[]{:S(2)}) collective-permute-start(bf16[256,512]{1,0:T(8,128)(2,1)} %refs_1_.1), channel_id=1, source_target_pairs={{0,16},{1,17},{2,18},{3,19},{4,20},{5,21},{6,22},{7,23},{8,24},{9,... | collective-permute-start | bytes 786440 | tf_op jit(solution)/shard_map/ppermute | solution.py:486
  2.1 3.0 %collective-permute-start = (bf16[128,512]{1,0:T(8,128)(2,1)}, bf16[128,512]{1,0:T(8,128)(2,1)S(1)}, u32[]{:S(2)}, u32[]{:S(2)}) collective-permute-start(bf16[128,512]{1,0:T(8,128)(2,1)} %refs_0_.1), channel_id=1, source_target_pairs={{0,2},{1,3},{2,0},{3,1},{4,6},{5,7},{6,4},{7,5},{8,10},{9,11},{10,... | collective-permute-start | bytes 393224 | tf_op jit(solution)/shard_map/ppermute | solution.py:486
  5.1 0.4 collective-permute-start.1
  5.5 2.3 %collective-permute-start.2 = (bf16[128,512]{1,0:T(8,128)(2,1)}, bf16[128,512]{1,0:T(8,128)(2,1)S(1)}, u32[]{:S(2)}, u32[]{:S(2)}) collective-permute-start(bf16[128,512]{1,0:T(8,128)(2,1)} %refs_0_.1), channel_id=1, source_target_pairs={{0,3},{1,0},{2,1},{3,2},{4,7},{5,4},{6,5},{7,6},{8,11},{9,8},{10,9... | collective-permute-start | bytes 393224 | tf_op jit(solution)/shard_map/ppermute | solution.py:486
  7.8 3.8 %collective-permute-start.4 = (bf16[256,512]{1,0:T(8,128)(2,1)}, bf16[256,512]{1,0:T(8,128)(2,1)S(1)}, u32[]{:S(2)}, u32[]{:S(2)}) collective-permute-start(bf16[256,512]{1,0:T(8,128)(2,1)} %refs_1_.1), channel_id=1, source_target_pairs={{0,32},{1,33},{2,34},{3,35},{4,36},{5,37},{6,38},{7,39},{8,40},{9,... | collective-permute-start | bytes 786440 | tf_op jit(solution)/shard_map/ppermute | solution.py:486
  11.6 1.1 %bring.1 = (bf16[128,512]{1,0:T(8,128)(2,1)S(1)}, bf16[256,512]{1,0:T(8,128)(2,1)S(1)}, f32[16,128]{1,0:T(8,128)S(1)}) custom-call(bf16[128,512]{1,0:T(8,128)(2,1)} %refs_0_.1, bf16[256,512]{1,0:T(8,128)(2,1)} %refs_1_.1, f32[16,128]{1,0:T(8,128)} %bitcast.7), custom_call_target="tpu_custom_call" | custom-call | tf_op jit(solution)/shard_map/bring/pallas_call | solution.py:357
  12.7 0.0 collective-permute-done.3.other_ref
  12.7 0.2 collective-permute-start.5
  12.9 1.3 %collective-permute-start.9 = (bf16[512,512]{1,0:T(8,128)(2,1)S(1)}, bf16[512,512]{1,0:T(8,128)(2,1)S(1)}, u32[]{:S(2)}, u32[]{:S(2)}) collective-permute-start(bf16[512,512]{1,0:T(8,128)(2,1)S(1)} %constant_dynamic-update-slice_fusion.refs_1_.points_ref), channel_id=1, source_target_pairs={{0,4},{1,5},{2,6},{3,7},{4,8},{5,9},{6,10},{7,11},{8,12},{9,13},{1... | collective-permute-start | bytes 1572872 | tf_op jit(solution)/shard_map/ppermute | solution.py:486
  14.2 1.0 %collective-permute-done.4.side_ref = bf16[256,512]{1,0:T(8,128)(2,1)S(1)} collective-permute-done((bf16[256,512]{1,0:T(8,128)(2,1)}, bf16[256,512]{1,0:T(8,128)(2,1)S(1)}, u32[]{:S(2)}, u32[]{:S(2)}) %collective-permute-start.4) | collective-permute-done | bytes 262176 | tf_op jit(solution)/shard_map/ppermute | solution.py:486
  15.2 3.1 %collective-permute-start.6 = (bf16[256,512]{1,0:T(8,128)(2,1)S(1)}, bf16[256,512]{1,0:T(8,128)(2,1)S(1)}, u32[]{:S(2)}, u32[]{:S(2)}) collective-permute-start(bf16[256,512]{1,0:T(8,128)(2,1)S(1)} %after.1), channel_id=1, source_target_pairs={{0,32},{1,33},{2,34},{3,35},{4,36},{5,37},{6,38},{7,39},{8,40},{9,... | collective-permute-start | bytes 786440 | tf_op jit(solution)/shard_map/ppermute | solution.py:486
  18.3 0.0 collective-permute-done.5.side_other_ref
  18.4 1.7 %collective-permute-start.7 = (bf16[512,512]{1,0:T(8,128)(2,1)S(1)}, bf16[512,512]{1,0:T(8,128)(2,1)S(1)}, u32[]{:S(2)}, u32[]{:S(2)}) collective-permute-start(bf16[512,512]{1,0:T(8,128)(2,1)S(1)} %pad_maximum_fusion), channel_id=1, source_target_pairs={{0,16},{1,17},{2,18},{3,19},{4,20},{5,21},{6,22},{7,23},{8,24},{9,... | collective-permute-start | bytes 1572872 | tf_op jit(solution)/shard_map/ppermute | solution.py:486
  20.1 0.9 %collective-permute-start.10 = (bf16[512,512]{1,0:T(8,128)(2,1)S(1)}, bf16[512,512]{1,0:T(8,128)(2,1)S(1)}, u32[]{:S(2)}, u32[]{:S(2)}) collective-permute-start(bf16[512,512]{1,0:T(8,128)(2,1)S(1)} %constant_dynamic-update-slice_fusion.refs_1_.points_ref), channel_id=1, source_target_pairs={{0,12},{1,13},{2,14},{3,15},{4,0},{5,1},{6,2},{7,3},{8,4},{9,5},{1... | collective-permute-start | bytes 1572872 | tf_op jit(solution)/shard_map/ppermute | solution.py:486
  21.0 0.6 collective-permute-done.6.far_ref
  21.6 3.2 %collective-permute-start.8 = (bf16[256,512]{1,0:T(8,128)(2,1)S(1)}, bf16[256,512]{1,0:T(8,128)(2,1)S(1)}, u32[]{:S(2)}, u32[]{:S(2)}) collective-permute-start(bf16[256,512]{1,0:T(8,128)(2,1)S(1)} %collective-permute-done.6.far_ref), channel_id=1, source_target_pairs={{0,16},{1,17},{2,18},{3,19},{4,20},{5,21},{6,22},{7,23},{8,24},{9,... | collective-permute-start | bytes 786440 | tf_op jit(solution)/shard_map/ppermute | solution.py:486
  24.9 0.0 collective-permute-start.11
  24.9 1.2 %collective-permute-done.8.theirs_far_ref = bf16[256,512]{1,0:T(8,128)(2,1)S(1)} collective-permute-done((bf16[256,512]{1,0:T(8,128)(2,1)S(1)}, bf16[256,512]{1,0:T(8,128)(2,1)S(1)}, u32[]{:S(2)}, u32[]{:S(2)}) %collective-permute-start.8) | collective-permute-done | bytes 262176 | tf_op jit(solution)/shard_map/ppermute | solution.py:486
  26.0 0.5 place.1
  26.6 2.0 %own_pass.1 = (f32[2048,2048]{1,0:T(8,128)S(1)}, f32[16,128]{1,0:T(8,128)S(1)}, f32[16,128]{1,0:T(8,128)S(1)}) custom-call(bf16[512,512]{1,0:T(8,128)(2,1)S(1)} %constant_dynamic-update-slice_fusion.refs_1_.points_ref, bf16[2048,512]{1,0:T(8,128)(2,1)S(1)} %get-tuple-element.31.tgt_ref, f32[16,128]{1,0:T(8,128)S(1)} %get-tuple-element.32.pot_ref), custom_call_target="tpu_custom_call" | custom-call | flops 1073741824 | bytes 8388608 | tf_op jit(solution)/shard_map/own_pass/pallas_call | solution.py:383
  28.5 2.0 %more_pass.3 = (f32[2048,2048]{1,0:T(8,128)S(1)}, f32[1,16,128]{2,1,0:T(8,128)S(1)}, f32[16,128]{1,0:T(8,128)S(1)}) custom-call(f32[2048,2048]{1,0:T(8,128)S(1)} %get-tuple-element.33.score_in_ref, f32[16,128]{1,0:T(8,128)S(1)} %get-tuple-element.34.rows_in_ref, f32[16,128]{1,0:T(8,128)S(1)} %get-tuple-element.35.src_sq_in_ref, ...), custom_call_target="tpu_custom_call", output_to_operand_aliasing={{0}: (0, {})} | custom-call | flops 1073741824 | bytes 8388608 | tf_op jit(solution)/shard_map/more_pass/pallas_call | solution.py:400
  30.5 2.0 %more_pass.4 = (f32[2048,2048]{1,0:T(8,128)S(1)}, f32[1,16,128]{2,1,0:T(8,128)S(1)}, f32[16,128]{1,0:T(8,128)S(1)}) custom-call(f32[2048,2048]{1,0:T(8,128)S(1)} %get-tuple-element.36.score_in_ref, f32[16,128]{1,0:T(8,128)S(1)} %bitcast.6, f32[16,128]{1,0:T(8,128)S(1)} %get-tuple-element.38.src_sq_in_ref, ...), custom_call_target="tpu_custom_call", output_to_operand_aliasing={{0}: (0, {})} | custom-call | flops 1073741824 | bytes 8388608 | tf_op jit(solution)/shard_map/more_pass/pallas_call | solution.py:400
  32.5 1.9 %collective-permute-done.11.refs_0_ = bf16[512,512]{1,0:T(8,128)(2,1)S(1)} collective-permute-done((bf16[512,512]{1,0:T(8,128)(2,1)S(1)}, bf16[512,512]{1,0:T(8,128)(2,1)S(1)}, u32[]{:S(2)}, u32[]{:S(2)}) %collective-permute-start.11) | collective-permute-done | bytes 524320 | tf_op jit(solution)/shard_map/ppermute | solution.py:486
  34.4 2.0 %more_pass.5 = (f32[2048,2048]{1,0:T(8,128)S(1)}, f32[16,16,128]{2,1,0:T(8,128)S(1)}, f32[16,128]{1,0:T(8,128)S(1)}) custom-call(f32[2048,2048]{1,0:T(8,128)S(1)} %get-tuple-element.39.score_in_ref, f32[16,128]{1,0:T(8,128)S(1)} %bitcast.5, f32[16,128]{1,0:T(8,128)S(1)} %get-tuple-element.41.src_sq_in_ref, ...), custom_call_target="tpu_custom_call", output_to_operand_aliasing={{0}: (0, {})} | custom-call | flops 1073741824 | bytes 8388608 | tf_op jit(solution)/shard_map/more_pass/pallas_call | solution.py:400
  36.4 11.0 %all_to_all.20.parts_ref = f32[16,16,128]{2,1,0:T(8,128)S(1)} all-to-all(f32[16,16,128]{2,1,0:T(8,128)S(1)} %get-tuple-element.43), channel_id=1, replica_groups=mesh['src'=8,'tgt'=16] {'tgt'}, dimensions={0} | all-to-all | bytes 262144 | tf_op jit(solution)/shard_map/all_to_all | solution.py:478
  47.4 4.4 %col_pass.1 = (f32[16,128]{1,0:T(8,128)S(1)}, f32[8,16,128]{2,1,0:T(8,128)S(1)}, bf16[2048,2048]{1,0:T(8,128)(2,1)S(1)}, f32[128,2048]{1,0:T(8,128)S(1)}) custom-call(f32[2048,2048]{1,0:T(8,128)S(1)} %get-tuple-element.42.score_ref, f32[16,16,128]{2,1,0:T(8,128)S(1)} %all_to_all.20.parts_ref), custom_call_target="tpu_custom_call" | custom-call | tf_op jit(solution)/shard_map/col_pass/pallas_call | solution.py:434
  51.8 9.8 %all_to_all.21.parts_ref = f32[8,16,128]{2,1,0:T(8,128)S(1)} all-to-all(f32[8,16,128]{2,1,0:T(8,128)S(1)} %get-tuple-element.44), channel_id=1, replica_groups=mesh['src'=8,'tgt'=16] {'src'}, dimensions={0} | all-to-all | bytes 131072 | tf_op jit(solution)/shard_map/all_to_all | solution.py:478
  61.5 4.6 %row_pass.1 = f32[16,16,128]{2,1,0:T(8,128)S(1)} custom-call(f32[2048,2048]{1,0:T(8,128)S(1)} %get-tuple-element.42.score_ref, f32[8,16,128]{2,1,0:T(8,128)S(1)} %all_to_all.21.parts_ref), custom_call_target="tpu_custom_call" | custom-call | tf_op jit(solution)/shard_map/row_pass/pallas_call | solution.py:415
  66.1 9.7 %all_to_all.22.parts_ref = f32[16,16,128]{2,1,0:T(8,128)S(1)} all-to-all(f32[16,16,128]{2,1,0:T(8,128)S(1)} %row_pass.1), channel_id=1, replica_groups=mesh['src'=8,'tgt'=16] {'tgt'}, dimensions={0} | all-to-all | bytes 262144 | tf_op jit(solution)/shard_map/all_to_all | solution.py:478
  75.8 2.5 %last_col_pass.1 = (f32[16,128]{1,0:T(8,128)S(1)}, f32[8,16,128]{2,1,0:T(8,128)S(1)}) custom-call(f32[2048,2048]{1,0:T(8,128)S(1)} %get-tuple-element.42.score_ref, f32[16,16,128]{2,1,0:T(8,128)S(1)} %all_to_all.22.parts_ref, bf16[2048,2048]{1,0:T(8,128)(2,1)S(1)} %get-tuple-element.45.table_ref, f32[128,2048]{1,0:T(8,128)S(1)} %get-tuple-element.46.kept_ref, ...), custom_call_target="tpu_custom_call" | custom-call | tf_op jit(solution)/shard_map/last_col_pass/pallas_call | solution.py:453
  78.3 9.4 %all_to_all.23.parts_ref = f32[8,16,128]{2,1,0:T(8,128)S(1)} all-to-all(f32[8,16,128]{2,1,0:T(8,128)S(1)} %get-tuple-element.48), channel_id=1, replica_groups=mesh['src'=8,'tgt'=16] {'src'}, dimensions={0} | all-to-all | bytes 131072 | tf_op jit(solution)/shard_map/all_to_all | solution.py:478
  87.7 0.6 last.1
  (13 shorter events, 0.1 us)
Async XLA Ops:
  0.6 12.1 %collective-permute-start.3 = (bf16[256,512]{1,0:T(8,128)(2,1)}, bf16[256,512]{1,0:T(8,128)(2,1)S(1)}, u32[]{:S(2)}, u32[]{:S(2)}) collective-permute-start(bf16[256,512]{1,0:T(8,128)(2,1)} %refs_1_.1), channel_id=1, source_target_pairs={{0,16},{1,17},{2,18},{3,19},{4,20},{5,21},{6,22},{7,23},{8,24},{9,... | collective-permute-start | bytes 786440 | tf_op jit(solution)/shard_map/ppermute | solution.py:486
  2.1 10.5 %collective-permute-start = (bf16[128,512]{1,0:T(8,128)(2,1)}, bf16[128,512]{1,0:T(8,128)(2,1)S(1)}, u32[]{:S(2)}, u32[]{:S(2)}) collective-permute-start(bf16[128,512]{1,0:T(8,128)(2,1)} %refs_0_.1), channel_id=1, source_target_pairs={{0,2},{1,3},{2,0},{3,1},{4,6},{5,7},{6,4},{7,5},{8,10},{9,11},{10,... | collective-permute-start | bytes 393224 | tf_op jit(solution)/shard_map/ppermute | solution.py:486
  5.1 7.8 %collective-permute-start.1 = (bf16[128,512]{1,0:T(8,128)(2,1)}, bf16[128,512]{1,0:T(8,128)(2,1)S(1)}, u32[]{:S(2)}, u32[]{:S(2)}) collective-permute-start(bf16[128,512]{1,0:T(8,128)(2,1)} %refs_0_.1), channel_id=1, source_target_pairs={{0,1},{1,2},{2,3},{3,0},{4,5},{5,6},{6,7},{7,4},{8,9},{9,10},{10,1... | collective-permute-start | bytes 393224 | tf_op jit(solution)/shard_map/ppermute | solution.py:486
  5.5 7.4 %collective-permute-start.2 = (bf16[128,512]{1,0:T(8,128)(2,1)}, bf16[128,512]{1,0:T(8,128)(2,1)S(1)}, u32[]{:S(2)}, u32[]{:S(2)}) collective-permute-start(bf16[128,512]{1,0:T(8,128)(2,1)} %refs_0_.1), channel_id=1, source_target_pairs={{0,3},{1,0},{2,1},{3,2},{4,7},{5,4},{6,5},{7,6},{8,11},{9,8},{10,9... | collective-permute-start | bytes 393224 | tf_op jit(solution)/shard_map/ppermute | solution.py:486
  7.8 7.4 %collective-permute-start.4 = (bf16[256,512]{1,0:T(8,128)(2,1)}, bf16[256,512]{1,0:T(8,128)(2,1)S(1)}, u32[]{:S(2)}, u32[]{:S(2)}) collective-permute-start(bf16[256,512]{1,0:T(8,128)(2,1)} %refs_1_.1), channel_id=1, source_target_pairs={{0,32},{1,33},{2,34},{3,35},{4,36},{5,37},{6,38},{7,39},{8,40},{9,... | collective-permute-start | bytes 786440 | tf_op jit(solution)/shard_map/ppermute | solution.py:486
  12.7 5.6 %collective-permute-start.5 = (bf16[256,512]{1,0:T(8,128)(2,1)S(1)}, bf16[256,512]{1,0:T(8,128)(2,1)S(1)}, u32[]{:S(2)}, u32[]{:S(2)}) collective-permute-start(bf16[256,512]{1,0:T(8,128)(2,1)S(1)} %collective-permute-done.3.other_ref), channel_id=1, source_target_pairs={{0,32},{1,33},{2,34},{3,35},{4,36},{5,37},{6,38},{7,39},{8,40},{9,... | collective-permute-start | bytes 786440 | tf_op jit(solution)/shard_map/ppermute | solution.py:486
  12.9 11.9 %collective-permute-start.9 = (bf16[512,512]{1,0:T(8,128)(2,1)S(1)}, bf16[512,512]{1,0:T(8,128)(2,1)S(1)}, u32[]{:S(2)}, u32[]{:S(2)}) collective-permute-start(bf16[512,512]{1,0:T(8,128)(2,1)S(1)} %constant_dynamic-update-slice_fusion.refs_1_.points_ref), channel_id=1, source_target_pairs={{0,4},{1,5},{2,6},{3,7},{4,8},{5,9},{6,10},{7,11},{8,12},{9,13},{1... | collective-permute-start | bytes 1572872 | tf_op jit(solution)/shard_map/ppermute | solution.py:486
  15.2 6.4 %collective-permute-start.6 = (bf16[256,512]{1,0:T(8,128)(2,1)S(1)}, bf16[256,512]{1,0:T(8,128)(2,1)S(1)}, u32[]{:S(2)}, u32[]{:S(2)}) collective-permute-start(bf16[256,512]{1,0:T(8,128)(2,1)S(1)} %after.1), channel_id=1, source_target_pairs={{0,32},{1,33},{2,34},{3,35},{4,36},{5,37},{6,38},{7,39},{8,40},{9,... | collective-permute-start | bytes 786440 | tf_op jit(solution)/shard_map/ppermute | solution.py:486
  18.4 7.7 %collective-permute-start.7 = (bf16[512,512]{1,0:T(8,128)(2,1)S(1)}, bf16[512,512]{1,0:T(8,128)(2,1)S(1)}, u32[]{:S(2)}, u32[]{:S(2)}) collective-permute-start(bf16[512,512]{1,0:T(8,128)(2,1)S(1)} %pad_maximum_fusion), channel_id=1, source_target_pairs={{0,16},{1,17},{2,18},{3,19},{4,20},{5,21},{6,22},{7,23},{8,24},{9,... | collective-permute-start | bytes 1572872 | tf_op jit(solution)/shard_map/ppermute | solution.py:486
  20.1 10.4 %collective-permute-start.10 = (bf16[512,512]{1,0:T(8,128)(2,1)S(1)}, bf16[512,512]{1,0:T(8,128)(2,1)S(1)}, u32[]{:S(2)}, u32[]{:S(2)}) collective-permute-start(bf16[512,512]{1,0:T(8,128)(2,1)S(1)} %constant_dynamic-update-slice_fusion.refs_1_.points_ref), channel_id=1, source_target_pairs={{0,12},{1,13},{2,14},{3,15},{4,0},{5,1},{6,2},{7,3},{8,4},{9,5},{1... | collective-permute-start | bytes 1572872 | tf_op jit(solution)/shard_map/ppermute | solution.py:486
  21.6 4.4 %collective-permute-start.8 = (bf16[256,512]{1,0:T(8,128)(2,1)S(1)}, bf16[256,512]{1,0:T(8,128)(2,1)S(1)}, u32[]{:S(2)}, u32[]{:S(2)}) collective-permute-start(bf16[256,512]{1,0:T(8,128)(2,1)S(1)} %collective-permute-done.6.far_ref), channel_id=1, source_target_pairs={{0,16},{1,17},{2,18},{3,19},{4,20},{5,21},{6,22},{7,23},{8,24},{9,... | collective-permute-start | bytes 786440 | tf_op jit(solution)/shard_map/ppermute | solution.py:486
  24.9 9.5 %collective-permute-start.11 = (bf16[512,512]{1,0:T(8,128)(2,1)S(1)}, bf16[512,512]{1,0:T(8,128)(2,1)S(1)}, u32[]{:S(2)}, u32[]{:S(2)}) collective-permute-start(bf16[512,512]{1,0:T(8,128)(2,1)S(1)} %collective-permute-done.9.refs_0_), channel_id=1, source_target_pairs={{0,4},{1,5},{2,6},{3,7},{4,8},{5,9},{6,10},{7,11},{8,12},{9,13},{1... | collective-permute-start | bytes 1572872 | tf_op jit(solution)/shard_map/ppermute | solution.py:486

commit v9 on v8

--- a/solution.py
+++ b/solution.py
@@ -78,7 +78,7 @@
 
 
 def place_kernel(
-    own_ref, other_ref, side_ref, side_other_ref, far_ref, theirs_ref, theirs_far_ref, start_ref, targets, sq_ref, pot_ref
+    own_ref, other_ref, side_ref, side_other_ref, far_ref, theirs_ref, theirs_other_ref, theirs_far_ref, start_ref, targets, sq_ref, pot_ref
 ):
     own = lax.axis_index("src")
     core = own % 2
@@ -99,8 +99,8 @@
     put(side_ref[...], side, core)
     put(side_other_ref[...], side, 1 - core)
     put(far_ref[...], 2, core)
-    put(theirs_ref[:size, :], -side, 1 - core)
-    put(theirs_ref[size:, :], -side, core)
+    put(theirs_ref[...], -side, 1 - core)
+    put(theirs_other_ref[...], -side, core)
     put(theirs_far_ref[...], 2, 1 - core)
     pot_ref[...] = (start_ref[...] - sq_ref[...]) * (1.0 / UNIT)
 
@@ -340,17 +340,17 @@
 IN_VMEM = pl.BlockSpec(memory_space=pltpu.VMEM)
 
 
-def place(own, other, side, side_other, far, theirs, theirs_far, start):
+def place(own, other, side, side_other, far, theirs, theirs_other, theirs_far, start):
     rows, width = 8 * own.shape[0], own.shape[1]
     return pl.pallas_call(
         place_kernel,
         out_shape=(pltpu.VMEM((rows, width), own.dtype), vec(rows), vec(rows)),
-        in_specs=[IN_VMEM] * 8,
+        in_specs=[IN_VMEM] * 9,
         out_specs=(IN_VMEM,) * 3,
         cost_estimate=cost(rows, width, 1),
         compiler_params=params(),
         name="place",
-    )(own, other, side, side_other, far, theirs, theirs_far, start)
+    )(own, other, side, side_other, far, theirs, theirs_other, theirs_far, start)
 
 
 def bring(*arrays):
@@ -502,29 +502,28 @@
     return move(block, lambda z, core, y, x: (z, core, y + (1 - core) * by, x + core * by))
 
 
-def after(value, earlier):
+def after(values, earlier):
     def kernel(*refs):
         del refs
 
     return pl.pallas_call(
         kernel,
-        out_shape=jax.ShapeDtypeStruct(value.shape, value.dtype),
-        in_specs=[ANYWHERE] * 2,
-        out_specs=ANYWHERE,
-        input_output_aliases={0: 0},
+        out_shape=tuple(jax.ShapeDtypeStruct(v.shape, v.dtype) for v in values),
+        in_specs=[ANYWHERE] * (len(values) + 1),
+        out_specs=(ANYWHERE,) * len(values),
+        input_output_aliases={i: i for i in range(len(values))},
         cost_estimate=pl.CostEstimate(flops=0, bytes_accessed=40_000_000, transcendentals=0),
         compiler_params=params(),
         name="after",
-    )(value, earlier)
+    )(*values, earlier)
 
 
 def gather_targets(own, earlier):
     side = round_z(own)
     other = other_core(own)
-    far = round_z(after(side, earlier))
-    side_other = round_z(other)
-    theirs = other_core(jnp.concatenate([side, side_other]))
-    return other, side, side_other, far, theirs, other_core(far)
+    later_side, later_other = after((side, other), earlier)
+    far, side_other = round_z(later_side), round_z(later_other)
+    return other, side, side_other, far, other_core(side), other_core(side_other), other_core(far)
 
 
 def local(src_points, tgt_points, tgt_start):

time: 88.6 us -> 89.9 us (1.015)
  starting transfers between devices: 21.3 us -> 24.5 us
  blocking collectives: 39.8 us -> 38.4 us
    ppermute x12 -> x13, starting transfers between devices: 21.3 us -> 24.5 us  [move(): return lax.ppermute(block, ('src', 'tgt'), pairs)]
    all_to_all x4, blocking collectives: 39.8 us -> 38.4 us  [exchange(): return lax.all_to_all(part, axis, 0, 0, tiled=True)]
    ppermute x12 -> x13, waiting for transfers between devices: 4.74 us -> 4.28 us  [move(): return lax.ppermute(block, ('src', 'tgt'), pairs)]
  transfers between devices with their start and end apart: 12 -> 13, of which waited for: 4 -> 3; matrix products, arithmetic and copies ran while one was open for 0% -> 0% of each run, Pallas kernels for 8% -> 8%
where the time goes in v9:
time: 89.9 us; the launch traced here: 89.7 us
  blocking collectives  38.4 us (43%)
  starting transfers between devices  24.5 us (27%)
  Pallas kernels  21.6 us (24%)
  waiting for transfers between devices  4.28 us (5%)
    all_to_all x4, blocking collectives, exchange(): return lax.all_to_all(part, axis, 0, 0, tiled=True)  38.4 us
    ppermute x13, starting transfers between devices, move(): return lax.ppermute(block, ('src', 'tgt'), pairs)  24.5 us
    pallas_call x3, Pallas kernels, more_pass(): pl.pallas_call(functools.partial(more_kernel, blocks), out_shape=(pltpu.V...  5.9 us
    pallas_call x1, Pallas kernels, row_pass_call(): pl.pallas_call(functools.partial(row_kernel, count), out_shape=vecs(copie...  4.57 us
    pallas_call x1, Pallas kernels, col_pass_call(): pl.pallas_call(functools.partial(col_kernel, count), out_shape=(pltpu.VME...  4.39 us
    ppermute x13, waiting for transfers between devices, move(): return lax.ppermute(block, ('src', 'tgt'), pairs)  4.28 us
    pallas_call x1, Pallas kernels, last_col_call(): pl.pallas_call(functools.partial(last_col_kernel, count), out_shape=(pltp...  2.52 us
    pallas_call x1, Pallas kernels, own_pass(): pl.pallas_call(own_kernel, out_shape=(pltpu.VMEM((rows, cols), jnp.float3...  1.95 us
  transfers between devices with their start and end apart: 13, of which 3 were waited for; matrix products, arithmetic and copies ran while one was open for 0% of the time, Pallas kernels for 8%

profile of v9, /device:TPU:1, one launch (start us, length us, event | category | flops | bytes accessed | tf_op | source)
XLA Modules:
  0.0 89.7 jit_solution(13047573327704604359)
XLA Ops:
  0.6 3.8 %collective-permute-start = (bf16[128,512]{1,0:T(8,128)(2,1)}, bf16[128,512]{1,0:T(8,128)(2,1)S(1)}, u32[]{:S(2)}, u32[]{:S(2)}) collective-permute-start(bf16[128,512]{1,0:T(8,128)(2,1)} %refs_0_.1), channel_id=1, source_target_pairs={{0,2},{1,3},{2,0},{3,1},{4,6},{5,7},{6,4},{7,5},{8,10},{9,11},{10,... | collective-permute-start | bytes 393224 | tf_op jit(solution)/shard_map/ppermute | solution.py:486
  4.5 0.4 collective-permute-start.1
  4.9 2.3 %collective-permute-start.2 = (bf16[128,512]{1,0:T(8,128)(2,1)}, bf16[128,512]{1,0:T(8,128)(2,1)S(1)}, u32[]{:S(2)}, u32[]{:S(2)}) collective-permute-start(bf16[128,512]{1,0:T(8,128)(2,1)} %refs_0_.1), channel_id=1, source_target_pairs={{0,3},{1,0},{2,1},{3,2},{4,7},{5,4},{6,5},{7,6},{8,11},{9,8},{10,9... | collective-permute-start | bytes 393224 | tf_op jit(solution)/shard_map/ppermute | solution.py:486
  7.1 3.8 %collective-permute-start.4 = (bf16[256,512]{1,0:T(8,128)(2,1)}, bf16[256,512]{1,0:T(8,128)(2,1)S(1)}, u32[]{:S(2)}, u32[]{:S(2)}) collective-permute-start(bf16[256,512]{1,0:T(8,128)(2,1)} %refs_1_.1), channel_id=1, source_target_pairs={{0,32},{1,33},{2,34},{3,35},{4,36},{5,37},{6,38},{7,39},{8,40},{9,... | collective-permute-start | bytes 786440 | tf_op jit(solution)/shard_map/ppermute | solution.py:486
  10.9 0.0 collective-permute-start.3
  10.9 1.1 %bring.1 = (bf16[128,512]{1,0:T(8,128)(2,1)S(1)}, bf16[256,512]{1,0:T(8,128)(2,1)S(1)}, f32[16,128]{1,0:T(8,128)S(1)}) custom-call(bf16[128,512]{1,0:T(8,128)(2,1)} %refs_0_.1, bf16[256,512]{1,0:T(8,128)(2,1)} %refs_1_.1, f32[16,128]{1,0:T(8,128)} %bitcast.7), custom_call_target="tpu_custom_call" | custom-call | tf_op jit(solution)/shard_map/bring/pallas_call | solution.py:357
  12.0 0.0 collective-permute-done
  12.1 1.3 %collective-permute-start.10 = (bf16[512,512]{1,0:T(8,128)(2,1)S(1)}, bf16[512,512]{1,0:T(8,128)(2,1)S(1)}, u32[]{:S(2)}, u32[]{:S(2)}) collective-permute-start(bf16[512,512]{1,0:T(8,128)(2,1)S(1)} %constant_dynamic-update-slice_fusion.refs_2_.points_ref), channel_id=1, source_target_pairs={{0,4},{1,5},{2,6},{3,7},{4,8},{5,9},{6,10},{7,11},{8,12},{9,13},{1... | collective-permute-start | bytes 1572872 | tf_op jit(solution)/shard_map/ppermute | solution.py:486
  13.3 1.2 %collective-permute-done.4.side_ref = bf16[256,512]{1,0:T(8,128)(2,1)S(1)} collective-permute-done((bf16[256,512]{1,0:T(8,128)(2,1)}, bf16[256,512]{1,0:T(8,128)(2,1)S(1)}, u32[]{:S(2)}, u32[]{:S(2)}) %collective-permute-start.4) | collective-permute-done | bytes 262176 | tf_op jit(solution)/shard_map/ppermute | solution.py:486
  14.6 3.1 %collective-permute-start.5 = (bf16[256,512]{1,0:T(8,128)(2,1)S(1)}, bf16[256,512]{1,0:T(8,128)(2,1)S(1)}, u32[]{:S(2)}, u32[]{:S(2)}) collective-permute-start(bf16[256,512]{1,0:T(8,128)(2,1)S(1)} %get-tuple-element.32), channel_id=1, source_target_pairs={{0,32},{1,33},{2,34},{3,35},{4,36},{5,37},{6,38},{7,39},{8,40},{9,... | collective-permute-start | bytes 786440 | tf_op jit(solution)/shard_map/ppermute | solution.py:486
  17.7 0.1 collective-permute-start.6
  17.8 2.5 %collective-permute-start.11 = (bf16[512,512]{1,0:T(8,128)(2,1)S(1)}, bf16[512,512]{1,0:T(8,128)(2,1)S(1)}, u32[]{:S(2)}, u32[]{:S(2)}) collective-permute-start(bf16[512,512]{1,0:T(8,128)(2,1)S(1)} %constant_dynamic-update-slice_fusion.refs_2_.points_ref), channel_id=1, source_target_pairs={{0,12},{1,13},{2,14},{3,15},{4,0},{5,1},{6,2},{7,3},{8,4},{9,5},{1... | collective-permute-start | bytes 1572872 | tf_op jit(solution)/shard_map/ppermute | solution.py:486
  20.2 1.8 %collective-permute-start.7 = (bf16[256,512]{1,0:T(8,128)(2,1)S(1)}, bf16[256,512]{1,0:T(8,128)(2,1)S(1)}, u32[]{:S(2)}, u32[]{:S(2)}) collective-permute-start(bf16[256,512]{1,0:T(8,128)(2,1)S(1)} %collective-permute-done.4.side_ref), channel_id=1, source_target_pairs={{0,16},{1,17},{2,18},{3,19},{4,20},{5,21},{6,22},{7,23},{8,24},{9,... | collective-permute-start | bytes 786440 | tf_op jit(solution)/shard_map/ppermute | solution.py:486
  22.0 0.0 collective-permute-done.5.side_other_ref
  22.1 2.7 %collective-permute-start.8 = (bf16[256,512]{1,0:T(8,128)(2,1)S(1)}, bf16[256,512]{1,0:T(8,128)(2,1)S(1)}, u32[]{:S(2)}, u32[]{:S(2)}) collective-permute-start(bf16[256,512]{1,0:T(8,128)(2,1)S(1)} %collective-permute-done.5.side_other_ref), channel_id=1, source_target_pairs={{0,16},{1,17},{2,18},{3,19},{4,20},{5,21},{6,22},{7,23},{8,24},{9,... | collective-permute-start | bytes 786440 | tf_op jit(solution)/shard_map/ppermute | solution.py:486
  24.8 2.8 %collective-permute-start.9 = (bf16[256,512]{1,0:T(8,128)(2,1)S(1)}, bf16[256,512]{1,0:T(8,128)(2,1)S(1)}, u32[]{:S(2)}, u32[]{:S(2)}) collective-permute-start(bf16[256,512]{1,0:T(8,128)(2,1)S(1)} %collective-permute-done.6.far_ref), channel_id=1, source_target_pairs={{0,16},{1,17},{2,18},{3,19},{4,20},{5,21},{6,22},{7,23},{8,24},{9,... | collective-permute-start | bytes 786440 | tf_op jit(solution)/shard_map/ppermute | solution.py:486
  27.6 0.0 collective-permute-start.12
  27.6 1.1 %collective-permute-done.9.theirs_far_ref = bf16[256,512]{1,0:T(8,128)(2,1)S(1)} collective-permute-done((bf16[256,512]{1,0:T(8,128)(2,1)S(1)}, bf16[256,512]{1,0:T(8,128)(2,1)S(1)}, u32[]{:S(2)}, u32[]{:S(2)}) %collective-permute-start.9) | collective-permute-done | bytes 262176 | tf_op jit(solution)/shard_map/ppermute | solution.py:486
  28.8 0.6 place.1
  29.3 1.9 %own_pass.1 = (f32[2048,2048]{1,0:T(8,128)S(1)}, f32[16,128]{1,0:T(8,128)S(1)}, f32[16,128]{1,0:T(8,128)S(1)}) custom-call(bf16[512,512]{1,0:T(8,128)(2,1)S(1)} %constant_dynamic-update-slice_fusion.refs_2_.points_ref, bf16[2048,512]{1,0:T(8,128)(2,1)S(1)} %get-tuple-element.35.tgt_ref, f32[16,128]{1,0:T(8,128)S(1)} %get-tuple-element.36.pot_ref), custom_call_target="tpu_custom_call" | custom-call | flops 1073741824 | bytes 8388608 | tf_op jit(solution)/shard_map/own_pass/pallas_call | solution.py:383
  31.3 2.0 %more_pass.3 = (f32[2048,2048]{1,0:T(8,128)S(1)}, f32[1,16,128]{2,1,0:T(8,128)S(1)}, f32[16,128]{1,0:T(8,128)S(1)}) custom-call(f32[2048,2048]{1,0:T(8,128)S(1)} %get-tuple-element.37.score_in_ref, f32[16,128]{1,0:T(8,128)S(1)} %get-tuple-element.38.rows_in_ref, f32[16,128]{1,0:T(8,128)S(1)} %get-tuple-element.39.src_sq_in_ref, ...), custom_call_target="tpu_custom_call", output_to_operand_aliasing={{0}: (0, {})} | custom-call | flops 1073741824 | bytes 8388608 | tf_op jit(solution)/shard_map/more_pass/pallas_call | solution.py:400
  33.2 2.0 %more_pass.4 = (f32[2048,2048]{1,0:T(8,128)S(1)}, f32[1,16,128]{2,1,0:T(8,128)S(1)}, f32[16,128]{1,0:T(8,128)S(1)}) custom-call(f32[2048,2048]{1,0:T(8,128)S(1)} %get-tuple-element.40.score_in_ref, f32[16,128]{1,0:T(8,128)S(1)} %bitcast.6, f32[16,128]{1,0:T(8,128)S(1)} %get-tuple-element.42.src_sq_in_ref, ...), custom_call_target="tpu_custom_call", output_to_operand_aliasing={{0}: (0, {})} | custom-call | flops 1073741824 | bytes 8388608 | tf_op jit(solution)/shard_map/more_pass/pallas_call | solution.py:400
  35.2 1.9 %collective-permute-done.12.refs_0_ = bf16[512,512]{1,0:T(8,128)(2,1)S(1)} collective-permute-done((bf16[512,512]{1,0:T(8,128)(2,1)S(1)}, bf16[512,512]{1,0:T(8,128)(2,1)S(1)}, u32[]{:S(2)}, u32[]{:S(2)}) %collective-permute-start.12) | collective-permute-done | bytes 524320 | tf_op jit(solution)/shard_map/ppermute | solution.py:486
  37.1 2.0 %more_pass.5 = (f32[2048,2048]{1,0:T(8,128)S(1)}, f32[16,16,128]{2,1,0:T(8,128)S(1)}, f32[16,128]{1,0:T(8,128)S(1)}) custom-call(f32[2048,2048]{1,0:T(8,128)S(1)} %get-tuple-element.43.score_in_ref, f32[16,128]{1,0:T(8,128)S(1)} %bitcast.5, f32[16,128]{1,0:T(8,128)S(1)} %get-tuple-element.45.src_sq_in_ref, ...), custom_call_target="tpu_custom_call", output_to_operand_aliasing={{0}: (0, {})} | custom-call | flops 1073741824 | bytes 8388608 | tf_op jit(solution)/shard_map/more_pass/pallas_call | solution.py:400
  39.1 11.0 %all_to_all.20.parts_ref = f32[16,16,128]{2,1,0:T(8,128)S(1)} all-to-all(f32[16,16,128]{2,1,0:T(8,128)S(1)} %get-tuple-element.47), channel_id=1, replica_groups=mesh['src'=8,'tgt'=16] {'tgt'}, dimensions={0} | all-to-all | bytes 262144 | tf_op jit(solution)/shard_map/all_to_all | solution.py:478
  50.1 4.4 %col_pass.1 = (f32[16,128]{1,0:T(8,128)S(1)}, f32[8,16,128]{2,1,0:T(8,128)S(1)}, bf16[2048,2048]{1,0:T(8,128)(2,1)S(1)}, f32[128,2048]{1,0:T(8,128)S(1)}) custom-call(f32[2048,2048]{1,0:T(8,128)S(1)} %get-tuple-element.46.score_ref, f32[16,16,128]{2,1,0:T(8,128)S(1)} %all_to_all.20.parts_ref), custom_call_target="tpu_custom_call" | custom-call | tf_op jit(solution)/shard_map/col_pass/pallas_call | solution.py:434
  54.5 8.3 %all_to_all.21.parts_ref = f32[8,16,128]{2,1,0:T(8,128)S(1)} all-to-all(f32[8,16,128]{2,1,0:T(8,128)S(1)} %get-tuple-element.48), channel_id=1, replica_groups=mesh['src'=8,'tgt'=16] {'src'}, dimensions={0} | all-to-all | bytes 131072 | tf_op jit(solution)/shard_map/all_to_all | solution.py:478
  62.9 4.6 %row_pass.1 = f32[16,16,128]{2,1,0:T(8,128)S(1)} custom-call(f32[2048,2048]{1,0:T(8,128)S(1)} %get-tuple-element.46.score_ref, f32[8,16,128]{2,1,0:T(8,128)S(1)} %all_to_all.21.parts_ref), custom_call_target="tpu_custom_call" | custom-call | tf_op jit(solution)/shard_map/row_pass/pallas_call | solution.py:415
  67.4 9.7 %all_to_all.22.parts_ref = f32[16,16,128]{2,1,0:T(8,128)S(1)} all-to-all(f32[16,16,128]{2,1,0:T(8,128)S(1)} %row_pass.1), channel_id=1, replica_groups=mesh['src'=8,'tgt'=16] {'tgt'}, dimensions={0} | all-to-all | bytes 262144 | tf_op jit(solution)/shard_map/all_to_all | solution.py:478
  77.1 2.5 %last_col_pass.1 = (f32[16,128]{1,0:T(8,128)S(1)}, f32[8,16,128]{2,1,0:T(8,128)S(1)}) custom-call(f32[2048,2048]{1,0:T(8,128)S(1)} %get-tuple-element.46.score_ref, f32[16,16,128]{2,1,0:T(8,128)S(1)} %all_to_all.22.parts_ref, bf16[2048,2048]{1,0:T(8,128)(2,1)S(1)} %get-tuple-element.49.table_ref, f32[128,2048]{1,0:T(8,128)S(1)} %get-tuple-element.50.kept_ref, ...), custom_call_target="tpu_custom_call" | custom-call | tf_op jit(solution)/shard_map/last_col_pass/pallas_call | solution.py:453
  79.6 9.4 %all_to_all.23.parts_ref = f32[8,16,128]{2,1,0:T(8,128)S(1)} all-to-all(f32[8,16,128]{2,1,0:T(8,128)S(1)} %get-tuple-element.52), channel_id=1, replica_groups=mesh['src'=8,'tgt'=16] {'src'}, dimensions={0} | all-to-all | bytes 131072 | tf_op jit(solution)/shard_map/all_to_all | solution.py:478
  89.0 0.6 last.1
  (15 shorter events, 0.1 us)
Async XLA Ops:
  0.6 11.3 %collective-permute-start = (bf16[128,512]{1,0:T(8,128)(2,1)}, bf16[128,512]{1,0:T(8,128)(2,1)S(1)}, u32[]{:S(2)}, u32[]{:S(2)}) collective-permute-start(bf16[128,512]{1,0:T(8,128)(2,1)} %refs_0_.1), channel_id=1, source_target_pairs={{0,2},{1,3},{2,0},{3,1},{4,6},{5,7},{6,4},{7,5},{8,10},{9,11},{10,... | collective-permute-start | bytes 393224 | tf_op jit(solution)/shard_map/ppermute | solution.py:486
  4.5 7.6 %collective-permute-start.1 = (bf16[128,512]{1,0:T(8,128)(2,1)}, bf16[128,512]{1,0:T(8,128)(2,1)S(1)}, u32[]{:S(2)}, u32[]{:S(2)}) collective-permute-start(bf16[128,512]{1,0:T(8,128)(2,1)} %refs_0_.1), channel_id=1, source_target_pairs={{0,1},{1,2},{2,3},{3,0},{4,5},{5,6},{6,7},{7,4},{8,9},{9,10},{10,1... | collective-permute-start | bytes 393224 | tf_op jit(solution)/shard_map/ppermute | solution.py:486
  4.9 7.2 %collective-permute-start.2 = (bf16[128,512]{1,0:T(8,128)(2,1)}, bf16[128,512]{1,0:T(8,128)(2,1)S(1)}, u32[]{:S(2)}, u32[]{:S(2)}) collective-permute-start(bf16[128,512]{1,0:T(8,128)(2,1)} %refs_0_.1), channel_id=1, source_target_pairs={{0,3},{1,0},{2,1},{3,2},{4,7},{5,4},{6,5},{7,6},{8,11},{9,8},{10,9... | collective-permute-start | bytes 393224 | tf_op jit(solution)/shard_map/ppermute | solution.py:486
  7.1 7.4 %collective-permute-start.4 = (bf16[256,512]{1,0:T(8,128)(2,1)}, bf16[256,512]{1,0:T(8,128)(2,1)S(1)}, u32[]{:S(2)}, u32[]{:S(2)}) collective-permute-start(bf16[256,512]{1,0:T(8,128)(2,1)} %refs_1_.1), channel_id=1, source_target_pairs={{0,32},{1,33},{2,34},{3,35},{4,36},{5,37},{6,38},{7,39},{8,40},{9,... | collective-permute-start | bytes 786440 | tf_op jit(solution)/shard_map/ppermute | solution.py:486
  10.9 3.7 %collective-permute-start.3 = (bf16[256,512]{1,0:T(8,128)(2,1)}, bf16[256,512]{1,0:T(8,128)(2,1)S(1)}, u32[]{:S(2)}, u32[]{:S(2)}) collective-permute-start(bf16[256,512]{1,0:T(8,128)(2,1)} %refs_1_.1), channel_id=1, source_target_pairs={{0,16},{1,17},{2,18},{3,19},{4,20},{5,21},{6,22},{7,23},{8,24},{9,... | collective-permute-start | bytes 786440 | tf_op jit(solution)/shard_map/ppermute | solution.py:486
  12.1 15.5 %collective-permute-start.10 = (bf16[512,512]{1,0:T(8,128)(2,1)S(1)}, bf16[512,512]{1,0:T(8,128)(2,1)S(1)}, u32[]{:S(2)}, u32[]{:S(2)}) collective-permute-start(bf16[512,512]{1,0:T(8,128)(2,1)S(1)} %constant_dynamic-update-slice_fusion.refs_2_.points_ref), channel_id=1, source_target_pairs={{0,4},{1,5},{2,6},{3,7},{4,8},{5,9},{6,10},{7,11},{8,12},{9,13},{1... | collective-permute-start | bytes 1572872 | tf_op jit(solution)/shard_map/ppermute | solution.py:486
  14.6 7.5 %collective-permute-start.5 = (bf16[256,512]{1,0:T(8,128)(2,1)S(1)}, bf16[256,512]{1,0:T(8,128)(2,1)S(1)}, u32[]{:S(2)}, u32[]{:S(2)}) collective-permute-start(bf16[256,512]{1,0:T(8,128)(2,1)S(1)} %get-tuple-element.32), channel_id=1, source_target_pairs={{0,32},{1,33},{2,34},{3,35},{4,36},{5,37},{6,38},{7,39},{8,40},{9,... | collective-permute-start | bytes 786440 | tf_op jit(solution)/shard_map/ppermute | solution.py:486
  17.7 7.1 %collective-permute-start.6 = (bf16[256,512]{1,0:T(8,128)(2,1)S(1)}, bf16[256,512]{1,0:T(8,128)(2,1)S(1)}, u32[]{:S(2)}, u32[]{:S(2)}) collective-permute-start(bf16[256,512]{1,0:T(8,128)(2,1)S(1)} %get-tuple-element.33), channel_id=1, source_target_pairs={{0,32},{1,33},{2,34},{3,35},{4,36},{5,37},{6,38},{7,39},{8,40},{9,... | collective-permute-start | bytes 786440 | tf_op jit(solution)/shard_map/ppermute | solution.py:486
  17.8 15.5 %collective-permute-start.11 = (bf16[512,512]{1,0:T(8,128)(2,1)S(1)}, bf16[512,512]{1,0:T(8,128)(2,1)S(1)}, u32[]{:S(2)}, u32[]{:S(2)}) collective-permute-start(bf16[512,512]{1,0:T(8,128)(2,1)S(1)} %constant_dynamic-update-slice_fusion.refs_2_.points_ref), channel_id=1, source_target_pairs={{0,12},{1,13},{2,14},{3,15},{4,0},{5,1},{6,2},{7,3},{8,4},{9,5},{1... | collective-permute-start | bytes 1572872 | tf_op jit(solution)/shard_map/ppermute | solution.py:486
  20.2 7.4 %collective-permute-start.7 = (bf16[256,512]{1,0:T(8,128)(2,1)S(1)}, bf16[256,512]{1,0:T(8,128)(2,1)S(1)}, u32[]{:S(2)}, u32[]{:S(2)}) collective-permute-start(bf16[256,512]{1,0:T(8,128)(2,1)S(1)} %collective-permute-done.4.side_ref), channel_id=1, source_target_pairs={{0,16},{1,17},{2,18},{3,19},{4,20},{5,21},{6,22},{7,23},{8,24},{9,... | collective-permute-start | bytes 786440 | tf_op jit(solution)/shard_map/ppermute | solution.py:486
  22.1 5.6 %collective-permute-start.8 = (bf16[256,512]{1,0:T(8,128)(2,1)S(1)}, bf16[256,512]{1,0:T(8,128)(2,1)S(1)}, u32[]{:S(2)}, u32[]{:S(2)}) collective-permute-start(bf16[256,512]{1,0:T(8,128)(2,1)S(1)} %collective-permute-done.5.side_other_ref), channel_id=1, source_target_pairs={{0,16},{1,17},{2,18},{3,19},{4,20},{5,21},{6,22},{7,23},{8,24},{9,... | collective-permute-start | bytes 786440 | tf_op jit(solution)/shard_map/ppermute | solution.py:486
  24.8 4.0 %collective-permute-start.9 = (bf16[256,512]{1,0:T(8,128)(2,1)S(1)}, bf16[256,512]{1,0:T(8,128)(2,1)S(1)}, u32[]{:S(2)}, u32[]{:S(2)}) collective-permute-start(bf16[256,512]{1,0:T(8,128)(2,1)S(1)} %collective-permute-done.6.far_ref), channel_id=1, source_target_pairs={{0,16},{1,17},{2,18},{3,19},{4,20},{5,21},{6,22},{7,23},{8,24},{9,... | collective-permute-start | bytes 786440 | tf_op jit(solution)/shard_map/ppermute | solution.py:486
  27.6 9.5 %collective-permute-start.12 = (bf16[512,512]{1,0:T(8,128)(2,1)S(1)}, bf16[512,512]{1,0:T(8,128)(2,1)S(1)}, u32[]{:S(2)}, u32[]{:S(2)}) collective-permute-start(bf16[512,512]{1,0:T(8,128)(2,1)S(1)} %collective-permute-done.10.refs_0_), channel_id=1, source_target_pairs={{0,4},{1,5},{2,6},{3,7},{4,8},{5,9},{6,10},{7,11},{8,12},{9,13},{1... | collective-permute-start | bytes 1572872 | tf_op jit(solution)/shard_map/ppermute | solution.py:486

commit v10 on v8

--- a/solution.py
+++ b/solution.py
@@ -232,8 +232,7 @@
 
     def run(block, wide):
         here = pl.ds(pl.multiple_of(block * LANES, LANES), LANES)
-        there = pl.ds(pl.multiple_of(block * SUB, SUB), SUB)
-        reduce(here, there, wide[...])
+        reduce(here, pl.ds(block, 1), wide[...])
 
     def step(block, is_even):
         widen(block, even if is_even else odd)
@@ -256,18 +255,18 @@
     rows, cols = score_ref.shape
 
     def reduce(here, there, pots):
-        for lanes in column_tiles(cols):
+        for k, lanes in enumerate(column_tiles(cols)):
             tiles = row_groups(score_ref[here, lanes] + pots)
-            peak = tree(jnp.maximum, tiles)
+            peak = jnp.max(tree(jnp.maximum, tiles), axis=0, keepdims=True)
             powers = [jnp.exp2(tile - peak) for tile in tiles]
-            peaks[there, lanes] = peak
-            totals[there, lanes] = tree(jnp.add, powers)
+            peaks[k, there, :] = peak
+            totals[k, there, :] = jnp.sum(tree(jnp.add, powers), axis=0, keepdims=True)
             if table_ref is not None:
                 table_ref[here, lanes] = jnp.concatenate(powers, axis=0).astype(jnp.bfloat16)
 
     by_row_blocks(pot_ref, rows // LANES, reduce, even, odd)
-    for k, lanes in enumerate(column_tiles(cols)):
-        part_ref[0, k : k + 1, :] = merge(peaks[:, lanes], totals[:, lanes])
+    for k in range(cols // LANES):
+        part_ref[0, k : k + 1, :] = merge(peaks[k], totals[k])
 
 
 def col_kernel(
@@ -292,15 +291,16 @@
     rows, cols = score_ref.shape
 
     def reduce(here, there, weights):
-        for lanes in column_tiles(cols):
+        for k, lanes in enumerate(column_tiles(cols)):
             tile = table_ref[here, lanes].astype(jnp.float32) * weights
-            totals[there, lanes] = tree(jnp.add, row_groups(tile))
+            total = tree(jnp.add, row_groups(tile))
+            totals[k, there, :] = jnp.sum(total, axis=0, keepdims=True)
 
     by_row_blocks(ratio_ref, rows // LANES, reduce, even, odd)
     sums = []
-    for k, lanes in enumerate(column_tiles(cols)):
-        peak = jnp.max(kept_ref[:, lanes], axis=0, keepdims=True)
-        scaled = totals[:, lanes] * jnp.exp2(kept_ref[:, lanes] - peak)
+    for k in range(cols // LANES):
+        peak = jnp.max(kept_ref[k], axis=0, keepdims=True)
+        scaled = totals[k] * jnp.exp2(kept_ref[k] - peak)
         sums.append(jnp.sum(scaled, axis=0, keepdims=True))
         part_ref[0, k : k + 1, :] = peak + jnp.log2(sums[-1])
 
@@ -430,7 +430,7 @@
 
 def col_pass_call(score, parts, count, copies):
     rows, cols = score.shape
-    kept = (rows // LANES * SUB, cols)
+    kept = (cols // LANES, rows // LANES, LANES)
     red_f, part, *table = pl.pallas_call(
         functools.partial(col_kernel, count),
         out_shape=(
@@ -456,7 +456,7 @@
         in_specs=[IN_VMEM] * 5,
         out_specs=(IN_VMEM, IN_VMEM),
         scratch_shapes=[scratch(rows // LANES, LANES)]
-        + [scratch(rows // LANES * SUB, cols)] * 2
+        + [scratch(cols // LANES, rows // LANES, LANES)] * 2
         + [scratch(LANES, LANES)] * 2,
         compiler_params=params(),
         name="last_col_pass",

time: 88.6 us -> 88.9 us (level)
  no operation moved by 1% of the time
where the time goes in v10:
time: 88.9 us; the launch traced here: 88.7 us
  blocking collectives  39.8 us (45%)
  Pallas kernels  21.9 us (25%)
  starting transfers between devices  21.3 us (24%)
  waiting for transfers between devices  4.74 us (5%)
    all_to_all x4, blocking collectives, exchange(): return lax.all_to_all(part, axis, 0, 0, tiled=True)  39.8 us
    ppermute x12, starting transfers between devices, move(): return lax.ppermute(block, ('src', 'tgt'), pairs)  21.3 us
    pallas_call x3, Pallas kernels, more_pass(): pl.pallas_call(functools.partial(more_kernel, blocks), out_shape=(pltpu.V...  5.9 us
    ppermute x12, waiting for transfers between devices, move(): return lax.ppermute(block, ('src', 'tgt'), pairs)  4.74 us
    pallas_call x1, Pallas kernels, col_pass_call(): pl.pallas_call(functools.partial(col_kernel, count), out_shape=(pltpu.VME...  4.72 us
    pallas_call x1, Pallas kernels, row_pass_call(): pl.pallas_call(functools.partial(row_kernel, count), out_shape=vecs(copie...  4.57 us
    pallas_call x1, Pallas kernels, last_col_call(): pl.pallas_call(functools.partial(last_col_kernel, count), out_shape=(pltp...  2.52 us
    pallas_call x1, Pallas kernels, own_pass(): pl.pallas_call(own_kernel, out_shape=(pltpu.VMEM((rows, cols), jnp.float3...  1.95 us
  transfers between devices with their start and end apart: 12, of which 4 were waited for; matrix products, arithmetic and copies ran while one was open for 0% of the time, Pallas kernels for 8%

profile of v10, /device:TPU:1, one launch (start us, length us, event | category | flops | bytes accessed | tf_op | source)
XLA Modules:
  0.0 88.7 jit_solution(10608045479687571543)
XLA Ops:
  0.6 1.5 %collective-permute-start.3 = (bf16[256,512]{1,0:T(8,128)(2,1)}, bf16[256,512]{1,0:T(8,128)(2,1)S(1)}, u32[]{:S(2)}, u32[]{:S(2)}) collective-permute-start(bf16[256,512]{1,0:T(8,128)(2,1)} %refs_1_.1), channel_id=1, source_target_pairs={{0,16},{1,17},{2,18},{3,19},{4,20},{5,21},{6,22},{7,23},{8,24},{9,... | collective-permute-start | bytes 786440 | tf_op jit(solution)/shard_map/ppermute | solution.py:486
  2.1 3.0 %collective-permute-start = (bf16[128,512]{1,0:T(8,128)(2,1)}, bf16[128,512]{1,0:T(8,128)(2,1)S(1)}, u32[]{:S(2)}, u32[]{:S(2)}) collective-permute-start(bf16[128,512]{1,0:T(8,128)(2,1)} %refs_0_.1), channel_id=1, source_target_pairs={{0,2},{1,3},{2,0},{3,1},{4,6},{5,7},{6,4},{7,5},{8,10},{9,11},{10,... | collective-permute-start | bytes 393224 | tf_op jit(solution)/shard_map/ppermute | solution.py:486
  5.1 0.4 collective-permute-start.1
  5.5 2.3 %collective-permute-start.2 = (bf16[128,512]{1,0:T(8,128)(2,1)}, bf16[128,512]{1,0:T(8,128)(2,1)S(1)}, u32[]{:S(2)}, u32[]{:S(2)}) collective-permute-start(bf16[128,512]{1,0:T(8,128)(2,1)} %refs_0_.1), channel_id=1, source_target_pairs={{0,3},{1,0},{2,1},{3,2},{4,7},{5,4},{6,5},{7,6},{8,11},{9,8},{10,9... | collective-permute-start | bytes 393224 | tf_op jit(solution)/shard_map/ppermute | solution.py:486
  7.8 3.8 %collective-permute-start.4 = (bf16[256,512]{1,0:T(8,128)(2,1)}, bf16[256,512]{1,0:T(8,128)(2,1)S(1)}, u32[]{:S(2)}, u32[]{:S(2)}) collective-permute-start(bf16[256,512]{1,0:T(8,128)(2,1)} %refs_1_.1), channel_id=1, source_target_pairs={{0,32},{1,33},{2,34},{3,35},{4,36},{5,37},{6,38},{7,39},{8,40},{9,... | collective-permute-start | bytes 786440 | tf_op jit(solution)/shard_map/ppermute | solution.py:486
  11.6 1.1 %bring.1 = (bf16[128,512]{1,0:T(8,128)(2,1)S(1)}, bf16[256,512]{1,0:T(8,128)(2,1)S(1)}, f32[16,128]{1,0:T(8,128)S(1)}) custom-call(bf16[128,512]{1,0:T(8,128)(2,1)} %refs_0_.1, bf16[256,512]{1,0:T(8,128)(2,1)} %refs_1_.1, f32[16,128]{1,0:T(8,128)} %bitcast.7), custom_call_target="tpu_custom_call" | custom-call | tf_op jit(solution)/shard_map/bring/pallas_call | solution.py:357
  12.7 0.0 collective-permute-done.3.other_ref
  12.7 0.2 collective-permute-start.5
  12.9 1.3 %collective-permute-start.9 = (bf16[512,512]{1,0:T(8,128)(2,1)S(1)}, bf16[512,512]{1,0:T(8,128)(2,1)S(1)}, u32[]{:S(2)}, u32[]{:S(2)}) collective-permute-start(bf16[512,512]{1,0:T(8,128)(2,1)S(1)} %constant_dynamic-update-slice_fusion.refs_1_.points_ref), channel_id=1, source_target_pairs={{0,4},{1,5},{2,6},{3,7},{4,8},{5,9},{6,10},{7,11},{8,12},{9,13},{1... | collective-permute-start | bytes 1572872 | tf_op jit(solution)/shard_map/ppermute | solution.py:486
  14.2 1.0 %collective-permute-done.4.side_ref = bf16[256,512]{1,0:T(8,128)(2,1)S(1)} collective-permute-done((bf16[256,512]{1,0:T(8,128)(2,1)}, bf16[256,512]{1,0:T(8,128)(2,1)S(1)}, u32[]{:S(2)}, u32[]{:S(2)}) %collective-permute-start.4) | collective-permute-done | bytes 262176 | tf_op jit(solution)/shard_map/ppermute | solution.py:486
  15.2 3.1 %collective-permute-start.6 = (bf16[256,512]{1,0:T(8,128)(2,1)S(1)}, bf16[256,512]{1,0:T(8,128)(2,1)S(1)}, u32[]{:S(2)}, u32[]{:S(2)}) collective-permute-start(bf16[256,512]{1,0:T(8,128)(2,1)S(1)} %after.1), channel_id=1, source_target_pairs={{0,32},{1,33},{2,34},{3,35},{4,36},{5,37},{6,38},{7,39},{8,40},{9,... | collective-permute-start | bytes 786440 | tf_op jit(solution)/shard_map/ppermute | solution.py:486
  18.3 0.0 collective-permute-done.5.side_other_ref
  18.4 1.7 %collective-permute-start.7 = (bf16[512,512]{1,0:T(8,128)(2,1)S(1)}, bf16[512,512]{1,0:T(8,128)(2,1)S(1)}, u32[]{:S(2)}, u32[]{:S(2)}) collective-permute-start(bf16[512,512]{1,0:T(8,128)(2,1)S(1)} %pad_maximum_fusion), channel_id=1, source_target_pairs={{0,16},{1,17},{2,18},{3,19},{4,20},{5,21},{6,22},{7,23},{8,24},{9,... | collective-permute-start | bytes 1572872 | tf_op jit(solution)/shard_map/ppermute | solution.py:486
  20.1 0.9 %collective-permute-start.10 = (bf16[512,512]{1,0:T(8,128)(2,1)S(1)}, bf16[512,512]{1,0:T(8,128)(2,1)S(1)}, u32[]{:S(2)}, u32[]{:S(2)}) collective-permute-start(bf16[512,512]{1,0:T(8,128)(2,1)S(1)} %constant_dynamic-update-slice_fusion.refs_1_.points_ref), channel_id=1, source_target_pairs={{0,12},{1,13},{2,14},{3,15},{4,0},{5,1},{6,2},{7,3},{8,4},{9,5},{1... | collective-permute-start | bytes 1572872 | tf_op jit(solution)/shard_map/ppermute | solution.py:486
  21.0 0.6 collective-permute-done.6.far_ref
  21.6 3.2 %collective-permute-start.8 = (bf16[256,512]{1,0:T(8,128)(2,1)S(1)}, bf16[256,512]{1,0:T(8,128)(2,1)S(1)}, u32[]{:S(2)}, u32[]{:S(2)}) collective-permute-start(bf16[256,512]{1,0:T(8,128)(2,1)S(1)} %collective-permute-done.6.far_ref), channel_id=1, source_target_pairs={{0,16},{1,17},{2,18},{3,19},{4,20},{5,21},{6,22},{7,23},{8,24},{9,... | collective-permute-start | bytes 786440 | tf_op jit(solution)/shard_map/ppermute | solution.py:486
  24.9 0.0 collective-permute-start.11
  24.9 1.2 %collective-permute-done.8.theirs_far_ref = bf16[256,512]{1,0:T(8,128)(2,1)S(1)} collective-permute-done((bf16[256,512]{1,0:T(8,128)(2,1)S(1)}, bf16[256,512]{1,0:T(8,128)(2,1)S(1)}, u32[]{:S(2)}, u32[]{:S(2)}) %collective-permute-start.8) | collective-permute-done | bytes 262176 | tf_op jit(solution)/shard_map/ppermute | solution.py:486
  26.0 0.5 place.1
  26.6 2.0 %own_pass.1 = (f32[2048,2048]{1,0:T(8,128)S(1)}, f32[16,128]{1,0:T(8,128)S(1)}, f32[16,128]{1,0:T(8,128)S(1)}) custom-call(bf16[512,512]{1,0:T(8,128)(2,1)S(1)} %constant_dynamic-update-slice_fusion.refs_1_.points_ref, bf16[2048,512]{1,0:T(8,128)(2,1)S(1)} %get-tuple-element.31.tgt_ref, f32[16,128]{1,0:T(8,128)S(1)} %get-tuple-element.32.pot_ref), custom_call_target="tpu_custom_call" | custom-call | flops 1073741824 | bytes 8388608 | tf_op jit(solution)/shard_map/own_pass/pallas_call | solution.py:383
  28.5 2.0 %more_pass.3 = (f32[2048,2048]{1,0:T(8,128)S(1)}, f32[1,16,128]{2,1,0:T(8,128)S(1)}, f32[16,128]{1,0:T(8,128)S(1)}) custom-call(f32[2048,2048]{1,0:T(8,128)S(1)} %get-tuple-element.33.score_in_ref, f32[16,128]{1,0:T(8,128)S(1)} %get-tuple-element.34.rows_in_ref, f32[16,128]{1,0:T(8,128)S(1)} %get-tuple-element.35.src_sq_in_ref, ...), custom_call_target="tpu_custom_call", output_to_operand_aliasing={{0}: (0, {})} | custom-call | flops 1073741824 | bytes 8388608 | tf_op jit(solution)/shard_map/more_pass/pallas_call | solution.py:400
  30.5 2.0 %more_pass.4 = (f32[2048,2048]{1,0:T(8,128)S(1)}, f32[1,16,128]{2,1,0:T(8,128)S(1)}, f32[16,128]{1,0:T(8,128)S(1)}) custom-call(f32[2048,2048]{1,0:T(8,128)S(1)} %get-tuple-element.36.score_in_ref, f32[16,128]{1,0:T(8,128)S(1)} %bitcast.6, f32[16,128]{1,0:T(8,128)S(1)} %get-tuple-element.38.src_sq_in_ref, ...), custom_call_target="tpu_custom_call", output_to_operand_aliasing={{0}: (0, {})} | custom-call | flops 1073741824 | bytes 8388608 | tf_op jit(solution)/shard_map/more_pass/pallas_call | solution.py:400
  32.5 1.9 %collective-permute-done.11.refs_0_ = bf16[512,512]{1,0:T(8,128)(2,1)S(1)} collective-permute-done((bf16[512,512]{1,0:T(8,128)(2,1)S(1)}, bf16[512,512]{1,0:T(8,128)(2,1)S(1)}, u32[]{:S(2)}, u32[]{:S(2)}) %collective-permute-start.11) | collective-permute-done | bytes 524320 | tf_op jit(solution)/shard_map/ppermute | solution.py:486
  34.4 2.0 %more_pass.5 = (f32[2048,2048]{1,0:T(8,128)S(1)}, f32[16,16,128]{2,1,0:T(8,128)S(1)}, f32[16,128]{1,0:T(8,128)S(1)}) custom-call(f32[2048,2048]{1,0:T(8,128)S(1)} %get-tuple-element.39.score_in_ref, f32[16,128]{1,0:T(8,128)S(1)} %bitcast.5, f32[16,128]{1,0:T(8,128)S(1)} %get-tuple-element.41.src_sq_in_ref, ...), custom_call_target="tpu_custom_call", output_to_operand_aliasing={{0}: (0, {})} | custom-call | flops 1073741824 | bytes 8388608 | tf_op jit(solution)/shard_map/more_pass/pallas_call | solution.py:400
  36.4 11.0 %all_to_all.20.parts_ref = f32[16,16,128]{2,1,0:T(8,128)S(1)} all-to-all(f32[16,16,128]{2,1,0:T(8,128)S(1)} %get-tuple-element.43), channel_id=1, replica_groups=mesh['src'=8,'tgt'=16] {'tgt'}, dimensions={0} | all-to-all | bytes 262144 | tf_op jit(solution)/shard_map/all_to_all | solution.py:478
  47.4 4.7 %col_pass.1 = (f32[16,128]{1,0:T(8,128)S(1)}, f32[8,16,128]{2,1,0:T(8,128)S(1)}, bf16[2048,2048]{1,0:T(8,128)(2,1)S(1)}, f32[16,16,128]{2,1,0:T(8,128)S(1)}) custom-call(f32[2048,2048]{1,0:T(8,128)S(1)} %get-tuple-element.42.score_ref, f32[16,16,128]{2,1,0:T(8,128)S(1)} %all_to_all.20.parts_ref), custom_call_target="tpu_custom_call" | custom-call | tf_op jit(solution)/shard_map/col_pass/pallas_call | solution.py:434
  52.1 9.8 %all_to_all.21.parts_ref = f32[8,16,128]{2,1,0:T(8,128)S(1)} all-to-all(f32[8,16,128]{2,1,0:T(8,128)S(1)} %get-tuple-element.44), channel_id=1, replica_groups=mesh['src'=8,'tgt'=16] {'src'}, dimensions={0} | all-to-all | bytes 131072 | tf_op jit(solution)/shard_map/all_to_all | solution.py:478
  61.9 4.6 %row_pass.1 = f32[16,16,128]{2,1,0:T(8,128)S(1)} custom-call(f32[2048,2048]{1,0:T(8,128)S(1)} %get-tuple-element.42.score_ref, f32[8,16,128]{2,1,0:T(8,128)S(1)} %all_to_all.21.parts_ref), custom_call_target="tpu_custom_call" | custom-call | tf_op jit(solution)/shard_map/row_pass/pallas_call | solution.py:415
  66.4 9.7 %all_to_all.22.parts_ref = f32[16,16,128]{2,1,0:T(8,128)S(1)} all-to-all(f32[16,16,128]{2,1,0:T(8,128)S(1)} %row_pass.1), channel_id=1, replica_groups=mesh['src'=8,'tgt'=16] {'tgt'}, dimensions={0} | all-to-all | bytes 262144 | tf_op jit(solution)/shard_map/all_to_all | solution.py:478
  76.1 2.5 %last_col_pass.1 = (f32[16,128]{1,0:T(8,128)S(1)}, f32[8,16,128]{2,1,0:T(8,128)S(1)}) custom-call(f32[2048,2048]{1,0:T(8,128)S(1)} %get-tuple-element.42.score_ref, f32[16,16,128]{2,1,0:T(8,128)S(1)} %all_to_all.22.parts_ref, bf16[2048,2048]{1,0:T(8,128)(2,1)S(1)} %get-tuple-element.45.table_ref, f32[16,16,128]{2,1,0:T(8,128)S(1)} %get-tuple-element.46.kept_ref, ...), custom_call_target="tpu_custom_call" | custom-call | tf_op jit(solution)/shard_map/last_col_pass/pallas_call | solution.py:453
  78.6 9.4 %all_to_all.23.parts_ref = f32[8,16,128]{2,1,0:T(8,128)S(1)} all-to-all(f32[8,16,128]{2,1,0:T(8,128)S(1)} %get-tuple-element.48), channel_id=1, replica_groups=mesh['src'=8,'tgt'=16] {'src'}, dimensions={0} | all-to-all | bytes 131072 | tf_op jit(solution)/shard_map/all_to_all | solution.py:478
  88.0 0.6 last.1
  (13 shorter events, 0.1 us)
Async XLA Ops:
  0.6 12.1 %collective-permute-start.3 = (bf16[256,512]{1,0:T(8,128)(2,1)}, bf16[256,512]{1,0:T(8,128)(2,1)S(1)}, u32[]{:S(2)}, u32[]{:S(2)}) collective-permute-start(bf16[256,512]{1,0:T(8,128)(2,1)} %refs_1_.1), channel_id=1, source_target_pairs={{0,16},{1,17},{2,18},{3,19},{4,20},{5,21},{6,22},{7,23},{8,24},{9,... | collective-permute-start | bytes 786440 | tf_op jit(solution)/shard_map/ppermute | solution.py:486
  2.1 10.5 %collective-permute-start = (bf16[128,512]{1,0:T(8,128)(2,1)}, bf16[128,512]{1,0:T(8,128)(2,1)S(1)}, u32[]{:S(2)}, u32[]{:S(2)}) collective-permute-start(bf16[128,512]{1,0:T(8,128)(2,1)} %refs_0_.1), channel_id=1, source_target_pairs={{0,2},{1,3},{2,0},{3,1},{4,6},{5,7},{6,4},{7,5},{8,10},{9,11},{10,... | collective-permute-start | bytes 393224 | tf_op jit(solution)/shard_map/ppermute | solution.py:486
  5.1 7.8 %collective-permute-start.1 = (bf16[128,512]{1,0:T(8,128)(2,1)}, bf16[128,512]{1,0:T(8,128)(2,1)S(1)}, u32[]{:S(2)}, u32[]{:S(2)}) collective-permute-start(bf16[128,512]{1,0:T(8,128)(2,1)} %refs_0_.1), channel_id=1, source_target_pairs={{0,1},{1,2},{2,3},{3,0},{4,5},{5,6},{6,7},{7,4},{8,9},{9,10},{10,1... | collective-permute-start | bytes 393224 | tf_op jit(solution)/shard_map/ppermute | solution.py:486
  5.5 7.4 %collective-permute-start.2 = (bf16[128,512]{1,0:T(8,128)(2,1)}, bf16[128,512]{1,0:T(8,128)(2,1)S(1)}, u32[]{:S(2)}, u32[]{:S(2)}) collective-permute-start(bf16[128,512]{1,0:T(8,128)(2,1)} %refs_0_.1), channel_id=1, source_target_pairs={{0,3},{1,0},{2,1},{3,2},{4,7},{5,4},{6,5},{7,6},{8,11},{9,8},{10,9... | collective-permute-start | bytes 393224 | tf_op jit(solution)/shard_map/ppermute | solution.py:486
  7.8 7.4 %collective-permute-start.4 = (bf16[256,512]{1,0:T(8,128)(2,1)}, bf16[256,512]{1,0:T(8,128)(2,1)S(1)}, u32[]{:S(2)}, u32[]{:S(2)}) collective-permute-start(bf16[256,512]{1,0:T(8,128)(2,1)} %refs_1_.1), channel_id=1, source_target_pairs={{0,32},{1,33},{2,34},{3,35},{4,36},{5,37},{6,38},{7,39},{8,40},{9,... | collective-permute-start | bytes 786440 | tf_op jit(solution)/shard_map/ppermute | solution.py:486
  12.7 5.6 %collective-permute-start.5 = (bf16[256,512]{1,0:T(8,128)(2,1)S(1)}, bf16[256,512]{1,0:T(8,128)(2,1)S(1)}, u32[]{:S(2)}, u32[]{:S(2)}) collective-permute-start(bf16[256,512]{1,0:T(8,128)(2,1)S(1)} %collective-permute-done.3.other_ref), channel_id=1, source_target_pairs={{0,32},{1,33},{2,34},{3,35},{4,36},{5,37},{6,38},{7,39},{8,40},{9,... | collective-permute-start | bytes 786440 | tf_op jit(solution)/shard_map/ppermute | solution.py:486
  12.9 11.9 %collective-permute-start.9 = (bf16[512,512]{1,0:T(8,128)(2,1)S(1)}, bf16[512,512]{1,0:T(8,128)(2,1)S(1)}, u32[]{:S(2)}, u32[]{:S(2)}) collective-permute-start(bf16[512,512]{1,0:T(8,128)(2,1)S(1)} %constant_dynamic-update-slice_fusion.refs_1_.points_ref), channel_id=1, source_target_pairs={{0,4},{1,5},{2,6},{3,7},{4,8},{5,9},{6,10},{7,11},{8,12},{9,13},{1... | collective-permute-start | bytes 1572872 | tf_op jit(solution)/shard_map/ppermute | solution.py:486
  15.2 6.4 %collective-permute-start.6 = (bf16[256,512]{1,0:T(8,128)(2,1)S(1)}, bf16[256,512]{1,0:T(8,128)(2,1)S(1)}, u32[]{:S(2)}, u32[]{:S(2)}) collective-permute-start(bf16[256,512]{1,0:T(8,128)(2,1)S(1)} %after.1), channel_id=1, source_target_pairs={{0,32},{1,33},{2,34},{3,35},{4,36},{5,37},{6,38},{7,39},{8,40},{9,... | collective-permute-start | bytes 786440 | tf_op jit(solution)/shard_map/ppermute | solution.py:486
  18.4 7.7 %collective-permute-start.7 = (bf16[512,512]{1,0:T(8,128)(2,1)S(1)}, bf16[512,512]{1,0:T(8,128)(2,1)S(1)}, u32[]{:S(2)}, u32[]{:S(2)}) collective-permute-start(bf16[512,512]{1,0:T(8,128)(2,1)S(1)} %pad_maximum_fusion), channel_id=1, source_target_pairs={{0,16},{1,17},{2,18},{3,19},{4,20},{5,21},{6,22},{7,23},{8,24},{9,... | collective-permute-start | bytes 1572872 | tf_op jit(solution)/shard_map/ppermute | solution.py:486
  20.1 10.4 %collective-permute-start.10 = (bf16[512,512]{1,0:T(8,128)(2,1)S(1)}, bf16[512,512]{1,0:T(8,128)(2,1)S(1)}, u32[]{:S(2)}, u32[]{:S(2)}) collective-permute-start(bf16[512,512]{1,0:T(8,128)(2,1)S(1)} %constant_dynamic-update-slice_fusion.refs_1_.points_ref), channel_id=1, source_target_pairs={{0,12},{1,13},{2,14},{3,15},{4,0},{5,1},{6,2},{7,3},{8,4},{9,5},{1... | collective-permute-start | bytes 1572872 | tf_op jit(solution)/shard_map/ppermute | solution.py:486
  21.6 4.4 %collective-permute-start.8 = (bf16[256,512]{1,0:T(8,128)(2,1)S(1)}, bf16[256,512]{1,0:T(8,128)(2,1)S(1)}, u32[]{:S(2)}, u32[]{:S(2)}) collective-permute-start(bf16[256,512]{1,0:T(8,128)(2,1)S(1)} %collective-permute-done.6.far_ref), channel_id=1, source_target_pairs={{0,16},{1,17},{2,18},{3,19},{4,20},{5,21},{6,22},{7,23},{8,24},{9,... | collective-permute-start | bytes 786440 | tf_op jit(solution)/shard_map/ppermute | solution.py:486
  24.9 9.5 %collective-permute-start.11 = (bf16[512,512]{1,0:T(8,128)(2,1)S(1)}, bf16[512,512]{1,0:T(8,128)(2,1)S(1)}, u32[]{:S(2)}, u32[]{:S(2)}) collective-permute-start(bf16[512,512]{1,0:T(8,128)(2,1)S(1)} %collective-permute-done.9.refs_0_), channel_id=1, source_target_pairs={{0,4},{1,5},{2,6},{3,7},{4,8},{5,9},{6,10},{7,11},{8,12},{9,13},{1... | collective-permute-start | bytes 1572872 | tf_op jit(solution)/shard_map/ppermute | solution.py:486
